TPU v7x, 32 devices: a whole 2x2x4 slice. The times are simulated.
32 devices in a mesh: tok: 8 (over y, x, core), feat: 4 (over z).
Axes of the slice: x: 2, y: 2, z: 4, core: 2. Of those that a mesh axis runs over, the one named last changes fastest.
Arguments:
- calib: float32 [1280, 28672], P('tok', 'feat'), may hold values from -6 to 6
- weight: float32 [28672, 512], P('feat', 'tok'), may hold values from -0.03125 to 0.03125
Outputs:
- gram_product: float32 [512, 28672], P('tok', 'feat')
All inputs are finite; a program needn't handle non-finite values.
Results may differ from a plain program's by a relative error of at most 0.000098.
Values sent between devices are 32-bit elements; how exact they have to be, the bound alone decides.
No kernel may reach another device: no remote copies, remote signals or barrier semaphores. Data moves between devices by JAX's collectives and lax.ppermute only.
A program may use at most 64 MiB of HBM per device.

v0:
```python
import math

import jax
import jax.numpy as jnp
from jax import lax
from jax.sharding import PartitionSpec as P


def shards(calib, weight):
    tokens_all = calib.shape[0] * lax.axis_size("tok")
    partial_rows = jnp.dot(
        calib,
        lax.all_gather(weight, "tok", axis=1, tiled=True),
        precision=lax.Precision.HIGHEST,
        preferred_element_type=jnp.float32,
    )
    shared = lax.psum_scatter(partial_rows, "feat", scatter_dimension=1, tiled=True)
    mixed = lax.all_gather(shared, "feat", axis=1, tiled=True)
    factor = 1.0 / math.sqrt(tokens_all)
    term = lax.dot_general(
        mixed,
        calib,
        (((0,), (0,)), ((), ())),
        precision=lax.Precision.HIGHEST,
        preferred_element_type=jnp.float32,
    )
    return lax.psum_scatter(term * factor, "tok", scatter_dimension=0, tiled=True)


def solution(mesh):
    return jax.shard_map(
        shards,
        mesh=mesh,
        in_specs=(P("tok", "feat"), P("feat", "tok")),
        out_specs=P("tok", "feat"),
        check_vma=False,
    )
```

profile of v0, /device:TPU:0, one launch (start us, length us, event | category | flops | bytes accessed | tf_op | source)
XLA Modules:
  0.0 274.0 jit_solution(18272923756002320146)
XLA Ops:
  6.5 0.0 all-gather.2.cloned.1.call-start
  6.5 0.7 all-gather.2.cloned.1.call-update
  7.3 0.0 reduce-scatter.3.cloned.1.call-start
  7.3 85.7 %all-gather.2.cloned.1.call-done = f32[7168,512]{0,1:T(8,128)} async-done(((f32[7168,64]{0,1:T(8,128)}), f32[7168,512]{0,1:T(8,128)}) %all-gather.2.cloned.1.call-update) | async-done | bytes 14680080 | tf_op jit(solution)/shard_map/all_gather | solution.py:13
  93.0 20.3 %fusion = f32[160,512]{1,0:T(8,128)} fusion(f32[160,7168]{1,0:T(8,128)} %param.2, f32[7168,512]{0,1:T(8,128)} %all-gather.2.cloned.1.call-done), kind=kOutput, calls=%fused_computation.1 | convolution fusion | flops 7046430720 | bytes 19595264 | tf_op jit(solution)/shard_map/dot_general | solution.py:11
  113.3 0.0 reduce-scatter.3.cloned.1.call-update
  113.3 0.0 reduce-scatter.5.cloned.1.call-start
  113.3 20.1 %reduce-scatter.3.cloned.1.call-done = f32[160,128]{1,0:T(8,128)} async-done(((f32[160,512]{1,0:T(8,128)}), f32[160,128]{1,0:T(8,128)}) %reduce-scatter.3.cloned.1.call-update) | async-done | bytes 81936 | tf_op jit(solution)/shard_map/reduce_scatter | solution.py:17
  133.5 14.4 %all_gather.7 = f32[160,512]{1,0:T(8,128)S(1)} all-gather(f32[160,128]{1,0:T(8,128)} %reduce-scatter.3.cloned.1.call-done), channel_id=1, replica_groups=mesh['tok'=8,'feat'=4] {'feat'}, dimensions={1}, use_global_device_ids=true | all-gather | bytes 409600 | tf_op jit(solution)/shard_map/all_gather | solution.py:18
  147.9 17.1 %convolution_multiply_fusion = f32[512,7168]{1,0:T(8,128)} fusion(f32[160,512]{1,0:T(8,128)S(1)} %all_gather.7, f32[160,7168]{1,0:T(8,128)} %param.2), kind=kOutput, calls=%fused_computation | convolution fusion | flops 7050100736 | bytes 19595264 | tf_op jit(solution)/shard_map/dot_general | solution.py:20
  165.0 0.0 reduce-scatter.5.cloned.1.call-update
  165.0 102.5 %reduce-scatter.5.cloned.1.call-done = f32[64,7168]{1,0:T(8,128)} async-done(((f32[512,7168]{1,0:T(8,128)}), f32[64,7168]{1,0:T(8,128)}) %reduce-scatter.5.cloned.1.call-update) | async-done | bytes 1835024 | tf_op jit(solution)/shard_map/reduce_scatter | solution.py:27
Async XLA Ops:
  6.5 86.4 %all-gather.2.cloned.1.call-start = ((), (), s32[]{:S(2)}) async-start(), calls=%async_computation.2 | async-start | bytes 16515072 | tf_op jit(solution)/shard_map/all_gather | solution.py:13
  7.3 126.2 %reduce-scatter.3.cloned.1.call-start = ((), (), s32[]{:S(2)}) async-start(), calls=%async_computation.3 | async-start | bytes 409600 | tf_op jit(solution)/shard_map/reduce_scatter | solution.py:17
  113.3 154.2 %reduce-scatter.5.cloned.1.call-start = ((), (), s32[]{:S(2)}) async-start(), calls=%async_computation.4 | async-start | bytes 16515072 | tf_op jit(solution)/shard_map/reduce_scatter | solution.py:27
Sparse Core Ops, SparseCore 0:
  9.2 83.6 all-gather.1
  113.4 20.0 reduce-scatter.2
  165.1 102.3 reduce-scatter.4
where the time goes:
time: 274 us
  waiting for transfers between devices  209 us (76%)
  matrix products  37.4 us (14%)
  blocking collectives  14.4 us (5%)
  between operations  13.1 us (5%)
    reduce_scatter x1, waiting for transfers between devices, shards(): lax.psum_scatter(term * factor, 'tok', scatter_dimension=0, tiled=True)  103 us
    all_gather x1, waiting for transfers between devices, shards(): lax.all_gather(weight, 'tok', axis=1, tiled=True)  85.7 us
    dot_general x1, matrix products, shards(): jnp.dot(calib, lax.all_gather(weight, 'tok', axis=1, tiled=True), precisi...  20.3 us
    reduce_scatter x1, waiting for transfers between devices, shards(): lax.psum_scatter(partial_rows, 'feat', scatter_dimension=1, tiled=True)  20.1 us
    dot_general x1, matrix products, shards(): lax.dot_general(mixed, calib, (((0,), (0,)), ((), ())), precision=lax.Pre...  17.1 us
    all_gather x1, blocking collectives, shards(): mixed = lax.all_gather(shared, 'feat', axis=1, tiled=True)  14.4 us
  transfers between devices with their start and end apart: 3, of which 3 were waited for; matrix products, arithmetic and copies ran while one was open for 0% of the time, Pallas kernels for 0%

commit v1 on v0

v1 whole, which is shorter than its diff:
```python
import math

import jax
import jax.numpy as jnp
from jax import lax
from jax.sharding import PartitionSpec as P

CHUNKS = 2


def routes(side):
    place = lambda a, b, core: ((a % side) * side + b % side) * 2 + core
    every = [(a, b, core) for a in range(side) for b in range(side) for core in (0, 1)]

    def over(step, cross, lead):
        pairs = []
        for a, b, core in every:
            along_a = (core ^ cross if lead == "receiver" else core) == 0
            there = (a + step, b) if along_a else (a, b + step)
            pairs.append((place(a, b, core), place(*there, core ^ cross)))
        return pairs

    def rows(step, cross):
        pairs = []
        for a, b, core in every:
            along_b = core ^ cross == 0
            there = (a, b + step) if along_b else (a + step, b)
            pairs.append((place(a, b, core), place(*there, core ^ cross)))
        return pairs

    def columns(step, cross):
        return over(step, cross, "receiver")

    def results(step, cross):
        return over(step, cross, "sender")

    def swap(row, column):
        pairs = []
        for a, b, core in every:
            there = (a + column, b + row) if core == 0 else (a + row, b + column)
            pairs.append((place(a, b, core), place(*there, 1 - core)))
        return pairs

    return rows, columns, results, swap


def split(x):
    high = lax.reduce_precision(x, 8, 7)
    return high.astype(jnp.bfloat16), (x - high).astype(jnp.bfloat16)


def product(left, right, dims):
    (lh, ll), (rh, rl) = left, right
    dot = lambda l, r: lax.dot_general(
        l, r, (dims, ((), ())), preferred_element_type=jnp.float32
    )
    return dot(lh, rh) + (dot(lh, rl) + dot(ll, rh))


def shards(side, chunks, calib, weight):
    zs = lax.axis_size("feat")
    z = lax.axis_index("feat")
    core = lax.axis_index("tok") % 2
    tokens, features = calib.shape
    half = features // 2
    width = weight.shape[1] // chunks
    part = tokens // zs
    rows, columns, results, swap = routes(side)
    turns = range(side)
    send = lambda x, pairs: lax.ppermute(x, "tok", pairs)
    factor = 1.0 / math.sqrt(tokens * lax.axis_size("tok"))

    def halves(x):
        own = lax.dynamic_slice_in_dim(x, core * half, half, 1)
        other = lax.dynamic_slice_in_dim(x, (1 - core) * half, half, 1)
        return own, other

    def gather(x, route):
        own, other = halves(x)
        got = {(0, 0): own}
        for s in turns:
            if s:
                got[-s % side, 0] = send(own, route(s, 0))
            got[-s % side, 1] = send(other, route(s, 1))
        return jnp.concatenate([got[r, c] for r in turns for c in (0, 1)], 0)

    acts = split(gather(calib, rows))
    turned = weight.T
    pieces = []
    for j in range(chunks):
        cols = split(gather(turned[j * width : (j + 1) * width], columns))
        mixed = product(acts, cols, ((1,), (1,)))
        mixed = mixed.reshape(side * 2, zs, part, side * 2 * width)

        def piece(at):
            return lax.dynamic_index_in_dim(mixed, at % zs, 1, keepdims=False)

        shift = lambda s: [(i, (i + s) % zs) for i in range(zs)]
        total = piece(z)
        for s in range(1, zs):
            total = total + lax.ppermute(piece(z + s), "feat", shift(s))
        blocks = total.reshape(side, 2, part, side, 2, width)
        grid = [[None] * side for _ in turns]
        for r in turns:
            for q in turns:
                block = blocks[r, ::-1, :, q, ::-1].reshape(2 * part, 2 * width)
                block = send(block, swap(r, q)).reshape(2, part, 2, width)
                mine = blocks[-q % side, :, :, -r % side]
                grid[-q % side][-r % side] = mine + block
        total = jnp.stack([jnp.stack(g, 2) for g in grid], 0)
        total = total.reshape(side * 2, part, side * 2 * width) * factor
        got = [total] + [
            lax.ppermute(total, "feat", shift(s)) for s in range(zs - 1, 0, -1)
        ]
        ring = jnp.stack(got + got, 1)
        mixed = lax.dynamic_slice_in_dim(ring, (zs - z) % zs, zs, 1)
        mixed = split(mixed.reshape(side * 2 * tokens, side * 2 * width))
        term = product(mixed, acts, ((0,), (0,)))
        term = term.reshape(side, 2, width, half)
        own, other = term[0, 0], send(term[0, 1], results(0, 1))
        for s in turns[1:]:
            own = own + send(term[s, 0], results(s, 0))
            other = other + send(term[s, 1], results(s, 1))
        left = jnp.where(core == 0, own, other)
        right = jnp.where(core == 0, other, own)
        pieces.append(jnp.concatenate([left, right], 1))
    return jnp.concatenate(pieces, 0)


def solution(mesh):
    side = math.isqrt(mesh.shape["tok"] // 2)

    def step(calib, weight):
        return shards(side, CHUNKS, calib, weight)

    return jax.shard_map(
        step,
        mesh=mesh,
        in_specs=(P("tok", "feat"), P("feat", "tok")),
        out_specs=P("tok", "feat"),
        check_vma=False,
    )
```

time: 274 us -> 155 us (0.57)
  waiting for transfers between devices: 209 us -> 81 us
  starting transfers between devices: 0.08 us -> 35.9 us
  matrix products: 37.4 us -> 19.5 us
  blocking collectives: 14.4 us -> 0 us
  between operations: 13.1 us -> 0.84 us
  local copies, waits for them, and re-layouts: 0 us -> 10.5 us
  other arithmetic: 0 us -> 5.59 us
    reduce_scatter x2 -> x0, waiting for transfers between devices: 123 us -> none  [the longest x1 103 us: shards(): lax.psum_scatter(term * factor, 'tok', scatter_dimension=0, tiled=True)]
    all_gather x1 -> x0, waiting for transfers between devices: 85.7 us -> none  [shards(): lax.all_gather(weight, 'tok', axis=1, tiled=True)]
    ppermute x0 -> x35, waiting for transfers between devices: none -> 81 us  [the longest x23 70.3 us: shards(): send = lambda x, pairs: lax.ppermute(x, 'tok', pairs)]
    ppermute x0 -> x35, starting transfers between devices: none -> 35.9 us  [the longest x23 17.6 us: shards(): send = lambda x, pairs: lax.ppermute(x, 'tok', pairs)]
    dot_general x2 -> x12, matrix products: 37.4 us -> 19.5 us  [product(): lax.dot_general(l, r, (dims, ((), ())), preferred_element_type=jnp.float32)]
    all_gather x1 -> x0, blocking collectives: 14.4 us -> none  [shards(): mixed = lax.all_gather(shared, 'feat', axis=1, tiled=True)]
    dynamic_slice x0 -> x7, local copies, waits for them, and re-layouts: none -> 5.32 us  [the longest x3 5.22 us: halves(): own = lax.dynamic_slice_in_dim(x, core * half, half, 1)]
    convert_element_type x0 -> x3, other arithmetic: none -> 3.8 us  [split(): return (high.astype(jnp.bfloat16), (x - high).astype(jnp.bfloat16))]
  transfers between devices with their start and end apart: 3 -> 35, of which waited for: 3 -> 9; matrix products, arithmetic and copies ran while one was open for 0% -> 19% of each run, Pallas kernels for 0% -> 0%
where the time goes in v1:
time: 155 us; the launch traced here: 153 us
  waiting for transfers between devices  81 us (52%)
  starting transfers between devices  35.9 us (23%)
  matrix products  19.5 us (13%)
  local copies, waits for them, and re-layouts  10.5 us (7%)
  other arithmetic  5.59 us (4%)
    ppermute x23, waiting for transfers between devices, shards(): send = lambda x, pairs: lax.ppermute(x, 'tok', pairs)  70.3 us
    dot_general x12, matrix products, product(): lax.dot_general(l, r, (dims, ((), ())), preferred_element_type=jnp.float32)  19.5 us
    ppermute x23, starting transfers between devices, shards(): send = lambda x, pairs: lax.ppermute(x, 'tok', pairs)  17.6 us
    ppermute x6, starting transfers between devices, shards(): total = total + lax.ppermute(piece(z + s), 'feat', shift(s))  9.67 us
    ppermute x6, starting transfers between devices, shards(): lax.ppermute(total, 'feat', shift(s))  8.7 us
    ppermute x6, waiting for transfers between devices, shards(): lax.ppermute(total, 'feat', shift(s))  5.42 us
    ppermute x6, waiting for transfers between devices, shards(): total = total + lax.ppermute(piece(z + s), 'feat', shift(s))  5.28 us
    dynamic_slice x3, local copies, waits for them, and re-layouts, halves(): own = lax.dynamic_slice_in_dim(x, core * half, half, 1)  5.22 us
  transfers between devices with their start and end apart: 35, of which 9 were waited for; matrix products, arithmetic and copies ran while one was open for 19% of the time, Pallas kernels for 0%

profile of v1, /device:TPU:0, one launch (start us, length us, event | category | flops | bytes accessed | tf_op | source)
XLA Modules:
  0.0 153.3 jit_solution(17351694921856107392)
XLA Ops:
  0.0 4.2 %constant_dynamic-slice_fusion.7 = (f32[160,3584]{1,0:T(8,128)S(1)}, f32[160,3584]{1,0:T(8,128)}) fusion(f32[160,7168]{1,0:T(8,128)} %param.2, s32[]{:T(128)S(6)} %select_n.90, s32[]{:T(128)S(6)} %select_n.91), kind=kLoop, calls=%fused_computation.90 | loop fusion | bytes 9175048 | tf_op jit(solution)/shard_map/dynamic_slice | solution.py:74
  4.2 0.5 collective-permute-start
  4.6 2.6 %collective-permute-start.2 = (f32[160,3584]{1,0:T(8,128)}, f32[160,3584]{1,0:T(8,128)}, u32[]{:S(2)}, u32[]{:S(2)}) collective-permute-start(f32[160,3584]{1,0:T(8,128)} %get-tuple-element.8), channel_id=1, source_target_pairs={{0,20},{4,8},{8,28},{12,0},{16,4},{20,24},{24,12},{28,16},{1,21},{... | collective-permute-start | bytes 6881288 | tf_op jit(solution)/shard_map/ppermute | solution.py:70
  7.2 1.5 collective-permute-start.1
  8.9 1.0 constant_dynamic-slice_fusion.5
  9.9 0.6 collective-permute-start.5
  10.7 47.3 %collective-permute-done.1 = f32[160,3584]{1,0:T(8,128)} collective-permute-done((f32[160,3584]{1,0:T(8,128)S(1)}, f32[160,3584]{1,0:T(8,128)}, u32[]{:S(2)}, u32[]{:S(2)}) %collective-permute-start.1) | collective-permute-done | bytes 2293792 | tf_op jit(solution)/shard_map/ppermute | solution.py:70
  57.9 0.6 collective-permute-start.21
  58.5 1.8 %collective-permute-start.4 = (f32[32,3584]{1,0:T(8,128)S(1)}, f32[32,3584]{1,0:T(8,128)S(1)}, u32[]{:S(2)}, u32[]{:S(2)}) collective-permute-start(f32[32,3584]{1,0:T(8,128)S(1)} %copy-done.3), channel_id=1, source_target_pairs={{0,16},{4,12},{8,24},{12,4},{16,0},{20,28},{24,8},{28,20},{1,17},{... | collective-permute-start | bytes 1376264 | tf_op jit(solution)/shard_map/ppermute | solution.py:70
  60.3 3.7 %reduce-precision_convert_fusion = (bf16[640,3584]{1,0:T(8,128)(2,1)S(1)}, bf16[640,3584]{1,0:T(8,128)(2,1)S(1)}) fusion(f32[160,3584]{1,0:T(8,128)} %collective-permute-done.2, f32[160,3584]{1,0:T(8,128)} %collective-permute-done.1, f32[160,3584]{1,0:T(8,128)} %collective-permute-done, f32[160,3584]{1,0:T(8,128)S(1)} %get-tuple-element.7), kind=kLoop, calls=%fused_computation.1 | loop fusion | flops 16056320 | bytes 18350080 | tf_op jit(solution)/shard_map/convert_element_type | solution.py:49
  64.3 7.6 %collective-permute-done.4 = f32[32,3584]{1,0:T(8,128)S(1)} collective-permute-done((f32[32,3584]{1,0:T(8,128)S(1)}, f32[32,3584]{1,0:T(8,128)S(1)}, u32[]{:S(2)}, u32[]{:S(2)}) %collective-permute-start.4) | collective-permute-done | bytes 458784 | tf_op jit(solution)/shard_map/ppermute | solution.py:70
  72.0 2.5 %fusion.15 = f32[640,128]{1,0:T(8,128)S(1)} fusion(bf16[640,3584]{1,0:T(8,128)(2,1)S(1)} %get-tuple-element.6, f32[32,3584]{1,0:T(8,128)} %collective-permute-done.5, f32[32,3584]{1,0:T(8,128)S(1)} %collective-permute-done.4, f32[32,3584]{1,0:T(8,128)} %collective-permute-done.3, f32[32,3584]{1,0:T(8,128)S(1)} %copy-done.3), kind=kOutput, calls=%fused_computation.93 | convolution fusion | flops 589496320 | bytes 6750208 | tf_op jit(solution)/shard_map/dot_general | solution.py:54
  74.5 2.5 %convolution_add_fusion.6 = f32[640,128]{1,0:T(8,128)S(1)} fusion(f32[640,128]{1,0:T(8,128)S(1)} %fusion.15, bf16[640,3584]{1,0:T(8,128)(2,1)S(1)} %get-tuple-element.5, f32[32,3584]{1,0:T(8,128)} %collective-permute-done.5, f32[32,3584]{1,0:T(8,128)S(1)} %collective-permute-done.4, f32[32,3584]{1,0:T(8,128)} %collective-permute-done.3, ...), kind=kOutput, calls=%fused_computation.19 | convolution fusion | flops 590036992 | bytes 7077888 | tf_op jit(solution)/shard_map/dot_general | solution.py:54
  77.0 2.5 %convolution_add_fusion.7 = f32[640,128]{1,0:T(8,128)S(1)} fusion(f32[640,128]{1,0:T(8,128)S(1)} %convolution_add_fusion.6, bf16[640,3584]{1,0:T(8,128)(2,1)S(1)} %get-tuple-element.5, f32[32,3584]{1,0:T(8,128)} %collective-permute-done.5, f32[32,3584]{1,0:T(8,128)S(1)} %collective-permute-done.4, f32[32,3584]{1,0:T(8,128)} %collective-permute-done.3, ...), kind=kOutput, calls=%fused_computation.20 | convolution fusion | flops 589578240 | bytes 7077888 | tf_op jit(solution)/shard_map/dot_general | solution.py:54
  79.6 1.9 %collective-permute-start.6 = (f32[4,40,128]{2,1,0:T(8,128)S(1)}, f32[4,40,128]{2,1,0:T(8,128)S(1)}, u32[]{:S(2)}, u32[]{:S(2)}) collective-permute-start(f32[4,40,128]{2,1,0:T(8,128)S(1)} %get-tuple-element.31), channel_id=1, source_target_pairs={{0,1},{1,2},{2,3},{3,0},{4,5},{5,6},{6,7},{7,4},{8,9},{9,10},{10,1... | collective-permute-start | bytes 245768 | tf_op jit(solution)/shard_map/ppermute | solution.py:101
  81.4 2.6 %collective-permute-start.7 = (f32[4,40,128]{2,1,0:T(8,128)S(1)}, f32[4,40,128]{2,1,0:T(8,128)S(1)}, u32[]{:S(2)}, u32[]{:S(2)}) collective-permute-start(f32[4,40,128]{2,1,0:T(8,128)S(1)} %get-tuple-element.33), channel_id=1, source_target_pairs={{0,2},{1,3},{2,0},{3,1},{4,6},{5,7},{6,4},{7,5},{8,10},{9,11},{10,... | collective-permute-start | bytes 245768 | tf_op jit(solution)/shard_map/ppermute | solution.py:101
  84.0 1.3 collective-permute-start.8
  85.4 1.3 fusion.16
  86.7 1.4 convolution_add_fusion.4
  88.1 1.4 convolution_add_fusion.5
  89.5 0.7 collective-permute-start.22
  90.6 2.8 %collective-permute-start.24 = (f32[4,40,128]{2,1,0:T(8,128)S(1)}, f32[4,40,128]{2,1,0:T(8,128)S(1)}, u32[]{:S(2)}, u32[]{:S(2)}) collective-permute-start(f32[4,40,128]{2,1,0:T(8,128)S(1)} %get-tuple-element.41), channel_id=1, source_target_pairs={{0,3},{1,0},{2,1},{3,2},{4,7},{5,4},{6,5},{7,6},{8,11},{9,8},{10,9... | collective-permute-start | bytes 245768 | tf_op jit(solution)/shard_map/ppermute | solution.py:101
  93.4 3.3 %collective-permute-done.22 = f32[4,40,128]{2,1,0:T(8,128)S(1)} collective-permute-done((f32[4,40,128]{2,1,0:T(8,128)S(1)}, f32[4,40,128]{2,1,0:T(8,128)S(1)}, u32[]{:S(2)}, u32[]{:S(2)}) %collective-permute-start.22) | collective-permute-done | bytes 81952 | tf_op jit(solution)/shard_map/ppermute | solution.py:101
  96.8 1.9 %collective-permute-done.23 = f32[4,40,128]{2,1,0:T(8,128)S(1)} collective-permute-done((f32[4,40,128]{2,1,0:T(8,128)S(1)}, f32[4,40,128]{2,1,0:T(8,128)S(1)}, u32[]{:S(2)}, u32[]{:S(2)}) %collective-permute-start.23) | collective-permute-done | bytes 81952 | tf_op jit(solution)/shard_map/ppermute | solution.py:101
  99.7 1.6 %collective-permute-start.10 = (f32[80,64]{0,1:T(8,128)S(1)}, f32[80,64]{0,1:T(8,128)S(1)}, u32[]{:S(2)}, u32[]{:S(2)}) collective-permute-start(f32[80,64]{0,1:T(8,128)S(1)} %reshape_squeeze.25), channel_id=1, source_target_pairs={{0,12},{4,16},{8,4},{12,24},{16,28},{20,0},{24,20},{28,8},{1,13},{... | collective-permute-start | bytes 61448 | tf_op jit(solution)/shard_map/ppermute | solution.py:70
  101.6 0.4 collective-permute-start.11
  102.2 1.9 %collective-permute-start.12 = (f32[80,64]{0,1:T(8,128)S(1)}, f32[80,64]{0,1:T(8,128)S(1)}, u32[]{:S(2)}, u32[]{:S(2)}) collective-permute-start(f32[80,64]{0,1:T(8,128)S(1)} %reshape_squeeze.27), channel_id=1, source_target_pairs={{0,28},{4,24},{8,20},{12,16},{16,12},{20,8},{24,4},{28,0},{1,29},{... | collective-permute-start | bytes 61448 | tf_op jit(solution)/shard_map/ppermute | solution.py:70
  105.7 0.6 collective-permute-start.26
  106.4 1.3 collective-permute-start.27
  107.8 1.3 collective-permute-start.28
  109.6 1.7 %collective-permute-start.13 = (f32[4,40,128]{2,1,0:T(8,128)S(1)}, f32[4,40,128]{2,1,0:T(8,128)S(1)}, u32[]{:S(2)}, u32[]{:S(2)}) collective-permute-start(f32[4,40,128]{2,1,0:T(8,128)S(1)} %copy.99), channel_id=1, source_target_pairs={{0,3},{1,0},{2,1},{3,2},{4,7},{5,4},{6,5},{7,6},{8,11},{9,8},{10,9... | collective-permute-start | bytes 245768 | tf_op jit(solution)/shard_map/ppermute | solution.py:113
  111.3 1.4 collective-permute-start.14
  113.5 3.8 %collective-permute-start.29 = (f32[4,40,128]{2,1,0:T(8,128)S(1)}, f32[4,40,128]{2,1,0:T(8,128)S(1)}, u32[]{:S(2)}, u32[]{:S(2)}) collective-permute-start(f32[4,40,128]{2,1,0:T(8,128)S(1)} %copy.101), channel_id=1, source_target_pairs={{0,3},{1,0},{2,1},{3,2},{4,7},{5,4},{6,5},{7,6},{8,11},{9,8},{10,9... | collective-permute-start | bytes 245768 | tf_op jit(solution)/shard_map/ppermute | solution.py:113
  117.6 1.6 %collective-permute-start.31 = (f32[4,40,128]{2,1,0:T(8,128)S(1)}, f32[4,40,128]{2,1,0:T(8,128)S(1)}, u32[]{:S(2)}, u32[]{:S(2)}) collective-permute-start(f32[4,40,128]{2,1,0:T(8,128)S(1)} %copy.101), channel_id=1, source_target_pairs={{0,1},{1,2},{2,3},{3,0},{4,5},{5,6},{6,7},{7,4},{8,9},{9,10},{10,1... | collective-permute-start | bytes 245768 | tf_op jit(solution)/shard_map/ppermute | solution.py:113
  119.3 5.4 %collective-permute-done.14 = f32[4,40,128]{2,1,0:T(8,128)S(1)} collective-permute-done((f32[4,40,128]{2,1,0:T(8,128)S(1)}, f32[4,40,128]{2,1,0:T(8,128)S(1)}, u32[]{:S(2)}, u32[]{:S(2)}) %collective-permute-start.14) | collective-permute-done | bytes 81952 | tf_op jit(solution)/shard_map/ppermute | solution.py:113
  124.9 3.3 %fusion.20 = f32[128,3584]{1,0:T(8,128)S(1)} fusion(bf16[640,128]{1,0:T(8,128)(2,1)S(1)} %get-tuple-element.26, bf16[640,3584]{1,0:T(8,128)(2,1)} %copy-done), kind=kOutput, calls=%fused_computation.98 | convolution fusion | flops 587202560 | bytes 6586368 | tf_op jit(solution)/shard_map/dot_general | solution.py:54
  128.4 0.9 convolution_add_fusion.2
  129.3 0.4 slice-done
  129.8 0.9 convolution_add_fusion.3
  131.1 1.9 %collective-permute-start.18 = (f32[32,3584]{1,0:T(8,128)S(1)}, f32[32,3584]{1,0:T(8,128)S(1)}, u32[]{:S(2)}, u32[]{:S(2)}) collective-permute-start(f32[32,3584]{1,0:T(8,128)S(1)} %get-tuple-element.14), channel_id=1, source_target_pairs={{0,20},{4,8},{8,28},{12,0},{16,4},{20,24},{24,12},{28,16},{1,21},{... | collective-permute-start | bytes 1376264 | tf_op jit(solution)/shard_map/ppermute | solution.py:70
  133.3 0.9 fusion.21
  134.2 0.9 convolution_add_fusion
  135.1 0.9 convolution_add_fusion.1
  136.4 3.0 %collective-permute-done.16 = f32[32,3584]{1,0:T(8,128)S(1)} collective-permute-done((f32[32,3584]{1,0:T(8,128)S(1)}, f32[32,3584]{1,0:T(8,128)S(1)}, u32[]{:S(2)}, u32[]{:S(2)}) %collective-permute-start.16) | collective-permute-done | bytes 458784 | tf_op jit(solution)/shard_map/ppermute | solution.py:70
  139.4 2.7 %collective-permute-done.18 = f32[32,3584]{1,0:T(8,128)S(1)} collective-permute-done((f32[32,3584]{1,0:T(8,128)S(1)}, f32[32,3584]{1,0:T(8,128)S(1)}, u32[]{:S(2)}, u32[]{:S(2)}) %collective-permute-start.18) | collective-permute-done | bytes 458784 | tf_op jit(solution)/shard_map/ppermute | solution.py:70
  142.1 7.1 %collective-permute-done.32 = f32[32,3584]{1,0:T(8,128)S(1)} collective-permute-done((f32[32,3584]{1,0:T(8,128)S(1)}, f32[32,3584]{1,0:T(8,128)S(1)}, u32[]{:S(2)}, u32[]{:S(2)}) %collective-permute-start.32) | collective-permute-done | bytes 458784 | tf_op jit(solution)/shard_map/ppermute | solution.py:70
  149.2 2.7 %collective-permute-done.34 = f32[32,3584]{1,0:T(8,128)S(1)} collective-permute-done((f32[32,3584]{1,0:T(8,128)S(1)}, f32[32,3584]{1,0:T(8,128)S(1)}, u32[]{:S(2)}, u32[]{:S(2)}) %collective-permute-start.34) | collective-permute-done | bytes 458784 | tf_op jit(solution)/shard_map/ppermute | solution.py:70
  152.0 1.3 maximum_maximum_fusion
  (149 shorter events, 7.0 us)
Async XLA Ops:
  0.0 8.7 %copy-start.2 = (f32[7168,64]{0,1:T(8,128)S(1)}, f32[7168,64]{0,1:T(8,128)}, u32[]{:S(2)}) copy-start(f32[7168,64]{0,1:T(8,128)} %param.3) | copy-start | bytes 5505028
  4.2 6.4 %collective-permute-start = (f32[160,3584]{1,0:T(8,128)}, f32[160,3584]{1,0:T(8,128)}, u32[]{:S(2)}, u32[]{:S(2)}) collective-permute-start(f32[160,3584]{1,0:T(8,128)} %get-tuple-element.8), channel_id=1, source_target_pairs={{0,4},{4,0},{8,12},{12,8},{16,20},{20,16},{24,28},{28,24},{1,5},{5... | collective-permute-start | bytes 6881288 | tf_op jit(solution)/shard_map/ppermute | solution.py:70
  4.6 53.9 %collective-permute-start.2 = (f32[160,3584]{1,0:T(8,128)}, f32[160,3584]{1,0:T(8,128)}, u32[]{:S(2)}, u32[]{:S(2)}) collective-permute-start(f32[160,3584]{1,0:T(8,128)} %get-tuple-element.8), channel_id=1, source_target_pairs={{0,20},{4,8},{8,28},{12,0},{16,4},{20,24},{24,12},{28,16},{1,21},{... | collective-permute-start | bytes 6881288 | tf_op jit(solution)/shard_map/ppermute | solution.py:70
  7.2 50.7 %collective-permute-start.1 = (f32[160,3584]{1,0:T(8,128)S(1)}, f32[160,3584]{1,0:T(8,128)}, u32[]{:S(2)}, u32[]{:S(2)}) collective-permute-start(f32[160,3584]{1,0:T(8,128)S(1)} %get-tuple-element.7), channel_id=1, source_target_pairs={{0,8},{4,20},{8,0},{12,28},{16,24},{20,4},{24,16},{28,12},{1,9},{5... | collective-permute-start | bytes 6881288 | tf_op jit(solution)/shard_map/ppermute | solution.py:70
  9.9 54.1 %collective-permute-start.3 = (f32[32,3584]{1,0:T(8,128)}, f32[32,3584]{1,0:T(8,128)}, u32[]{:S(2)}, u32[]{:S(2)}) collective-permute-start(f32[32,3584]{1,0:T(8,128)} %get-tuple-element.22), channel_id=1, source_target_pairs={{0,4},{4,0},{8,12},{12,8},{16,20},{20,16},{24,28},{28,24},{1,5},{5... | collective-permute-start | bytes 1376264 | tf_op jit(solution)/shard_map/ppermute | solution.py:70
  9.9 62.1 %collective-permute-start.5 = (f32[32,3584]{1,0:T(8,128)}, f32[32,3584]{1,0:T(8,128)}, u32[]{:S(2)}, u32[]{:S(2)}) collective-permute-start(f32[32,3584]{1,0:T(8,128)} %get-tuple-element.22), channel_id=1, source_target_pairs={{0,12},{4,16},{8,4},{12,24},{16,28},{20,0},{24,20},{28,8},{1,13},{... | collective-permute-start | bytes 1376264 | tf_op jit(solution)/shard_map/ppermute | solution.py:70
  10.5 48.0 %copy-start.3 = (f32[32,3584]{1,0:T(8,128)S(1)}, f32[32,3584]{1,0:T(8,128)}, u32[]{:S(2)}) copy-start(f32[32,3584]{1,0:T(8,128)} %get-tuple-element.21) | copy-start | bytes 1376260
  10.6 73.4 %collective-permute-start.19 = (f32[32,3584]{1,0:T(8,128)S(1)}, f32[32,3584]{1,0:T(8,128)S(1)}, u32[]{:S(2)}, u32[]{:S(2)}) collective-permute-start(f32[32,3584]{1,0:T(8,128)S(1)} %get-tuple-element.24), channel_id=1, source_target_pairs={{0,4},{4,0},{8,12},{12,8},{16,20},{20,16},{24,28},{28,24},{1,5},{5... | collective-permute-start | bytes 1376264 | tf_op jit(solution)/shard_map/ppermute | solution.py:70
  57.9 27.5 %collective-permute-start.21 = (f32[32,3584]{1,0:T(8,128)S(1)}, f32[32,3584]{1,0:T(8,128)S(1)}, u32[]{:S(2)}, u32[]{:S(2)}) collective-permute-start(f32[32,3584]{1,0:T(8,128)S(1)} %get-tuple-element.24), channel_id=1, source_target_pairs={{0,12},{4,16},{8,4},{12,24},{16,28},{20,0},{24,20},{28,8},{1,13},{... | collective-permute-start | bytes 1376264 | tf_op jit(solution)/shard_map/ppermute | solution.py:70
  58.5 13.5 %collective-permute-start.4 = (f32[32,3584]{1,0:T(8,128)S(1)}, f32[32,3584]{1,0:T(8,128)S(1)}, u32[]{:S(2)}, u32[]{:S(2)}) collective-permute-start(f32[32,3584]{1,0:T(8,128)S(1)} %copy-done.3), channel_id=1, source_target_pairs={{0,16},{4,12},{8,24},{12,4},{16,0},{20,28},{24,8},{28,20},{1,17},{... | collective-permute-start | bytes 1376264 | tf_op jit(solution)/shard_map/ppermute | solution.py:70
  64.0 21.4 %copy-start.1 = (bf16[640,3584]{1,0:T(8,128)(2,1)}, bf16[640,3584]{1,0:T(8,128)(2,1)S(1)}, u32[]{:S(2)}) copy-start(bf16[640,3584]{1,0:T(8,128)(2,1)S(1)} %get-tuple-element.6) | copy-start | bytes 13762564
  64.0 24.2 %copy-start = (bf16[640,3584]{1,0:T(8,128)(2,1)}, bf16[640,3584]{1,0:T(8,128)(2,1)S(1)}, u32[]{:S(2)}) copy-start(bf16[640,3584]{1,0:T(8,128)(2,1)S(1)} %get-tuple-element.5) | copy-start | bytes 13762564
  64.0 21.4 %collective-permute-start.20 = (f32[32,3584]{1,0:T(8,128)S(1)}, f32[32,3584]{1,0:T(8,128)S(1)}, u32[]{:S(2)}, u32[]{:S(2)}) collective-permute-start(f32[32,3584]{1,0:T(8,128)S(1)} %get-tuple-element.23), channel_id=1, source_target_pairs={{0,16},{4,12},{8,24},{12,4},{16,0},{20,28},{24,8},{28,20},{1,17},{... | collective-permute-start | bytes 1376264 | tf_op jit(solution)/shard_map/ppermute | solution.py:70
  79.6 11.0 %collective-permute-start.6 = (f32[4,40,128]{2,1,0:T(8,128)S(1)}, f32[4,40,128]{2,1,0:T(8,128)S(1)}, u32[]{:S(2)}, u32[]{:S(2)}) collective-permute-start(f32[4,40,128]{2,1,0:T(8,128)S(1)} %get-tuple-element.31), channel_id=1, source_target_pairs={{0,1},{1,2},{2,3},{3,0},{4,5},{5,6},{6,7},{7,4},{8,9},{9,10},{10,1... | collective-permute-start | bytes 245768 | tf_op jit(solution)/shard_map/ppermute | solution.py:101
  81.4 12.0 %collective-permute-start.7 = (f32[4,40,128]{2,1,0:T(8,128)S(1)}, f32[4,40,128]{2,1,0:T(8,128)S(1)}, u32[]{:S(2)}, u32[]{:S(2)}) collective-permute-start(f32[4,40,128]{2,1,0:T(8,128)S(1)} %get-tuple-element.33), channel_id=1, source_target_pairs={{0,2},{1,3},{2,0},{3,1},{4,6},{5,7},{6,4},{7,5},{8,10},{9,11},{10,... | collective-permute-start | bytes 245768 | tf_op jit(solution)/shard_map/ppermute | solution.py:101
  84.0 9.4 %collective-permute-start.8 = (f32[4,40,128]{2,1,0:T(8,128)S(1)}, f32[4,40,128]{2,1,0:T(8,128)S(1)}, u32[]{:S(2)}, u32[]{:S(2)}) collective-permute-start(f32[4,40,128]{2,1,0:T(8,128)S(1)} %get-tuple-element.32), channel_id=1, source_target_pairs={{0,3},{1,0},{2,1},{3,2},{4,7},{5,4},{6,5},{7,6},{8,11},{9,8},{10,9... | collective-permute-start | bytes 245768 | tf_op jit(solution)/shard_map/ppermute | solution.py:101
  89.5 7.2 %collective-permute-start.22 = (f32[4,40,128]{2,1,0:T(8,128)S(1)}, f32[4,40,128]{2,1,0:T(8,128)S(1)}, u32[]{:S(2)}, u32[]{:S(2)}) collective-permute-start(f32[4,40,128]{2,1,0:T(8,128)S(1)} %get-tuple-element.40), channel_id=1, source_target_pairs={{0,1},{1,2},{2,3},{3,0},{4,5},{5,6},{6,7},{7,4},{8,9},{9,10},{10,1... | collective-permute-start | bytes 245768 | tf_op jit(solution)/shard_map/ppermute | solution.py:101
  90.3 8.4 %collective-permute-start.23 = (f32[4,40,128]{2,1,0:T(8,128)S(1)}, f32[4,40,128]{2,1,0:T(8,128)S(1)}, u32[]{:S(2)}, u32[]{:S(2)}) collective-permute-start(f32[4,40,128]{2,1,0:T(8,128)S(1)} %get-tuple-element.42), channel_id=1, source_target_pairs={{0,2},{1,3},{2,0},{3,1},{4,6},{5,7},{6,4},{7,5},{8,10},{9,11},{10,... | collective-permute-start | bytes 245768 | tf_op jit(solution)/shard_map/ppermute | solution.py:101
  90.6 8.1 %collective-permute-start.24 = (f32[4,40,128]{2,1,0:T(8,128)S(1)}, f32[4,40,128]{2,1,0:T(8,128)S(1)}, u32[]{:S(2)}, u32[]{:S(2)}) collective-permute-start(f32[4,40,128]{2,1,0:T(8,128)S(1)} %get-tuple-element.41), channel_id=1, source_target_pairs={{0,3},{1,0},{2,1},{3,2},{4,7},{5,4},{6,5},{7,6},{8,11},{9,8},{10,9... | collective-permute-start | bytes 245768 | tf_op jit(solution)/shard_map/ppermute | solution.py:101
  99.4 6.3 %collective-permute-start.9 = (f32[80,64]{0,1:T(8,128)S(1)}, f32[80,64]{0,1:T(8,128)S(1)}, u32[]{:S(2)}, u32[]{:S(2)}) collective-permute-start(f32[80,64]{0,1:T(8,128)S(1)} %reshape_squeeze.24), channel_id=1, source_target_pairs={{0,4},{4,0},{8,12},{12,8},{16,20},{20,16},{24,28},{28,24},{1,5},{5... | collective-permute-start | bytes 61448 | tf_op jit(solution)/shard_map/ppermute | solution.py:70
  99.7 6.6 %collective-permute-start.10 = (f32[80,64]{0,1:T(8,128)S(1)}, f32[80,64]{0,1:T(8,128)S(1)}, u32[]{:S(2)}, u32[]{:S(2)}) collective-permute-start(f32[80,64]{0,1:T(8,128)S(1)} %reshape_squeeze.25), channel_id=1, source_target_pairs={{0,12},{4,16},{8,4},{12,24},{16,28},{20,0},{24,20},{28,8},{1,13},{... | collective-permute-start | bytes 61448 | tf_op jit(solution)/shard_map/ppermute | solution.py:70
  101.6 6.2 %collective-permute-start.11 = (f32[80,64]{0,1:T(8,128)S(1)}, f32[80,64]{0,1:T(8,128)S(1)}, u32[]{:S(2)}, u32[]{:S(2)}) collective-permute-start(f32[80,64]{0,1:T(8,128)S(1)} %reshape_squeeze.26), channel_id=1, source_target_pairs={{0,20},{4,8},{8,28},{12,0},{16,4},{20,24},{24,12},{28,16},{1,21},{... | collective-permute-start | bytes 61448 | tf_op jit(solution)/shard_map/ppermute | solution.py:70
  102.2 7.0 %collective-permute-start.12 = (f32[80,64]{0,1:T(8,128)S(1)}, f32[80,64]{0,1:T(8,128)S(1)}, u32[]{:S(2)}, u32[]{:S(2)}) collective-permute-start(f32[80,64]{0,1:T(8,128)S(1)} %reshape_squeeze.27), channel_id=1, source_target_pairs={{0,28},{4,24},{8,20},{12,16},{16,12},{20,8},{24,4},{28,0},{1,29},{... | collective-permute-start | bytes 61448 | tf_op jit(solution)/shard_map/ppermute | solution.py:70
  104.8 6.5 %collective-permute-start.25 = (f32[80,64]{0,1:T(8,128)S(1)}, f32[80,64]{0,1:T(8,128)S(1)}, u32[]{:S(2)}, u32[]{:S(2)}) collective-permute-start(f32[80,64]{0,1:T(8,128)S(1)} %reshape_squeeze.28), channel_id=1, source_target_pairs={{0,4},{4,0},{8,12},{12,8},{16,20},{20,16},{24,28},{28,24},{1,5},{5... | collective-permute-start | bytes 61448 | tf_op jit(solution)/shard_map/ppermute | solution.py:70
  105.7 7.2 %collective-permute-start.26 = (f32[80,64]{0,1:T(8,128)S(1)}, f32[80,64]{0,1:T(8,128)S(1)}, u32[]{:S(2)}, u32[]{:S(2)}) collective-permute-start(f32[80,64]{0,1:T(8,128)S(1)} %reshape_squeeze.29), channel_id=1, source_target_pairs={{0,12},{4,16},{8,4},{12,24},{16,28},{20,0},{24,20},{28,8},{1,13},{... | collective-permute-start | bytes 61448 | tf_op jit(solution)/shard_map/ppermute | solution.py:70
  106.4 6.7 %collective-permute-start.27 = (f32[80,64]{0,1:T(8,128)S(1)}, f32[80,64]{0,1:T(8,128)S(1)}, u32[]{:S(2)}, u32[]{:S(2)}) collective-permute-start(f32[80,64]{0,1:T(8,128)S(1)} %reshape_squeeze.30), channel_id=1, source_target_pairs={{0,20},{4,8},{8,28},{12,0},{16,4},{20,24},{24,12},{28,16},{1,21},{... | collective-permute-start | bytes 61448 | tf_op jit(solution)/shard_map/ppermute | solution.py:70
  107.8 5.4 %collective-permute-start.28 = (f32[80,64]{0,1:T(8,128)S(1)}, f32[80,64]{0,1:T(8,128)S(1)}, u32[]{:S(2)}, u32[]{:S(2)}) collective-permute-start(f32[80,64]{0,1:T(8,128)S(1)} %reshape_squeeze.31), channel_id=1, source_target_pairs={{0,28},{4,24},{8,20},{12,16},{16,12},{20,8},{24,4},{28,0},{1,29},{... | collective-permute-start | bytes 61448 | tf_op jit(solution)/shard_map/ppermute | solution.py:70
  109.4 18.9 %slice-start.2 = ((s8[4587520]{0:T(1024)(128)(4,1)}), s8[393216]{0:T(1024)(128)(4,1)S(1)}, s32[]{:S(2)}) async-start(s8[4587520]{0:T(1024)(128)(4,1)} %bitcast.161), calls=%async_computation.2 | async-start | bytes 786432
  109.6 8.0 %collective-permute-start.13 = (f32[4,40,128]{2,1,0:T(8,128)S(1)}, f32[4,40,128]{2,1,0:T(8,128)S(1)}, u32[]{:S(2)}, u32[]{:S(2)}) collective-permute-start(f32[4,40,128]{2,1,0:T(8,128)S(1)} %copy.99), channel_id=1, source_target_pairs={{0,3},{1,0},{2,1},{3,2},{4,7},{5,4},{6,5},{7,6},{8,11},{9,8},{10,9... | collective-permute-start | bytes 245768 | tf_op jit(solution)/shard_map/ppermute | solution.py:113
  111.3 13.3 %collective-permute-start.14 = (f32[4,40,128]{2,1,0:T(8,128)S(1)}, f32[4,40,128]{2,1,0:T(8,128)S(1)}, u32[]{:S(2)}, u32[]{:S(2)}) collective-permute-start(f32[4,40,128]{2,1,0:T(8,128)S(1)} %copy.99), channel_id=1, source_target_pairs={{0,2},{1,3},{2,0},{3,1},{4,6},{5,7},{6,4},{7,5},{8,10},{9,11},{10,... | collective-permute-start | bytes 245768 | tf_op jit(solution)/shard_map/ppermute | solution.py:113
  112.9 11.8 %collective-permute-start.15 = (f32[4,40,128]{2,1,0:T(8,128)S(1)}, f32[4,40,128]{2,1,0:T(8,128)S(1)}, u32[]{:S(2)}, u32[]{:S(2)}) collective-permute-start(f32[4,40,128]{2,1,0:T(8,128)S(1)} %copy.99), channel_id=1, source_target_pairs={{0,1},{1,2},{2,3},{3,0},{4,5},{5,6},{6,7},{7,4},{8,9},{9,10},{10,1... | collective-permute-start | bytes 245768 | tf_op jit(solution)/shard_map/ppermute | solution.py:113
  113.5 17.6 %collective-permute-start.29 = (f32[4,40,128]{2,1,0:T(8,128)S(1)}, f32[4,40,128]{2,1,0:T(8,128)S(1)}, u32[]{:S(2)}, u32[]{:S(2)}) collective-permute-start(f32[4,40,128]{2,1,0:T(8,128)S(1)} %copy.101), channel_id=1, source_target_pairs={{0,3},{1,0},{2,1},{3,2},{4,7},{5,4},{6,5},{7,6},{8,11},{9,8},{10,9... | collective-permute-start | bytes 245768 | tf_op jit(solution)/shard_map/ppermute | solution.py:113
  117.4 15.7 %collective-permute-start.30 = (f32[4,40,128]{2,1,0:T(8,128)S(1)}, f32[4,40,128]{2,1,0:T(8,128)S(1)}, u32[]{:S(2)}, u32[]{:S(2)}) collective-permute-start(f32[4,40,128]{2,1,0:T(8,128)S(1)} %copy.101), channel_id=1, source_target_pairs={{0,2},{1,3},{2,0},{3,1},{4,6},{5,7},{6,4},{7,5},{8,10},{9,11},{10,... | collective-permute-start | bytes 245768 | tf_op jit(solution)/shard_map/ppermute | solution.py:113
  117.6 15.5 %collective-permute-start.31 = (f32[4,40,128]{2,1,0:T(8,128)S(1)}, f32[4,40,128]{2,1,0:T(8,128)S(1)}, u32[]{:S(2)}, u32[]{:S(2)}) collective-permute-start(f32[4,40,128]{2,1,0:T(8,128)S(1)} %copy.101), channel_id=1, source_target_pairs={{0,1},{1,2},{2,3},{3,0},{4,5},{5,6},{6,7},{7,4},{8,9},{9,10},{10,1... | collective-permute-start | bytes 245768 | tf_op jit(solution)/shard_map/ppermute | solution.py:113
  124.8 3.6 %slice-start.3 = ((s8[4587520]{0:T(1024)(128)(4,1)}), s8[4194304]{0:T(1024)(128)(4,1)S(1)}, s32[]{:S(2)}) async-start(s8[4587520]{0:T(1024)(128)(4,1)} %bitcast.161), calls=%async_computation.3 | async-start | bytes 8388608
  124.9 4.8 %slice-start = ((s8[4587520]{0:T(1024)(128)(4,1)}), s8[4194304]{0:T(1024)(128)(4,1)S(1)}, s32[]{:S(2)}) async-start(s8[4587520]{0:T(1024)(128)(4,1)} %bitcast.159), calls=%async_computation | async-start | bytes 8388608
  128.4 1.5 slice-start.1
  130.8 8.5 %collective-permute-start.16 = (f32[32,3584]{1,0:T(8,128)S(1)}, f32[32,3584]{1,0:T(8,128)S(1)}, u32[]{:S(2)}, u32[]{:S(2)}) collective-permute-start(f32[32,3584]{1,0:T(8,128)S(1)} %get-tuple-element.13), channel_id=1, source_target_pairs={{0,16},{4,12},{8,24},{12,4},{16,0},{20,28},{24,8},{28,20},{1,17},{... | collective-permute-start | bytes 1376264 | tf_op jit(solution)/shard_map/ppermute | solution.py:70
  131.1 8.3 %collective-permute-start.17 = (f32[32,3584]{1,0:T(8,128)S(1)}, f32[32,3584]{1,0:T(8,128)S(1)}, u32[]{:S(2)}, u32[]{:S(2)}) collective-permute-start(f32[32,3584]{1,0:T(8,128)S(1)} %get-tuple-element.15), channel_id=1, source_target_pairs={{0,4},{4,0},{8,12},{12,8},{16,20},{20,16},{24,28},{28,24},{1,5},{5... | collective-permute-start | bytes 1376264 | tf_op jit(solution)/shard_map/ppermute | solution.py:70
  131.1 10.9 %collective-permute-start.18 = (f32[32,3584]{1,0:T(8,128)S(1)}, f32[32,3584]{1,0:T(8,128)S(1)}, u32[]{:S(2)}, u32[]{:S(2)}) collective-permute-start(f32[32,3584]{1,0:T(8,128)S(1)} %get-tuple-element.14), channel_id=1, source_target_pairs={{0,20},{4,8},{8,28},{12,0},{16,4},{20,24},{24,12},{28,16},{1,21},{... | collective-permute-start | bytes 1376264 | tf_op jit(solution)/shard_map/ppermute | solution.py:70
  136.1 13.1 %collective-permute-start.32 = (f32[32,3584]{1,0:T(8,128)S(1)}, f32[32,3584]{1,0:T(8,128)S(1)}, u32[]{:S(2)}, u32[]{:S(2)}) collective-permute-start(f32[32,3584]{1,0:T(8,128)S(1)} %get-tuple-element.18), channel_id=1, source_target_pairs={{0,16},{4,12},{8,24},{12,4},{16,0},{20,28},{24,8},{28,20},{1,17},{... | collective-permute-start | bytes 1376264 | tf_op jit(solution)/shard_map/ppermute | solution.py:70
  136.4 12.8 %collective-permute-start.33 = (f32[32,3584]{1,0:T(8,128)S(1)}, f32[32,3584]{1,0:T(8,128)S(1)}, u32[]{:S(2)}, u32[]{:S(2)}) collective-permute-start(f32[32,3584]{1,0:T(8,128)S(1)} %get-tuple-element.20), channel_id=1, source_target_pairs={{0,4},{4,0},{8,12},{12,8},{16,20},{20,16},{24,28},{28,24},{1,5},{5... | collective-permute-start | bytes 1376264 | tf_op jit(solution)/shard_map/ppermute | solution.py:70
  139.4 12.5 %collective-permute-start.34 = (f32[32,3584]{1,0:T(8,128)S(1)}, f32[32,3584]{1,0:T(8,128)S(1)}, u32[]{:S(2)}, u32[]{:S(2)}) collective-permute-start(f32[32,3584]{1,0:T(8,128)S(1)} %get-tuple-element.19), channel_id=1, source_target_pairs={{0,20},{4,8},{8,28},{12,0},{16,4},{20,24},{24,12},{28,16},{1,21},{... | collective-permute-start | bytes 1376264 | tf_op jit(solution)/shard_map/ppermute | solution.py:70

commit v2 on v0

v2 whole, which is shorter than its diff:
```python
import functools
import math

import jax
import jax.numpy as jnp
from jax import lax
from jax.experimental import pallas as pl
from jax.experimental.pallas import tpu as pltpu
from jax.sharding import PartitionSpec as P

VMEM = pl.BlockSpec(memory_space=pltpu.VMEM)
PARAMS = pltpu.CompilerParams(vmem_limit_bytes=20 * 2**20)


def routes(side):
    place = lambda a, b, core: ((a % side) * side + b % side) * 2 + core
    every = [(a, b, core) for a in range(side) for b in range(side) for core in (0, 1)]

    def along(step, cross, which):
        pairs = []
        for a, b, core in every:
            moves_a = {"rows": core ^ cross == 1, "columns": core ^ cross == 0, "results": core == 0}
            there = (a + step, b) if moves_a[which] else (a, b + step)
            pairs.append((place(a, b, core), place(*there, core ^ cross)))
        return pairs

    def swap(row, column):
        pairs = []
        for a, b, core in every:
            there = (a + column, b + row) if core == 0 else (a + row, b + column)
            pairs.append((place(a, b, core), place(*there, 1 - core)))
        return pairs

    return along, swap


def split(x):
    high = x.astype(jnp.bfloat16)
    return high, (x - high.astype(jnp.float32)).astype(jnp.bfloat16)


def dot(left, right):
    return jnp.dot(left, right, preferred_element_type=jnp.float32)


def block_of(size, most):
    return next(b for b in range(most, 0, -128) if size % b == 0)


def cut_kernel(cuts, calib, turned, *refs):
    outs, sems = refs[:-1], refs[-1]
    half = turned.shape[1] // 2
    core = lax.axis_index("tok") & 1
    copies = []
    for source, start, size in [(turned, 0, turned.shape[0])] + [(calib, *cut) for cut in cuts]:
        for first in (1 - core, core):
            at = pl.ds(pl.multiple_of(first * half, half), half)
            k = len(copies)
            copy = pltpu.make_async_copy(
                source.at[pl.ds(start, size), at], outs[k], sems.at[k]
            )
            copy.start()
            copies.append(copy)
    for copy in copies:
        copy.wait()


def cut(calib, turned, cuts):
    half = calib.shape[1] // 2
    sizes = [turned.shape[0]] + [size for _, size in cuts]
    return pl.pallas_call(
        functools.partial(cut_kernel, cuts),
        out_shape=[jax.ShapeDtypeStruct((n, half), jnp.float32) for n in sizes for _ in range(2)],
        in_specs=[pl.BlockSpec(memory_space=pltpu.HBM)] * 2,
        out_specs=[VMEM] * (2 * len(sizes)),
        scratch_shapes=[pltpu.SemaphoreType.DMA((2 * len(sizes),))],
        compiler_params=PARAMS,
        name="cut",
    )(calib, turned)


def turn_kernel(*refs):
    inputs, out = refs[:-1], refs[-1]
    width, half = inputs[0].shape
    columns = width * len(inputs)
    step = block_of(half, 512)

    @pl.loop(0, half // step)
    def _(i):
        at = pl.ds(pl.multiple_of(i * step, step), step)
        x = jnp.concatenate([ref[:, at] for ref in inputs], 0).T
        out[at, :columns], out[at, columns:] = split(x)


def turn(inputs):
    width, half = inputs[0].shape
    return pl.pallas_call(
        turn_kernel,
        out_shape=jax.ShapeDtypeStruct((half, 2 * width * len(inputs)), jnp.bfloat16),
        in_specs=[VMEM] * len(inputs),
        out_specs=VMEM,
        compiler_params=PARAMS,
        name="turn",
    )(*inputs)


def mix_kernel(count, zs, *refs):
    inputs, cols = refs[:count], refs[count]
    pieces, (high, low), acc = refs[count + 1 : count + 1 + zs], refs[-3:-1], refs[-1]
    half = inputs[0].shape[1]
    width = acc.shape[1]
    z = lax.axis_index("feat")
    step = block_of(half, 1024)
    acc[...] = jnp.zeros(acc.shape, jnp.float32)

    @pl.loop(0, half // step)
    def _(i):
        at = pl.ds(pl.multiple_of(i * step, step), step)
        h, l = split(jnp.concatenate([x[:, at] for x in inputs], 0))
        high[:, at], low[:, at] = h, l
        w = cols[at, :]
        d = dot(h, w)
        acc[...] += d[:, :width] + (d[:, width:] + dot(l, w[:, :width]))

    first = 0
    for x in inputs:
        part = x.shape[0] // zs
        for s in range(zs):
            pieces[s][first // zs : first // zs + part] = acc[pl.ds(first + (z ^ s) * part, part)]
        first += x.shape[0]


def mix(inputs, cols, zs):
    count, half = len(inputs), inputs[0].shape[1]
    rows = sum(x.shape[0] for x in inputs)
    width = cols.shape[1] // 2
    act = jax.ShapeDtypeStruct((rows, half), jnp.bfloat16)
    piece = jax.ShapeDtypeStruct((rows // zs, width), jnp.float32)
    outs = pl.pallas_call(
        functools.partial(mix_kernel, count, zs),
        out_shape=[piece] * zs + [act] * 2,
        in_specs=[VMEM] * (count + 1),
        out_specs=[VMEM] * (zs + 2),
        scratch_shapes=[pltpu.VMEM((rows, width), jnp.float32)],
        compiler_params=PARAMS,
        cost_estimate=pl.CostEstimate(
            flops=6 * rows * half * width,
            bytes_accessed=8 * rows * half + 4 * half * width,
            transcendentals=0,
        ),
        name="mix",
    )(*inputs, cols)
    return outs[:zs], outs[zs:]


def pack_kernel(side, zs, moves, *refs):
    total, outs = refs[len(moves) * zs], refs[len(moves) * zs + 1 :]
    rows, columns = total.shape
    head = rows // side
    part, width = head // 2, columns // side // 2
    for k, segments in enumerate(moves):
        got = refs[k * zs : (k + 1) * zs]
        for start, size, to in segments:
            x = got[0][start : start + size]
            for g in got[1:]:
                x = x + g[start : start + size]
            total[to : to + size] = x
    for r in range(side):
        for q in range(side):
            out = outs[r * side + q]
            for e in (0, 1):
                a = r * head + (1 - e) * part
                x = total[a : a + part, 2 * q * width : 2 * (q + 1) * width]
                out[e * part : (e + 1) * part] = jnp.concatenate([x[:, width:], x[:, :width]], 1)


def pack(side, groups, moves):
    zs, columns = len(groups[0]), groups[0][0].shape[1]
    rows = sum(group[0].shape[0] for group in groups)
    block = jax.ShapeDtypeStruct((rows // side, columns // side), jnp.float32)
    outs = pl.pallas_call(
        functools.partial(pack_kernel, side, zs, moves),
        out_shape=[jax.ShapeDtypeStruct((rows, columns), jnp.float32)] + [block] * side**2,
        in_specs=[VMEM] * (len(moves) * zs),
        out_specs=[VMEM] * (1 + side**2),
        compiler_params=PARAMS,
        name="pack",
    )(*[x for group in groups for x in group])
    return outs[0], outs[1:]


def merge_kernel(side, factor, qs, count, *refs):
    out = refs[-1]
    first = 0
    for c in range(count):
        total, *got = refs[c * (1 + side * len(qs)) : (c + 1) * (1 + side * len(qs))]
        head, width = got[0].shape
        for i, q in enumerate(qs):
            for r in range(side):
                x = total[r * head : (r + 1) * head, q * width : (q + 1) * width]
                x = (x + got[i * side + r][...]) * factor
                out[first + r * head : first + (r + 1) * head, i * width : (i + 1) * width] = x
        first += total.shape[0]


def merge(side, factor, qs, chunks):
    inputs = []
    for total, got in chunks:
        inputs += [total] + [got[(-q % side) * side + -r % side] for q in qs for r in range(side)]
    rows = sum(total.shape[0] for total, _ in chunks)
    columns = chunks[0][0].shape[1] // side * len(qs)
    return pl.pallas_call(
        functools.partial(merge_kernel, side, factor, qs, len(chunks)),
        out_shape=jax.ShapeDtypeStruct((rows, columns), jnp.float32),
        in_specs=[VMEM] * len(inputs),
        out_specs=VMEM,
        compiler_params=PARAMS,
        name="merge",
    )(*inputs)


def term_kernel(zs, spots, groups, *refs):
    got = [refs[c * zs : (c + 1) * zs] for c in range(len(spots))]
    refs = refs[len(spots) * zs :]
    acts = refs[: 2 * groups]
    outs, full = refs[2 * groups : -1], refs[-1]
    columns = full.shape[1]
    width, half = outs[0].shape
    z = lax.axis_index("feat")
    for pieces, segments in zip(got, spots):
        for s in range(zs):
            for at, part, to in segments:
                full[pl.ds(to + (z ^ s) * part, part)] = pieces[s][at : at + part]
    h, l = split(full[...].T)
    both = jnp.concatenate([h, l], 0)
    step = block_of(half, 512)

    @pl.loop(0, half // step)
    def _(i):
        at = pl.ds(pl.multiple_of(i * step, step), step)
        high = jnp.concatenate([x[:, at] for x in acts[::2]], 0)
        low = jnp.concatenate([x[:, at] for x in acts[1::2]], 0)
        d = dot(both, high)
        total = d[:columns] + (d[columns:] + dot(h, low))
        for o, out in enumerate(outs):
            out[:, at] = total[o * width : (o + 1) * width]


def terms(got, acts, spots, width, cost=1):
    zs, columns = len(got[0]), got[0][0].shape[1]
    half = acts[0][0].shape[1]
    count = columns // width
    rows = sum(act[0].shape[0] for act in acts)
    return pl.pallas_call(
        functools.partial(term_kernel, zs, spots, len(acts)),
        out_shape=[jax.ShapeDtypeStruct((width, half), jnp.float32)] * count,
        in_specs=[VMEM] * (zs * len(got) + 2 * len(acts)),
        out_specs=[VMEM] * count,
        scratch_shapes=[pltpu.VMEM((rows, columns), jnp.float32)],
        compiler_params=PARAMS,
        cost_estimate=pl.CostEstimate(
            flops=cost * 6 * rows * columns * half,
            bytes_accessed=cost * (4 * rows * half + 4 * columns * half),
            transcendentals=0,
        ),
        name="term",
    )(*[x for pieces in got for x in pieces], *[x for act in acts for x in act])


def join_kernel(count, *refs):
    out = refs[-1]
    core = lax.axis_index("tok") & 1
    half = out.shape[1] // 2
    for side, at in ((refs[:count], core), (refs[count : 2 * count], 1 - core)):
        total = side[0][...]
        for x in side[1:]:
            total = total + x[...]
        out[:, pl.ds(pl.multiple_of(at * half, half), half)] = total


def arrived_kernel(*refs):
    refs[-1][...] = jnp.zeros_like(refs[-1])


def arrived(blocks):
    return pl.pallas_call(
        arrived_kernel,
        out_shape=jax.ShapeDtypeStruct((8, 128), jnp.float32),
        in_specs=[pl.BlockSpec(memory_space=pl.ANY)] * len(blocks),
        out_specs=VMEM,
        compiler_params=PARAMS,
        cost_estimate=pl.CostEstimate(flops=10**10, bytes_accessed=0, transcendentals=0),
        name="arrived",
    )(*blocks)


def join(own, other, mark):
    width, half = own[0].shape
    rows = 16 if width % 16 == 0 else width
    return pl.pallas_call(
        functools.partial(join_kernel, len(own)),
        grid=(width // rows,),
        out_shape=jax.ShapeDtypeStruct((width, 2 * half), jnp.float32),
        in_specs=[pl.BlockSpec((rows, half), lambda i: (i, 0))] * (2 * len(own))
        + [pl.BlockSpec(memory_space=pl.ANY)],
        out_specs=pl.BlockSpec((rows, 2 * half), lambda i: (i, 0)),
        compiler_params=PARAMS,
        name="join",
    )(*own, *other, mark)


def shards(side, calib, weight):
    zs = lax.axis_size("feat")
    tokens = calib.shape[0]
    width = weight.shape[1]
    along, swap = routes(side)
    turns = range(side)
    send = lambda x, pairs: lax.ppermute(x, "tok", pairs)
    across = lambda x, s: lax.ppermute(x, "feat", [(i, i ^ s) for i in range(zs)])
    factor = 1.0 / math.sqrt(tokens * lax.axis_size("tok"))
    unit = 8 * zs if tokens % (8 * zs) == 0 else zs
    late = unit * max(1, tokens // unit * 2 // 5)
    sizes = [tokens - late, late]

    def reduce(group, cols):
        pieces, act = mix(group, cols, zs)
        return list(pieces[:1]) + [across(pieces[s], s) for s in order][::-1], act

    order = range(zs - 1, 0, -1)

    def far(own, other, which):
        got = []
        for r in turns[1:]:
            got.append(send(own, along(side - r, 0, which)))
            got.append(send(other, along(side - r, 1, which)))
        return got

    cuts = [(0, sizes[0]), (sizes[0], sizes[1])]
    parts = cut(calib, weight.T, cuts)
    other, own = parts[:2]
    cols = turn([own, send(other, along(0, 1, "columns"))] + far(own, other, "columns"))
    near = []
    for c in (0, 1):
        other, own = parts[2 + 2 * c : 4 + 2 * c]
        near += [own, send(other, along(0, 1, "rows"))]
    hold = lax.optimization_barrier
    last, act = reduce(near, cols)
    acts, groups = [act], [last]
    for other, own in (parts[2:4], parts[4:6]):
        group, groups[-1] = hold((far(own, other, "rows"), groups[-1]))
        last, act = reduce(group, cols)
        acts.append(act)
        groups.append(last)

    part, first = tokens // zs, 2 * tokens
    moves, spots = [[], [], []], []
    for c in (0, 1):
        size = sizes[c] // zs
        for p in range(2 * side):
            at = p * part + c * sizes[0] // zs
            if p < 2:
                start = 2 * c * sizes[0] + p * sizes[c]
                moves[0].append((start // zs, size, at))
            else:
                start = first + (p - 2) * sizes[c]
                moves[c + 1].append(((p - 2) * size, size, at))
            spots.append((at, size, start))
        first += (2 * side - 2) * sizes[c]

    total, payloads = pack(side, groups, moves)
    pairs = [swap(r, q) for r in turns for q in turns]
    chunk = (total, [send(x, pair) for x, pair in zip(payloads, pairs)])

    def spread(mine):
        return [mine] + [across(mine, s) for s in order][::-1]

    away = spread(merge(side, factor, turns[1:], [chunk]))
    here = merge(side, factor, turns[:1], [chunk])
    here, away = hold((here, away))
    term = terms([away], acts, [spots], width, 0)
    same = [send(term[2 * q - 2], along(q, 0, "results")) for q in turns[1:]]
    cross = [send(term[2 * q - 1], along(q, 1, "results")) for q in turns[1:]]
    here = spread(here)
    here, term = hold((here, term))
    mine, near = terms([here], acts, [spots], width, 0)
    near = send(near, along(0, 1, "results"))
    return join([mine] + same, [near] + cross, arrived(same + cross))


def solution(mesh):
    side = math.isqrt(mesh.shape["tok"] // 2)

    def step(calib, weight):
        return shards(side, calib, weight)

    return jax.shard_map(
        step,
        mesh=mesh,
        in_specs=(P("tok", "feat"), P("feat", "tok")),
        out_specs=P("tok", "feat"),
        check_vma=False,
    )
```

time: 274 us -> 132 us (0.48)
  waiting for transfers between devices: 209 us -> 70 us
  starting transfers between devices: 0.08 us -> 40.6 us
  matrix products: 37.4 us -> 0 us
  Pallas kernels: 0 us -> 17.3 us
  blocking collectives: 14.4 us -> 0 us
  between operations: 13.1 us -> 0.16 us
  local copies, waits for them, and re-layouts: 0 us -> 3.8 us
    reduce_scatter x2 -> x0, waiting for transfers between devices: 123 us -> none  [the longest x1 103 us: shards(): lax.psum_scatter(term * factor, 'tok', scatter_dimension=0, tiled=True)]
    all_gather x1 -> x0, waiting for transfers between devices: 85.7 us -> none  [shards(): lax.all_gather(weight, 'tok', axis=1, tiled=True)]
    ppermute x0 -> x31, waiting for transfers between devices: none -> 70 us  [the longest x16 52.1 us: shards(): send = lambda x, pairs: lax.ppermute(x, 'tok', pairs)]
    ppermute x0 -> x31, starting transfers between devices: none -> 40.6 us  [the longest x15 26.5 us: shards(): lax.ppermute(x, 'feat', [(i, i ^ s) for i in range(zs)])]
    dot_general x2 -> x0, matrix products: 37.4 us -> none  [the longest x1 20.3 us: shards(): jnp.dot(calib, lax.all_gather(weight, 'tok', axis=1, tiled=True), precisi...]
    pallas_call x0 -> x12, Pallas kernels: none -> 17.3 us  [the longest x2 7 us: terms(): pl.pallas_call(functools.partial(term_kernel, zs, spots, len(acts)), out_...]
    all_gather x1 -> x0, blocking collectives: 14.4 us -> none  [shards(): mixed = lax.all_gather(shared, 'feat', axis=1, tiled=True)]
    unnamed x0 -> x4, local copies, waits for them, and re-layouts: none -> 3.8 us
  transfers between devices with their start and end apart: 3 -> 31, of which waited for: 3 -> 17; matrix products, arithmetic and copies ran while one was open for 0% -> 0% of each run, Pallas kernels for 0% -> 7%
where the time goes in v2:
time: 132 us
  waiting for transfers between devices  70 us (53%)
  starting transfers between devices  40.6 us (31%)
  Pallas kernels  17.3 us (13%)
  local copies, waits for them, and re-layouts  3.8 us (3%)
    ppermute x16, waiting for transfers between devices, shards(): send = lambda x, pairs: lax.ppermute(x, 'tok', pairs)  52.1 us
    ppermute x15, starting transfers between devices, shards(): lax.ppermute(x, 'feat', [(i, i ^ s) for i in range(zs)])  26.5 us
    ppermute x15, waiting for transfers between devices, shards(): lax.ppermute(x, 'feat', [(i, i ^ s) for i in range(zs)])  17.9 us
    ppermute x16, starting transfers between devices, shards(): send = lambda x, pairs: lax.ppermute(x, 'tok', pairs)  14 us
    pallas_call x2, Pallas kernels, terms(): pl.pallas_call(functools.partial(term_kernel, zs, spots, len(acts)), out_...  7 us
    pallas_call x3, Pallas kernels, mix(): pl.pallas_call(functools.partial(mix_kernel, count, zs), out_shape=[piece...  6.35 us
    unnamed x4, local copies, waits for them, and re-layouts  3.8 us
  transfers between devices with their start and end apart: 31, of which 17 were waited for; matrix products, arithmetic and copies ran while one was open for 0% of the time, Pallas kernels for 7%

profile of v2, /device:TPU:0, one launch (start us, length us, event | category | flops | bytes accessed | tf_op | source)
XLA Modules:
  0.0 131.9 jit_solution(3004614567201969057)
XLA Ops:
  0.0 2.3 %copy-done = f32[160,7168]{1,0:T(8,128)S(1)} copy-done((f32[160,7168]{1,0:T(8,128)S(1)}, f32[160,7168]{1,0:T(8,128)}, u32[]{:S(2)}) %copy-start) | copy-done | bytes 4587544
  2.3 1.5 %copy-done.1 = f32[7168,64]{0,1:T(8,128)S(1)} copy-done((f32[7168,64]{0,1:T(8,128)S(1)}, f32[7168,64]{0,1:T(8,128)}, u32[]{:S(2)}) %copy-start.1) | copy-done | bytes 1835032
  3.8 0.6 cut.1
  4.4 0.5 collective-permute-start.4
  4.9 2.6 %collective-permute-start.5 = (f32[64,3584]{1,0:T(8,128)S(1)}, f32[64,3584]{1,0:T(8,128)S(1)}, u32[]{:S(2)}, u32[]{:S(2)}) collective-permute-start(f32[64,3584]{1,0:T(8,128)S(1)} %get-tuple-element.63.refs_0_), channel_id=1, source_target_pairs={{0,16},{4,12},{8,24},{12,4},{16,0},{20,28},{24,8},{28,20},{1,17},{... | collective-permute-start | bytes 2752520 | tf_op jit(solution)/shard_map/ppermute | solution.py:318
  7.7 0.4 collective-permute-start.2
  8.1 1.8 %collective-permute-start = (f32[96,3584]{1,0:T(8,128)S(1)}, f32[96,3584]{1,0:T(8,128)S(1)}, u32[]{:S(2)}, u32[]{:S(2)}) collective-permute-start(f32[96,3584]{1,0:T(8,128)S(1)} %get-tuple-element.59.refs_0_), channel_id=1, source_target_pairs={{0,8},{4,20},{8,0},{12,28},{16,24},{20,4},{24,16},{28,12},{1,9},{5... | collective-permute-start | bytes 4128776 | tf_op jit(solution)/shard_map/ppermute | solution.py:318
  9.9 18.3 %collective-permute-done.5.refs_2_ = f32[64,3584]{1,0:T(8,128)S(1)} collective-permute-done((f32[64,3584]{1,0:T(8,128)S(1)}, f32[64,3584]{1,0:T(8,128)S(1)}, u32[]{:S(2)}, u32[]{:S(2)}) %collective-permute-start.5) | collective-permute-done | bytes 917536 | tf_op jit(solution)/shard_map/ppermute | solution.py:318
  28.2 0.5 collective-permute-done.6.refs_3_
  28.7 2.0 %collective-permute-start.10 = (f32[64,3584]{1,0:T(8,128)S(1)}, f32[64,3584]{1,0:T(8,128)S(1)}, u32[]{:S(2)}, u32[]{:S(2)}) collective-permute-start(f32[64,3584]{1,0:T(8,128)S(1)} %get-tuple-element.61.refs_2_), channel_id=1, source_target_pairs={{0,8},{4,20},{8,0},{12,28},{16,24},{20,4},{24,16},{28,12},{1,9},{5... | collective-permute-start | bytes 2752520 | tf_op jit(solution)/shard_map/ppermute | solution.py:318
  30.7 1.3 collective-permute-start.11
  32.0 1.4 %turn.1.refs_4_.refs_2_ = bf16[3584,512]{1,0:T(8,128)(2,1)S(1)} custom-call(f32[64,3584]{1,0:T(8,128)S(1)} %get-tuple-element.63.refs_0_, f32[64,3584]{1,0:T(8,128)S(1)} %collective-permute-done.4.refs_1_, f32[64,3584]{1,0:T(8,128)S(1)} %collective-permute-done.5.refs_2_, f32[64,3584]{1,0:T(8,128)S(1)} %collective-permute-done.6.refs_3_), custom_call_target="tpu_custom_call" | custom-call | tf_op jit(solution)/shard_map/turn/pallas_call | solution.py:97
  33.5 2.9 %mix.3 = (f32[80,256]{1,0:T(8,128)S(1)}, f32[80,256]{1,0:T(8,128)S(1)}, f32[80,256]{1,0:T(8,128)S(1)}, f32[80,256]{1,0:T(8,128)S(1)}, bf16[320,3584]{1,0:T(8,128)(2,1)S(1)}, /*index=5*/bf16[320,3584]{1,0:T(8,128)(2,1)S(1)}) custom-call(f32[96,3584]{1,0:T(8,128)S(1)} %get-tuple-element.59.refs_0_, f32[96,3584]{1,0:T(8,128)S(1)} %collective-permute-done.2.refs_1_, ...), custom_call_target="tpu_custom_call" | custom-call | flops 1761607680 | bytes 12845056 | tf_op jit(solution)/shard_map/mix/pallas_call | solution.py:139
  36.3 1.6 %collective-permute-start.7 = (f32[80,256]{1,0:T(8,128)S(1)}, f32[80,256]{1,0:T(8,128)S(1)}, u32[]{:S(2)}, u32[]{:S(2)}) collective-permute-start(f32[80,256]{1,0:T(8,128)S(1)} %get-tuple-element.66), channel_id=1, source_target_pairs={{0,1},{1,0},{2,3},{3,2},{4,5},{5,4},{6,7},{7,6},{8,9},{9,8},{10,11... | collective-permute-start | bytes 245768 | tf_op jit(solution)/shard_map/ppermute | solution.py:319
  38.0 17.1 %collective-permute-done.refs_0_ = f32[96,3584]{1,0:T(8,128)S(1)} collective-permute-done((f32[96,3584]{1,0:T(8,128)S(1)}, f32[96,3584]{1,0:T(8,128)S(1)}, u32[]{:S(2)}, u32[]{:S(2)}) %collective-permute-start) | collective-permute-done | bytes 1376288 | tf_op jit(solution)/shard_map/ppermute | solution.py:318
  55.1 3.0 %collective-permute-start.8 = (f32[80,256]{1,0:T(8,128)S(1)}, f32[80,256]{1,0:T(8,128)S(1)}, u32[]{:S(2)}, u32[]{:S(2)}) collective-permute-start(f32[80,256]{1,0:T(8,128)S(1)} %get-tuple-element.67), channel_id=1, source_target_pairs={{0,2},{1,3},{2,0},{3,1},{4,6},{5,7},{6,4},{7,5},{8,10},{9,11},{10,... | collective-permute-start | bytes 245768 | tf_op jit(solution)/shard_map/ppermute | solution.py:319
  58.1 2.6 %collective-permute-done.1.refs_1_ = f32[96,3584]{1,0:T(8,128)S(1)} collective-permute-done((f32[96,3584]{1,0:T(8,128)S(1)}, f32[96,3584]{1,0:T(8,128)S(1)}, u32[]{:S(2)}, u32[]{:S(2)}) %collective-permute-start.1) | collective-permute-done | bytes 1376288 | tf_op jit(solution)/shard_map/ppermute | solution.py:318
  60.7 3.7 %collective-permute-start.9 = (f32[80,256]{1,0:T(8,128)S(1)}, f32[80,256]{1,0:T(8,128)S(1)}, u32[]{:S(2)}, u32[]{:S(2)}) collective-permute-start(f32[80,256]{1,0:T(8,128)S(1)} %get-tuple-element.68), channel_id=1, source_target_pairs={{0,3},{1,2},{2,1},{3,0},{4,7},{5,6},{6,5},{7,4},{8,11},{9,10},{10,... | collective-permute-start | bytes 245768 | tf_op jit(solution)/shard_map/ppermute | solution.py:319
  64.4 3.2 %collective-permute-done.9.refs_3_ = f32[80,256]{1,0:T(8,128)S(1)} collective-permute-done((f32[80,256]{1,0:T(8,128)S(1)}, f32[80,256]{1,0:T(8,128)S(1)}, u32[]{:S(2)}, u32[]{:S(2)}) %collective-permute-start.9) | collective-permute-done | bytes 81952 | tf_op jit(solution)/shard_map/ppermute | solution.py:319
  67.6 2.0 %mix.4 = (f32[48,256]{1,0:T(8,128)S(1)}, f32[48,256]{1,0:T(8,128)S(1)}, f32[48,256]{1,0:T(8,128)S(1)}, f32[48,256]{1,0:T(8,128)S(1)}, bf16[192,3584]{1,0:T(8,128)(2,1)S(1)}, /*index=5*/bf16[192,3584]{1,0:T(8,128)(2,1)S(1)}) custom-call(f32[96,3584]{1,0:T(8,128)S(1)} %collective-permute-done.refs_0_, f32[96,3584]{1,0:T(8,128)S(1)} %collective-permute-done.1.refs_1_, ...), custom_call_target="tpu_custom_call" | custom-call | flops 1056964608 | bytes 9175040 | tf_op jit(solution)/shard_map/mix/pallas_call | solution.py:139
  69.6 1.8 %collective-permute-start.12 = (f32[48,256]{1,0:T(8,128)S(1)}, f32[48,256]{1,0:T(8,128)S(1)}, u32[]{:S(2)}, u32[]{:S(2)}) collective-permute-start(f32[48,256]{1,0:T(8,128)S(1)} %get-tuple-element.76), channel_id=1, source_target_pairs={{0,1},{1,0},{2,3},{3,2},{4,5},{5,4},{6,7},{7,6},{8,9},{9,8},{10,11... | collective-permute-start | bytes 147464 | tf_op jit(solution)/shard_map/ppermute | solution.py:319
  71.4 2.6 %collective-permute-start.13 = (f32[48,256]{1,0:T(8,128)S(1)}, f32[48,256]{1,0:T(8,128)S(1)}, u32[]{:S(2)}, u32[]{:S(2)}) collective-permute-start(f32[48,256]{1,0:T(8,128)S(1)} %get-tuple-element.77), channel_id=1, source_target_pairs={{0,2},{1,3},{2,0},{3,1},{4,6},{5,7},{6,4},{7,5},{8,10},{9,11},{10,... | collective-permute-start | bytes 147464 | tf_op jit(solution)/shard_map/ppermute | solution.py:319
  74.0 0.7 collective-permute-done.10.refs_0_
  74.8 2.8 %collective-permute-done.11.refs_1_ = f32[64,3584]{1,0:T(8,128)S(1)} collective-permute-done((f32[64,3584]{1,0:T(8,128)S(1)}, f32[64,3584]{1,0:T(8,128)S(1)}, u32[]{:S(2)}, u32[]{:S(2)}) %collective-permute-start.11) | collective-permute-done | bytes 917536 | tf_op jit(solution)/shard_map/ppermute | solution.py:318
  77.6 2.3 %collective-permute-done.14.refs_7_ = f32[48,256]{1,0:T(8,128)S(1)} collective-permute-done((f32[48,256]{1,0:T(8,128)S(1)}, f32[48,256]{1,0:T(8,128)S(1)}, u32[]{:S(2)}, u32[]{:S(2)}) %collective-permute-start.14) | collective-permute-done | bytes 49184 | tf_op jit(solution)/shard_map/ppermute | solution.py:319
  79.9 1.5 %mix.5 = (f32[32,256]{1,0:T(8,128)S(1)}, f32[32,256]{1,0:T(8,128)S(1)}, f32[32,256]{1,0:T(8,128)S(1)}, f32[32,256]{1,0:T(8,128)S(1)}, bf16[128,3584]{1,0:T(8,128)(2,1)S(1)}, /*index=5*/bf16[128,3584]{1,0:T(8,128)(2,1)S(1)}) custom-call(f32[64,3584]{1,0:T(8,128)S(1)} %collective-permute-done.10.refs_0_, f32[64,3584]{1,0:T(8,128)S(1)} %collective-permute-done.11.refs_1_, ...), custom_call_target="tpu_custom_call" | custom-call | flops 704643072 | bytes 7340032 | tf_op jit(solution)/shard_map/mix/pallas_call | solution.py:139
  81.5 2.1 %collective-permute-start.16 = (f32[32,256]{1,0:T(8,128)S(1)}, f32[32,256]{1,0:T(8,128)S(1)}, u32[]{:S(2)}, u32[]{:S(2)}) collective-permute-start(f32[32,256]{1,0:T(8,128)S(1)} %get-tuple-element.87), channel_id=1, source_target_pairs={{0,2},{1,3},{2,0},{3,1},{4,6},{5,7},{6,4},{7,5},{8,10},{9,11},{10,... | collective-permute-start | bytes 98312 | tf_op jit(solution)/shard_map/ppermute | solution.py:319
  83.6 2.2 %collective-permute-start.17 = (f32[32,256]{1,0:T(8,128)S(1)}, f32[32,256]{1,0:T(8,128)S(1)}, u32[]{:S(2)}, u32[]{:S(2)}) collective-permute-start(f32[32,256]{1,0:T(8,128)S(1)} %get-tuple-element.88), channel_id=1, source_target_pairs={{0,3},{1,2},{2,1},{3,0},{4,7},{5,6},{6,5},{7,4},{8,11},{9,10},{10,... | collective-permute-start | bytes 98312 | tf_op jit(solution)/shard_map/ppermute | solution.py:319
  85.8 0.7 collective-permute-done.16.refs_10_
  86.5 2.7 %collective-permute-done.17.refs_11_ = f32[32,256]{1,0:T(8,128)S(1)} collective-permute-done((f32[32,256]{1,0:T(8,128)S(1)}, f32[32,256]{1,0:T(8,128)S(1)}, u32[]{:S(2)}, u32[]{:S(2)}) %collective-permute-start.17) | collective-permute-done | bytes 32800 | tf_op jit(solution)/shard_map/ppermute | solution.py:319
  89.5 2.7 %collective-permute-start.21 = (f32[80,128]{1,0:T(8,128)S(1)}, f32[80,128]{1,0:T(8,128)S(1)}, u32[]{:S(2)}, u32[]{:S(2)}) collective-permute-start(f32[80,128]{1,0:T(8,128)S(1)} %get-tuple-element.93), channel_id=1, source_target_pairs={{0,28},{4,24},{8,20},{12,16},{16,12},{20,8},{24,4},{28,0},{1,29},{... | collective-permute-start | bytes 122888 | tf_op jit(solution)/shard_map/ppermute | solution.py:318
  92.1 0.8 collective-permute-done.20.refs_1_
  92.9 1.4 %collective-permute-done.21.refs_2_ = f32[80,128]{1,0:T(8,128)S(1)} collective-permute-done((f32[80,128]{1,0:T(8,128)S(1)}, f32[80,128]{1,0:T(8,128)S(1)}, u32[]{:S(2)}, u32[]{:S(2)}) %collective-permute-start.21) | collective-permute-done | bytes 40992 | tf_op jit(solution)/shard_map/ppermute | solution.py:318
  94.4 2.6 %collective-permute-start.23 = (f32[160,128]{1,0:T(8,128)S(1)}, f32[160,128]{1,0:T(8,128)S(1)}, u32[]{:S(2)}, u32[]{:S(2)}) collective-permute-start(f32[160,128]{1,0:T(8,128)S(1)} %merge.3.refs_0_), channel_id=1, source_target_pairs={{0,2},{1,3},{2,0},{3,1},{4,6},{5,7},{6,4},{7,5},{8,10},{9,11},{10,... | collective-permute-start | bytes 245768 | tf_op jit(solution)/shard_map/ppermute | solution.py:319
  97.0 1.8 %collective-permute-start.24 = (f32[160,128]{1,0:T(8,128)S(1)}, f32[160,128]{1,0:T(8,128)S(1)}, u32[]{:S(2)}, u32[]{:S(2)}) collective-permute-start(f32[160,128]{1,0:T(8,128)S(1)} %merge.3.refs_0_), channel_id=1, source_target_pairs={{0,3},{1,2},{2,1},{3,0},{4,7},{5,6},{6,5},{7,4},{8,11},{9,10},{10,... | collective-permute-start | bytes 245768 | tf_op jit(solution)/shard_map/ppermute | solution.py:319
  99.0 0.9 collective-permute-start.19
  100.0 2.5 %collective-permute-done.19.refs_2_ = f32[80,128]{1,0:T(8,128)S(1)} collective-permute-done((f32[80,128]{1,0:T(8,128)S(1)}, f32[80,128]{1,0:T(8,128)S(1)}, u32[]{:S(2)}, u32[]{:S(2)}) %collective-permute-start.19) | collective-permute-done | bytes 40992 | tf_op jit(solution)/shard_map/ppermute | solution.py:318
  102.5 1.5 %collective-permute-done.24.refs_3_ = f32[160,128]{1,0:T(8,128)S(1)} collective-permute-done((f32[160,128]{1,0:T(8,128)S(1)}, f32[160,128]{1,0:T(8,128)S(1)}, u32[]{:S(2)}, u32[]{:S(2)}) %collective-permute-start.24) | collective-permute-done | bytes 81952 | tf_op jit(solution)/shard_map/ppermute | solution.py:319
  104.0 3.5 %term.2 = (f32[64,3584]{1,0:T(8,128)S(1)}, f32[64,3584]{1,0:T(8,128)S(1)}) custom-call(f32[160,128]{1,0:T(8,128)S(1)} %merge.3.refs_0_, f32[160,128]{1,0:T(8,128)S(1)} %collective-permute-done.22.refs_1_, f32[160,128]{1,0:T(8,128)S(1)} %collective-permute-done.23.refs_2_, f32[160,128]{1,0:T(8,128)S(1)} %collective-permute-done.24.refs_3_, ...), custom_call_target="tpu_custom_call" | custom-call | tf_op jit(solution)/shard_map/term/pallas_call | solution.py:254
  107.6 1.3 collective-permute-start.28
  108.8 2.5 %collective-permute-start.25 = (f32[160,128]{1,0:T(8,128)S(1)}, f32[160,128]{1,0:T(8,128)S(1)}, u32[]{:S(2)}, u32[]{:S(2)}) collective-permute-start(f32[160,128]{1,0:T(8,128)S(1)} %merge.2.refs_0_), channel_id=1, source_target_pairs={{0,1},{1,0},{2,3},{3,2},{4,5},{5,4},{6,7},{7,6},{8,9},{9,8},{10,11... | collective-permute-start | bytes 245768 | tf_op jit(solution)/shard_map/ppermute | solution.py:319
  111.4 0.6 collective-permute-start.26
  111.9 1.8 %collective-permute-start.27 = (f32[160,128]{1,0:T(8,128)S(1)}, f32[160,128]{1,0:T(8,128)S(1)}, u32[]{:S(2)}, u32[]{:S(2)}) collective-permute-start(f32[160,128]{1,0:T(8,128)S(1)} %merge.2.refs_0_), channel_id=1, source_target_pairs={{0,3},{1,2},{2,1},{3,0},{4,7},{5,6},{6,5},{7,4},{8,11},{9,10},{10,... | collective-permute-start | bytes 245768 | tf_op jit(solution)/shard_map/ppermute | solution.py:319
  113.7 0.7 collective-permute-done.25.refs_1_
  114.4 6.7 %collective-permute-done.26.refs_2_ = f32[160,128]{1,0:T(8,128)S(1)} collective-permute-done((f32[160,128]{1,0:T(8,128)S(1)}, f32[160,128]{1,0:T(8,128)S(1)}, u32[]{:S(2)}, u32[]{:S(2)}) %collective-permute-start.26) | collective-permute-done | bytes 81952 | tf_op jit(solution)/shard_map/ppermute | solution.py:319
  121.1 3.5 %term.3 = (f32[64,3584]{1,0:T(8,128)S(1)}, f32[64,3584]{1,0:T(8,128)S(1)}) custom-call(f32[160,128]{1,0:T(8,128)S(1)} %merge.2.refs_0_, f32[160,128]{1,0:T(8,128)S(1)} %collective-permute-done.25.refs_1_, f32[160,128]{1,0:T(8,128)S(1)} %collective-permute-done.26.refs_2_, f32[160,128]{1,0:T(8,128)S(1)} %collective-permute-done.27.refs_3_, ...), custom_call_target="tpu_custom_call" | custom-call | tf_op jit(solution)/shard_map/term/pallas_call | solution.py:254
  124.7 5.4 %collective-permute-done.30.refs_1_.refs_3_ = f32[64,3584]{1,0:T(8,128)S(1)} collective-permute-done((f32[64,3584]{1,0:T(8,128)S(1)}, f32[64,3584]{1,0:T(8,128)S(1)}, u32[]{:S(2)}, u32[]{:S(2)}) %collective-permute-start.30) | collective-permute-done | bytes 917536 | tf_op jit(solution)/shard_map/ppermute | solution.py:318
  130.1 1.8 %join.1 = f32[64,7168]{1,0:T(8,128)} custom-call(f32[64,3584]{1,0:T(8,128)S(1)} %get-tuple-element.111.refs_0_, f32[64,3584]{1,0:T(8,128)S(1)} %collective-permute-done.28.refs_0_.refs_1_, f32[64,3584]{1,0:T(8,128)S(1)} %collective-permute-done.29.refs_2_, f32[64,3584]{1,0:T(8,128)S(1)} %collective-permute-done.30.refs_1_.refs_3_, f32[8,128]{1,0:T(8,128)S(1)} %arrived.1.refs_4_), custom_call_target="tpu_custom_call" | custom-call | tf_op jit(solution)/shard_map/join/pallas_call | solution.py:300
  (30 shorter events, 1.0 us)
Async XLA Ops:
  0.0 2.3 %copy-start = (f32[160,7168]{1,0:T(8,128)S(1)}, f32[160,7168]{1,0:T(8,128)}, u32[]{:S(2)}) copy-start(f32[160,7168]{1,0:T(8,128)} %calib.1) | copy-start | bytes 13762564
  2.3 1.5 %copy-start.1 = (f32[7168,64]{0,1:T(8,128)S(1)}, f32[7168,64]{0,1:T(8,128)}, u32[]{:S(2)}) copy-start(f32[7168,64]{0,1:T(8,128)} %param.3) | copy-start | bytes 5505028
  4.4 3.7 %collective-permute-start.4 = (f32[64,3584]{1,0:T(8,128)S(1)}, f32[64,3584]{1,0:T(8,128)S(1)}, u32[]{:S(2)}, u32[]{:S(2)}) collective-permute-start(f32[64,3584]{1,0:T(8,128)S(1)} %get-tuple-element.64), channel_id=1, source_target_pairs={{0,4},{4,0},{8,12},{12,8},{16,20},{20,16},{24,28},{28,24},{1,5},{5... | collective-permute-start | bytes 2752520 | tf_op jit(solution)/shard_map/ppermute | solution.py:318
  4.9 23.3 %collective-permute-start.5 = (f32[64,3584]{1,0:T(8,128)S(1)}, f32[64,3584]{1,0:T(8,128)S(1)}, u32[]{:S(2)}, u32[]{:S(2)}) collective-permute-start(f32[64,3584]{1,0:T(8,128)S(1)} %get-tuple-element.63.refs_0_), channel_id=1, source_target_pairs={{0,16},{4,12},{8,24},{12,4},{16,0},{20,28},{24,8},{28,20},{1,17},{... | collective-permute-start | bytes 2752520 | tf_op jit(solution)/shard_map/ppermute | solution.py:318
  7.5 21.2 %collective-permute-start.6 = (f32[64,3584]{1,0:T(8,128)S(1)}, f32[64,3584]{1,0:T(8,128)S(1)}, u32[]{:S(2)}, u32[]{:S(2)}) collective-permute-start(f32[64,3584]{1,0:T(8,128)S(1)} %get-tuple-element.64), channel_id=1, source_target_pairs={{0,12},{4,16},{8,4},{12,24},{16,28},{20,0},{24,20},{28,8},{1,13},{... | collective-permute-start | bytes 2752520 | tf_op jit(solution)/shard_map/ppermute | solution.py:318
  7.5 23.2 %collective-permute-start.3 = (f32[64,3584]{1,0:T(8,128)S(1)}, f32[64,3584]{1,0:T(8,128)S(1)}, u32[]{:S(2)}, u32[]{:S(2)}) collective-permute-start(f32[64,3584]{1,0:T(8,128)S(1)} %get-tuple-element.62), channel_id=1, source_target_pairs={{0,4},{4,0},{8,12},{12,8},{16,20},{20,16},{24,28},{28,24},{1,5},{5... | collective-permute-start | bytes 2752520 | tf_op jit(solution)/shard_map/ppermute | solution.py:318
  7.7 25.8 %collective-permute-start.2 = (f32[96,3584]{1,0:T(8,128)S(1)}, f32[96,3584]{1,0:T(8,128)S(1)}, u32[]{:S(2)}, u32[]{:S(2)}) collective-permute-start(f32[96,3584]{1,0:T(8,128)S(1)} %get-tuple-element.60), channel_id=1, source_target_pairs={{0,4},{4,0},{8,12},{12,8},{16,20},{20,16},{24,28},{28,24},{1,5},{5... | collective-permute-start | bytes 4128776 | tf_op jit(solution)/shard_map/ppermute | solution.py:318
  8.1 47.0 %collective-permute-start = (f32[96,3584]{1,0:T(8,128)S(1)}, f32[96,3584]{1,0:T(8,128)S(1)}, u32[]{:S(2)}, u32[]{:S(2)}) collective-permute-start(f32[96,3584]{1,0:T(8,128)S(1)} %get-tuple-element.59.refs_0_), channel_id=1, source_target_pairs={{0,8},{4,20},{8,0},{12,28},{16,24},{20,4},{24,16},{28,12},{1,9},{5... | collective-permute-start | bytes 4128776 | tf_op jit(solution)/shard_map/ppermute | solution.py:318
  28.2 32.5 %collective-permute-start.1 = (f32[96,3584]{1,0:T(8,128)S(1)}, f32[96,3584]{1,0:T(8,128)S(1)}, u32[]{:S(2)}, u32[]{:S(2)}) collective-permute-start(f32[96,3584]{1,0:T(8,128)S(1)} %get-tuple-element.60), channel_id=1, source_target_pairs={{0,20},{4,8},{8,28},{12,0},{16,4},{20,24},{24,12},{28,16},{1,21},{... | collective-permute-start | bytes 4128776 | tf_op jit(solution)/shard_map/ppermute | solution.py:318
  28.7 46.1 %collective-permute-start.10 = (f32[64,3584]{1,0:T(8,128)S(1)}, f32[64,3584]{1,0:T(8,128)S(1)}, u32[]{:S(2)}, u32[]{:S(2)}) collective-permute-start(f32[64,3584]{1,0:T(8,128)S(1)} %get-tuple-element.61.refs_2_), channel_id=1, source_target_pairs={{0,8},{4,20},{8,0},{12,28},{16,24},{20,4},{24,16},{28,12},{1,9},{5... | collective-permute-start | bytes 2752520 | tf_op jit(solution)/shard_map/ppermute | solution.py:318
  30.7 46.9 %collective-permute-start.11 = (f32[64,3584]{1,0:T(8,128)S(1)}, f32[64,3584]{1,0:T(8,128)S(1)}, u32[]{:S(2)}, u32[]{:S(2)}) collective-permute-start(f32[64,3584]{1,0:T(8,128)S(1)} %get-tuple-element.62), channel_id=1, source_target_pairs={{0,20},{4,8},{8,28},{12,0},{16,4},{20,24},{24,12},{28,16},{1,21},{... | collective-permute-start | bytes 2752520 | tf_op jit(solution)/shard_map/ppermute | solution.py:318
  36.3 28.1 %collective-permute-start.7 = (f32[80,256]{1,0:T(8,128)S(1)}, f32[80,256]{1,0:T(8,128)S(1)}, u32[]{:S(2)}, u32[]{:S(2)}) collective-permute-start(f32[80,256]{1,0:T(8,128)S(1)} %get-tuple-element.66), channel_id=1, source_target_pairs={{0,1},{1,0},{2,3},{3,2},{4,5},{5,4},{6,7},{7,6},{8,9},{9,8},{10,11... | collective-permute-start | bytes 245768 | tf_op jit(solution)/shard_map/ppermute | solution.py:319
  55.1 9.3 %collective-permute-start.8 = (f32[80,256]{1,0:T(8,128)S(1)}, f32[80,256]{1,0:T(8,128)S(1)}, u32[]{:S(2)}, u32[]{:S(2)}) collective-permute-start(f32[80,256]{1,0:T(8,128)S(1)} %get-tuple-element.67), channel_id=1, source_target_pairs={{0,2},{1,3},{2,0},{3,1},{4,6},{5,7},{6,4},{7,5},{8,10},{9,11},{10,... | collective-permute-start | bytes 245768 | tf_op jit(solution)/shard_map/ppermute | solution.py:319
  60.7 6.9 %collective-permute-start.9 = (f32[80,256]{1,0:T(8,128)S(1)}, f32[80,256]{1,0:T(8,128)S(1)}, u32[]{:S(2)}, u32[]{:S(2)}) collective-permute-start(f32[80,256]{1,0:T(8,128)S(1)} %get-tuple-element.68), channel_id=1, source_target_pairs={{0,3},{1,2},{2,1},{3,0},{4,7},{5,6},{6,5},{7,4},{8,11},{9,10},{10,... | collective-permute-start | bytes 245768 | tf_op jit(solution)/shard_map/ppermute | solution.py:319
  69.6 8.0 %collective-permute-start.12 = (f32[48,256]{1,0:T(8,128)S(1)}, f32[48,256]{1,0:T(8,128)S(1)}, u32[]{:S(2)}, u32[]{:S(2)}) collective-permute-start(f32[48,256]{1,0:T(8,128)S(1)} %get-tuple-element.76), channel_id=1, source_target_pairs={{0,1},{1,0},{2,3},{3,2},{4,5},{5,4},{6,7},{7,6},{8,9},{9,8},{10,11... | collective-permute-start | bytes 147464 | tf_op jit(solution)/shard_map/ppermute | solution.py:319
  71.4 6.2 %collective-permute-start.13 = (f32[48,256]{1,0:T(8,128)S(1)}, f32[48,256]{1,0:T(8,128)S(1)}, u32[]{:S(2)}, u32[]{:S(2)}) collective-permute-start(f32[48,256]{1,0:T(8,128)S(1)} %get-tuple-element.77), channel_id=1, source_target_pairs={{0,2},{1,3},{2,0},{3,1},{4,6},{5,7},{6,4},{7,5},{8,10},{9,11},{10,... | collective-permute-start | bytes 147464 | tf_op jit(solution)/shard_map/ppermute | solution.py:319
  74.0 5.9 %collective-permute-start.14 = (f32[48,256]{1,0:T(8,128)S(1)}, f32[48,256]{1,0:T(8,128)S(1)}, u32[]{:S(2)}, u32[]{:S(2)}) collective-permute-start(f32[48,256]{1,0:T(8,128)S(1)} %get-tuple-element.78), channel_id=1, source_target_pairs={{0,3},{1,2},{2,1},{3,0},{4,7},{5,6},{6,5},{7,4},{8,11},{9,10},{10,... | collective-permute-start | bytes 147464 | tf_op jit(solution)/shard_map/ppermute | solution.py:319
  81.4 4.5 %collective-permute-start.15 = (f32[32,256]{1,0:T(8,128)S(1)}, f32[32,256]{1,0:T(8,128)S(1)}, u32[]{:S(2)}, u32[]{:S(2)}) collective-permute-start(f32[32,256]{1,0:T(8,128)S(1)} %get-tuple-element.86), channel_id=1, source_target_pairs={{0,1},{1,0},{2,3},{3,2},{4,5},{5,4},{6,7},{7,6},{8,9},{9,8},{10,11... | collective-permute-start | bytes 98312 | tf_op jit(solution)/shard_map/ppermute | solution.py:319
  81.5 5.1 %collective-permute-start.16 = (f32[32,256]{1,0:T(8,128)S(1)}, f32[32,256]{1,0:T(8,128)S(1)}, u32[]{:S(2)}, u32[]{:S(2)}) collective-permute-start(f32[32,256]{1,0:T(8,128)S(1)} %get-tuple-element.87), channel_id=1, source_target_pairs={{0,2},{1,3},{2,0},{3,1},{4,6},{5,7},{6,4},{7,5},{8,10},{9,11},{10,... | collective-permute-start | bytes 98312 | tf_op jit(solution)/shard_map/ppermute | solution.py:319
  83.6 5.7 %collective-permute-start.17 = (f32[32,256]{1,0:T(8,128)S(1)}, f32[32,256]{1,0:T(8,128)S(1)}, u32[]{:S(2)}, u32[]{:S(2)}) collective-permute-start(f32[32,256]{1,0:T(8,128)S(1)} %get-tuple-element.88), channel_id=1, source_target_pairs={{0,3},{1,2},{2,1},{3,0},{4,7},{5,6},{6,5},{7,4},{8,11},{9,10},{10,... | collective-permute-start | bytes 98312 | tf_op jit(solution)/shard_map/ppermute | solution.py:319
  89.4 3.5 %collective-permute-start.20 = (f32[80,128]{1,0:T(8,128)S(1)}, f32[80,128]{1,0:T(8,128)S(1)}, u32[]{:S(2)}, u32[]{:S(2)}) collective-permute-start(f32[80,128]{1,0:T(8,128)S(1)} %get-tuple-element.92), channel_id=1, source_target_pairs={{0,12},{4,16},{8,4},{12,24},{16,28},{20,0},{24,20},{28,8},{1,13},{... | collective-permute-start | bytes 122888 | tf_op jit(solution)/shard_map/ppermute | solution.py:318
  89.5 4.8 %collective-permute-start.21 = (f32[80,128]{1,0:T(8,128)S(1)}, f32[80,128]{1,0:T(8,128)S(1)}, u32[]{:S(2)}, u32[]{:S(2)}) collective-permute-start(f32[80,128]{1,0:T(8,128)S(1)} %get-tuple-element.93), channel_id=1, source_target_pairs={{0,28},{4,24},{8,20},{12,16},{16,12},{20,8},{24,4},{28,0},{1,29},{... | collective-permute-start | bytes 122888 | tf_op jit(solution)/shard_map/ppermute | solution.py:318
  94.3 8.2 %collective-permute-start.22 = (f32[160,128]{1,0:T(8,128)S(1)}, f32[160,128]{1,0:T(8,128)S(1)}, u32[]{:S(2)}, u32[]{:S(2)}) collective-permute-start(f32[160,128]{1,0:T(8,128)S(1)} %merge.3.refs_0_), channel_id=1, source_target_pairs={{0,1},{1,0},{2,3},{3,2},{4,5},{5,4},{6,7},{7,6},{8,9},{9,8},{10,11... | collective-permute-start | bytes 245768 | tf_op jit(solution)/shard_map/ppermute | solution.py:319
  94.4 8.1 %collective-permute-start.23 = (f32[160,128]{1,0:T(8,128)S(1)}, f32[160,128]{1,0:T(8,128)S(1)}, u32[]{:S(2)}, u32[]{:S(2)}) collective-permute-start(f32[160,128]{1,0:T(8,128)S(1)} %merge.3.refs_0_), channel_id=1, source_target_pairs={{0,2},{1,3},{2,0},{3,1},{4,6},{5,7},{6,4},{7,5},{8,10},{9,11},{10,... | collective-permute-start | bytes 245768 | tf_op jit(solution)/shard_map/ppermute | solution.py:319
  97.0 7.1 %collective-permute-start.24 = (f32[160,128]{1,0:T(8,128)S(1)}, f32[160,128]{1,0:T(8,128)S(1)}, u32[]{:S(2)}, u32[]{:S(2)}) collective-permute-start(f32[160,128]{1,0:T(8,128)S(1)} %merge.3.refs_0_), channel_id=1, source_target_pairs={{0,3},{1,2},{2,1},{3,0},{4,7},{5,6},{6,5},{7,4},{8,11},{9,10},{10,... | collective-permute-start | bytes 245768 | tf_op jit(solution)/shard_map/ppermute | solution.py:319
  98.8 1.2 collective-permute-start.18
  99.0 3.4 %collective-permute-start.19 = (f32[80,128]{1,0:T(8,128)S(1)}, f32[80,128]{1,0:T(8,128)S(1)}, u32[]{:S(2)}, u32[]{:S(2)}) collective-permute-start(f32[80,128]{1,0:T(8,128)S(1)} %get-tuple-element.91), channel_id=1, source_target_pairs={{0,20},{4,8},{8,28},{12,0},{16,4},{20,24},{24,12},{28,16},{1,21},{... | collective-permute-start | bytes 122888 | tf_op jit(solution)/shard_map/ppermute | solution.py:318
  107.6 17.1 %collective-permute-start.28 = (f32[64,3584]{1,0:T(8,128)S(1)}, f32[64,3584]{1,0:T(8,128)S(1)}, u32[]{:S(2)}, u32[]{:S(2)}) collective-permute-start(f32[64,3584]{1,0:T(8,128)S(1)} %get-tuple-element.105), channel_id=1, source_target_pairs={{0,16},{4,12},{8,24},{12,4},{16,0},{20,28},{24,8},{28,20},{1,17},{... | collective-permute-start | bytes 2752520 | tf_op jit(solution)/shard_map/ppermute | solution.py:318
  108.8 21.2 %collective-permute-start.30 = (f32[64,3584]{1,0:T(8,128)S(1)}, f32[64,3584]{1,0:T(8,128)S(1)}, u32[]{:S(2)}, u32[]{:S(2)}) collective-permute-start(f32[64,3584]{1,0:T(8,128)S(1)} %get-tuple-element.106), channel_id=1, source_target_pairs={{0,20},{4,8},{8,28},{12,0},{16,4},{20,24},{24,12},{28,16},{1,21},{... | collective-permute-start | bytes 2752520 | tf_op jit(solution)/shard_map/ppermute | solution.py:318
  108.8 5.5 %collective-permute-start.25 = (f32[160,128]{1,0:T(8,128)S(1)}, f32[160,128]{1,0:T(8,128)S(1)}, u32[]{:S(2)}, u32[]{:S(2)}) collective-permute-start(f32[160,128]{1,0:T(8,128)S(1)} %merge.2.refs_0_), channel_id=1, source_target_pairs={{0,1},{1,0},{2,3},{3,2},{4,5},{5,4},{6,7},{7,6},{8,9},{9,8},{10,11... | collective-permute-start | bytes 245768 | tf_op jit(solution)/shard_map/ppermute | solution.py:319
  111.4 9.7 %collective-permute-start.26 = (f32[160,128]{1,0:T(8,128)S(1)}, f32[160,128]{1,0:T(8,128)S(1)}, u32[]{:S(2)}, u32[]{:S(2)}) collective-permute-start(f32[160,128]{1,0:T(8,128)S(1)} %merge.2.refs_0_), channel_id=1, source_target_pairs={{0,2},{1,3},{2,0},{3,1},{4,6},{5,7},{6,4},{7,5},{8,10},{9,11},{10,... | collective-permute-start | bytes 245768 | tf_op jit(solution)/shard_map/ppermute | solution.py:319
  111.9 9.2 %collective-permute-start.27 = (f32[160,128]{1,0:T(8,128)S(1)}, f32[160,128]{1,0:T(8,128)S(1)}, u32[]{:S(2)}, u32[]{:S(2)}) collective-permute-start(f32[160,128]{1,0:T(8,128)S(1)} %merge.2.refs_0_), channel_id=1, source_target_pairs={{0,3},{1,2},{2,1},{3,0},{4,7},{5,6},{6,5},{7,4},{8,11},{9,10},{10,... | collective-permute-start | bytes 245768 | tf_op jit(solution)/shard_map/ppermute | solution.py:319
  124.6 5.5 %collective-permute-start.29 = (f32[64,3584]{1,0:T(8,128)S(1)}, f32[64,3584]{1,0:T(8,128)S(1)}, u32[]{:S(2)}, u32[]{:S(2)}) collective-permute-start(f32[64,3584]{1,0:T(8,128)S(1)} %get-tuple-element.112), channel_id=1, source_target_pairs={{0,4},{4,0},{8,12},{12,8},{16,20},{20,16},{24,28},{28,24},{1,5},{5... | collective-permute-start | bytes 2752520 | tf_op jit(solution)/shard_map/ppermute | solution.py:318

commit v3 on v2

--- a/solution.py
+++ b/solution.py
@@ -47,12 +47,12 @@
     return next(b for b in range(most, 0, -128) if size % b == 0)
 
 
-def cut_kernel(cuts, calib, turned, *refs):
+def cut_kernel(cuts, source, *refs):
     outs, sems = refs[:-1], refs[-1]
-    half = turned.shape[1] // 2
+    half = source.shape[1] // 2
     core = lax.axis_index("tok") & 1
     copies = []
-    for source, start, size in [(turned, 0, turned.shape[0])] + [(calib, *cut) for cut in cuts]:
+    for start, size in cuts:
         for first in (1 - core, core):
             at = pl.ds(pl.multiple_of(first * half, half), half)
             k = len(copies)
@@ -65,18 +65,18 @@
         copy.wait()
 
 
-def cut(calib, turned, cuts):
-    half = calib.shape[1] // 2
-    sizes = [turned.shape[0]] + [size for _, size in cuts]
-    return pl.pallas_call(
+def cut(source, cuts):
+    half = source.shape[1] // 2
+    outs = pl.pallas_call(
         functools.partial(cut_kernel, cuts),
-        out_shape=[jax.ShapeDtypeStruct((n, half), jnp.float32) for n in sizes for _ in range(2)],
-        in_specs=[pl.BlockSpec(memory_space=pltpu.HBM)] * 2,
-        out_specs=[VMEM] * (2 * len(sizes)),
-        scratch_shapes=[pltpu.SemaphoreType.DMA((2 * len(sizes),))],
+        out_shape=[jax.ShapeDtypeStruct((n, half), jnp.float32) for _, n in cuts for _ in range(2)],
+        in_specs=[pl.BlockSpec(memory_space=pl.ANY)],
+        out_specs=[VMEM] * (2 * len(cuts)),
+        scratch_shapes=[pltpu.SemaphoreType.DMA((2 * len(cuts),))],
         compiler_params=PARAMS,
         name="cut",
-    )(calib, turned)
+    )(source)
+    return [(outs[2 * i + 1], outs[2 * i]) for i in range(len(cuts))]
 
 
 def turn_kernel(*refs):
@@ -335,10 +335,12 @@
             got.append(send(other, along(side - r, 1, which)))
         return got
 
-    cuts = [(0, sizes[0]), (sizes[0], sizes[1])]
-    parts = cut(calib, weight.T, cuts)
-    other, own = parts[:2]
-    cols = turn([own, send(other, along(0, 1, "columns"))] + far(own, other, "columns"))
+    ((own, other),) = cut(weight.T, [(0, width)])
+    close = send(other, along(0, 1, "columns"))
+    cols = turn([own, close] + far(own, other, "columns"))
+    parts = [own, other]
+    for own, other in cut(calib, [(0, sizes[0]), (sizes[0], sizes[1])]):
+        parts += [other, own]
     near = []
     for c in (0, 1):
         other, own = parts[2 + 2 * c : 4 + 2 * c]

time: 132 us -> 129 us (0.977)
  waiting for transfers between devices: 70 us -> 67.3 us
    ppermute x16, waiting for transfers between devices: 52.1 us -> 49.5 us  [shards(): send = lambda x, pairs: lax.ppermute(x, 'tok', pairs)]
  transfers between devices with their start and end apart: 31 -> 31, of which waited for: 17 -> 17; matrix products, arithmetic and copies ran while one was open for 0% -> 0% of each run, Pallas kernels for 7% -> 8%
where the time goes in v3:
time: 129 us
  waiting for transfers between devices  67.3 us (52%)
  starting transfers between devices  40.5 us (31%)
  Pallas kernels  17.3 us (13%)
  local copies, waits for them, and re-layouts  3.8 us (3%)
    ppermute x16, waiting for transfers between devices, shards(): send = lambda x, pairs: lax.ppermute(x, 'tok', pairs)  49.5 us
    ppermute x15, starting transfers between devices, shards(): lax.ppermute(x, 'feat', [(i, i ^ s) for i in range(zs)])  26.5 us
    ppermute x15, waiting for transfers between devices, shards(): lax.ppermute(x, 'feat', [(i, i ^ s) for i in range(zs)])  17.9 us
    ppermute x16, starting transfers between devices, shards(): send = lambda x, pairs: lax.ppermute(x, 'tok', pairs)  14 us
    pallas_call x2, Pallas kernels, terms(): pl.pallas_call(functools.partial(term_kernel, zs, spots, len(acts)), out_...  6.99 us
    pallas_call x3, Pallas kernels, mix(): pl.pallas_call(functools.partial(mix_kernel, count, zs), out_shape=[piece...  6.36 us
    unnamed x4, local copies, waits for them, and re-layouts  3.8 us
  transfers between devices with their start and end apart: 31, of which 17 were waited for; matrix products, arithmetic and copies ran while one was open for 0% of the time, Pallas kernels for 8%

profile of v3, /device:TPU:0, one launch (start us, length us, event | category | flops | bytes accessed | tf_op | source)
XLA Modules:
  0.0 129.2 jit_solution(7604967125512543902)
XLA Ops:
  0.0 1.5 %copy-done.1 = f32[7168,64]{0,1:T(8,128)S(1)} copy-done((f32[7168,64]{0,1:T(8,128)S(1)}, f32[7168,64]{0,1:T(8,128)}, u32[]{:S(2)}) %copy-start.1) | copy-done | bytes 1835032
  1.7 0.5 collective-permute-start.4
  2.2 2.6 %collective-permute-start.5 = (f32[64,3584]{1,0:T(8,128)S(1)}, f32[64,3584]{1,0:T(8,128)S(1)}, u32[]{:S(2)}, u32[]{:S(2)}) collective-permute-start(f32[64,3584]{1,0:T(8,128)S(1)} %get-tuple-element.63.refs_0_), channel_id=1, source_target_pairs={{0,16},{4,12},{8,24},{12,4},{16,0},{20,28},{24,8},{28,20},{1,17},{... | collective-permute-start | bytes 2752520 | tf_op jit(solution)/shard_map/ppermute | solution.py:318
  4.8 2.3 %copy-done = f32[160,7168]{1,0:T(8,128)S(1)} copy-done((f32[160,7168]{1,0:T(8,128)S(1)}, f32[160,7168]{1,0:T(8,128)}, u32[]{:S(2)}) %copy-start) | copy-done | bytes 4587544
  7.1 0.4 cut.2
  7.7 0.4 collective-permute-start.2
  8.1 1.7 %collective-permute-start = (f32[96,3584]{1,0:T(8,128)S(1)}, f32[96,3584]{1,0:T(8,128)S(1)}, u32[]{:S(2)}, u32[]{:S(2)}) collective-permute-start(f32[96,3584]{1,0:T(8,128)S(1)} %get-tuple-element.59.refs_0_), channel_id=1, source_target_pairs={{0,8},{4,20},{8,0},{12,28},{16,24},{20,4},{24,16},{28,12},{1,9},{5... | collective-permute-start | bytes 4128776 | tf_op jit(solution)/shard_map/ppermute | solution.py:318
  9.8 15.6 %collective-permute-done.5.refs_2_ = f32[64,3584]{1,0:T(8,128)S(1)} collective-permute-done((f32[64,3584]{1,0:T(8,128)S(1)}, f32[64,3584]{1,0:T(8,128)S(1)}, u32[]{:S(2)}, u32[]{:S(2)}) %collective-permute-start.5) | collective-permute-done | bytes 917536 | tf_op jit(solution)/shard_map/ppermute | solution.py:318
  25.5 0.5 collective-permute-done.6.refs_3_
  26.0 2.0 %collective-permute-start.10 = (f32[64,3584]{1,0:T(8,128)S(1)}, f32[64,3584]{1,0:T(8,128)S(1)}, u32[]{:S(2)}, u32[]{:S(2)}) collective-permute-start(f32[64,3584]{1,0:T(8,128)S(1)} %get-tuple-element.61.refs_2_), channel_id=1, source_target_pairs={{0,8},{4,20},{8,0},{12,28},{16,24},{20,4},{24,16},{28,12},{1,9},{5... | collective-permute-start | bytes 2752520 | tf_op jit(solution)/shard_map/ppermute | solution.py:318
  28.0 1.3 %collective-permute-start.11 = (f32[64,3584]{1,0:T(8,128)S(1)}, f32[64,3584]{1,0:T(8,128)S(1)}, u32[]{:S(2)}, u32[]{:S(2)}) collective-permute-start(f32[64,3584]{1,0:T(8,128)S(1)} %get-tuple-element.62), channel_id=1, source_target_pairs={{0,20},{4,8},{8,28},{12,0},{16,4},{20,24},{24,12},{28,16},{1,21},{... | collective-permute-start | bytes 2752520 | tf_op jit(solution)/shard_map/ppermute | solution.py:318
  29.3 1.4 %turn.1.refs_4_.refs_2_ = bf16[3584,512]{1,0:T(8,128)(2,1)S(1)} custom-call(f32[64,3584]{1,0:T(8,128)S(1)} %get-tuple-element.63.refs_0_, f32[64,3584]{1,0:T(8,128)S(1)} %collective-permute-done.4.refs_1_, f32[64,3584]{1,0:T(8,128)S(1)} %collective-permute-done.5.refs_2_, f32[64,3584]{1,0:T(8,128)S(1)} %collective-permute-done.6.refs_3_), custom_call_target="tpu_custom_call" | custom-call | tf_op jit(solution)/shard_map/turn/pallas_call | solution.py:97
  30.7 2.9 %mix.3 = (f32[80,256]{1,0:T(8,128)S(1)}, f32[80,256]{1,0:T(8,128)S(1)}, f32[80,256]{1,0:T(8,128)S(1)}, f32[80,256]{1,0:T(8,128)S(1)}, bf16[320,3584]{1,0:T(8,128)(2,1)S(1)}, /*index=5*/bf16[320,3584]{1,0:T(8,128)(2,1)S(1)}) custom-call(f32[96,3584]{1,0:T(8,128)S(1)} %get-tuple-element.59.refs_0_, f32[96,3584]{1,0:T(8,128)S(1)} %collective-permute-done.2.refs_1_, ...), custom_call_target="tpu_custom_call" | custom-call | flops 1761607680 | bytes 12845056 | tf_op jit(solution)/shard_map/mix/pallas_call | solution.py:139
  33.6 1.6 %collective-permute-start.7 = (f32[80,256]{1,0:T(8,128)S(1)}, f32[80,256]{1,0:T(8,128)S(1)}, u32[]{:S(2)}, u32[]{:S(2)}) collective-permute-start(f32[80,256]{1,0:T(8,128)S(1)} %get-tuple-element.66), channel_id=1, source_target_pairs={{0,1},{1,0},{2,3},{3,2},{4,5},{5,4},{6,7},{7,6},{8,9},{9,8},{10,11... | collective-permute-start | bytes 245768 | tf_op jit(solution)/shard_map/ppermute | solution.py:319
  35.3 17.1 %collective-permute-done.refs_0_ = f32[96,3584]{1,0:T(8,128)S(1)} collective-permute-done((f32[96,3584]{1,0:T(8,128)S(1)}, f32[96,3584]{1,0:T(8,128)S(1)}, u32[]{:S(2)}, u32[]{:S(2)}) %collective-permute-start) | collective-permute-done | bytes 1376288 | tf_op jit(solution)/shard_map/ppermute | solution.py:318
  52.4 3.0 %collective-permute-start.8 = (f32[80,256]{1,0:T(8,128)S(1)}, f32[80,256]{1,0:T(8,128)S(1)}, u32[]{:S(2)}, u32[]{:S(2)}) collective-permute-start(f32[80,256]{1,0:T(8,128)S(1)} %get-tuple-element.67), channel_id=1, source_target_pairs={{0,2},{1,3},{2,0},{3,1},{4,6},{5,7},{6,4},{7,5},{8,10},{9,11},{10,... | collective-permute-start | bytes 245768 | tf_op jit(solution)/shard_map/ppermute | solution.py:319
  55.4 2.6 %collective-permute-done.1.refs_1_ = f32[96,3584]{1,0:T(8,128)S(1)} collective-permute-done((f32[96,3584]{1,0:T(8,128)S(1)}, f32[96,3584]{1,0:T(8,128)S(1)}, u32[]{:S(2)}, u32[]{:S(2)}) %collective-permute-start.1) | collective-permute-done | bytes 1376288 | tf_op jit(solution)/shard_map/ppermute | solution.py:318
  58.0 3.7 %collective-permute-start.9 = (f32[80,256]{1,0:T(8,128)S(1)}, f32[80,256]{1,0:T(8,128)S(1)}, u32[]{:S(2)}, u32[]{:S(2)}) collective-permute-start(f32[80,256]{1,0:T(8,128)S(1)} %get-tuple-element.68), channel_id=1, source_target_pairs={{0,3},{1,2},{2,1},{3,0},{4,7},{5,6},{6,5},{7,4},{8,11},{9,10},{10,... | collective-permute-start | bytes 245768 | tf_op jit(solution)/shard_map/ppermute | solution.py:319
  61.7 3.2 %collective-permute-done.9.refs_3_ = f32[80,256]{1,0:T(8,128)S(1)} collective-permute-done((f32[80,256]{1,0:T(8,128)S(1)}, f32[80,256]{1,0:T(8,128)S(1)}, u32[]{:S(2)}, u32[]{:S(2)}) %collective-permute-start.9) | collective-permute-done | bytes 81952 | tf_op jit(solution)/shard_map/ppermute | solution.py:319
  64.9 2.0 %mix.4 = (f32[48,256]{1,0:T(8,128)S(1)}, f32[48,256]{1,0:T(8,128)S(1)}, f32[48,256]{1,0:T(8,128)S(1)}, f32[48,256]{1,0:T(8,128)S(1)}, bf16[192,3584]{1,0:T(8,128)(2,1)S(1)}, /*index=5*/bf16[192,3584]{1,0:T(8,128)(2,1)S(1)}) custom-call(f32[96,3584]{1,0:T(8,128)S(1)} %collective-permute-done.refs_0_, f32[96,3584]{1,0:T(8,128)S(1)} %collective-permute-done.1.refs_1_, ...), custom_call_target="tpu_custom_call" | custom-call | flops 1056964608 | bytes 9175040 | tf_op jit(solution)/shard_map/mix/pallas_call | solution.py:139
  66.9 1.8 %collective-permute-start.12 = (f32[48,256]{1,0:T(8,128)S(1)}, f32[48,256]{1,0:T(8,128)S(1)}, u32[]{:S(2)}, u32[]{:S(2)}) collective-permute-start(f32[48,256]{1,0:T(8,128)S(1)} %get-tuple-element.76), channel_id=1, source_target_pairs={{0,1},{1,0},{2,3},{3,2},{4,5},{5,4},{6,7},{7,6},{8,9},{9,8},{10,11... | collective-permute-start | bytes 147464 | tf_op jit(solution)/shard_map/ppermute | solution.py:319
  68.7 2.6 %collective-permute-start.13 = (f32[48,256]{1,0:T(8,128)S(1)}, f32[48,256]{1,0:T(8,128)S(1)}, u32[]{:S(2)}, u32[]{:S(2)}) collective-permute-start(f32[48,256]{1,0:T(8,128)S(1)} %get-tuple-element.77), channel_id=1, source_target_pairs={{0,2},{1,3},{2,0},{3,1},{4,6},{5,7},{6,4},{7,5},{8,10},{9,11},{10,... | collective-permute-start | bytes 147464 | tf_op jit(solution)/shard_map/ppermute | solution.py:319
  71.3 0.7 collective-permute-done.10.refs_0_
  72.1 2.8 %collective-permute-done.11.refs_1_ = f32[64,3584]{1,0:T(8,128)S(1)} collective-permute-done((f32[64,3584]{1,0:T(8,128)S(1)}, f32[64,3584]{1,0:T(8,128)S(1)}, u32[]{:S(2)}, u32[]{:S(2)}) %collective-permute-start.11) | collective-permute-done | bytes 917536 | tf_op jit(solution)/shard_map/ppermute | solution.py:318
  74.9 2.3 %collective-permute-done.14.refs_7_ = f32[48,256]{1,0:T(8,128)S(1)} collective-permute-done((f32[48,256]{1,0:T(8,128)S(1)}, f32[48,256]{1,0:T(8,128)S(1)}, u32[]{:S(2)}, u32[]{:S(2)}) %collective-permute-start.14) | collective-permute-done | bytes 49184 | tf_op jit(solution)/shard_map/ppermute | solution.py:319
  77.2 1.5 %mix.5 = (f32[32,256]{1,0:T(8,128)S(1)}, f32[32,256]{1,0:T(8,128)S(1)}, f32[32,256]{1,0:T(8,128)S(1)}, f32[32,256]{1,0:T(8,128)S(1)}, bf16[128,3584]{1,0:T(8,128)(2,1)S(1)}, /*index=5*/bf16[128,3584]{1,0:T(8,128)(2,1)S(1)}) custom-call(f32[64,3584]{1,0:T(8,128)S(1)} %collective-permute-done.10.refs_0_, f32[64,3584]{1,0:T(8,128)S(1)} %collective-permute-done.11.refs_1_, ...), custom_call_target="tpu_custom_call" | custom-call | flops 704643072 | bytes 7340032 | tf_op jit(solution)/shard_map/mix/pallas_call | solution.py:139
  78.7 2.1 %collective-permute-start.16 = (f32[32,256]{1,0:T(8,128)S(1)}, f32[32,256]{1,0:T(8,128)S(1)}, u32[]{:S(2)}, u32[]{:S(2)}) collective-permute-start(f32[32,256]{1,0:T(8,128)S(1)} %get-tuple-element.87), channel_id=1, source_target_pairs={{0,2},{1,3},{2,0},{3,1},{4,6},{5,7},{6,4},{7,5},{8,10},{9,11},{10,... | collective-permute-start | bytes 98312 | tf_op jit(solution)/shard_map/ppermute | solution.py:319
  80.9 2.2 %collective-permute-start.17 = (f32[32,256]{1,0:T(8,128)S(1)}, f32[32,256]{1,0:T(8,128)S(1)}, u32[]{:S(2)}, u32[]{:S(2)}) collective-permute-start(f32[32,256]{1,0:T(8,128)S(1)} %get-tuple-element.88), channel_id=1, source_target_pairs={{0,3},{1,2},{2,1},{3,0},{4,7},{5,6},{6,5},{7,4},{8,11},{9,10},{10,... | collective-permute-start | bytes 98312 | tf_op jit(solution)/shard_map/ppermute | solution.py:319
  83.1 0.7 collective-permute-done.16.refs_10_
  83.8 2.7 %collective-permute-done.17.refs_11_ = f32[32,256]{1,0:T(8,128)S(1)} collective-permute-done((f32[32,256]{1,0:T(8,128)S(1)}, f32[32,256]{1,0:T(8,128)S(1)}, u32[]{:S(2)}, u32[]{:S(2)}) %collective-permute-start.17) | collective-permute-done | bytes 32800 | tf_op jit(solution)/shard_map/ppermute | solution.py:319
  86.8 2.7 %collective-permute-start.21 = (f32[80,128]{1,0:T(8,128)S(1)}, f32[80,128]{1,0:T(8,128)S(1)}, u32[]{:S(2)}, u32[]{:S(2)}) collective-permute-start(f32[80,128]{1,0:T(8,128)S(1)} %get-tuple-element.93), channel_id=1, source_target_pairs={{0,28},{4,24},{8,20},{12,16},{16,12},{20,8},{24,4},{28,0},{1,29},{... | collective-permute-start | bytes 122888 | tf_op jit(solution)/shard_map/ppermute | solution.py:318
  89.4 0.8 collective-permute-done.20.refs_1_
  90.2 1.4 %collective-permute-done.21.refs_2_ = f32[80,128]{1,0:T(8,128)S(1)} collective-permute-done((f32[80,128]{1,0:T(8,128)S(1)}, f32[80,128]{1,0:T(8,128)S(1)}, u32[]{:S(2)}, u32[]{:S(2)}) %collective-permute-start.21) | collective-permute-done | bytes 40992 | tf_op jit(solution)/shard_map/ppermute | solution.py:318
  91.7 2.6 %collective-permute-start.23 = (f32[160,128]{1,0:T(8,128)S(1)}, f32[160,128]{1,0:T(8,128)S(1)}, u32[]{:S(2)}, u32[]{:S(2)}) collective-permute-start(f32[160,128]{1,0:T(8,128)S(1)} %merge.3.refs_0_), channel_id=1, source_target_pairs={{0,2},{1,3},{2,0},{3,1},{4,6},{5,7},{6,4},{7,5},{8,10},{9,11},{10,... | collective-permute-start | bytes 245768 | tf_op jit(solution)/shard_map/ppermute | solution.py:319
  94.2 1.8 %collective-permute-start.24 = (f32[160,128]{1,0:T(8,128)S(1)}, f32[160,128]{1,0:T(8,128)S(1)}, u32[]{:S(2)}, u32[]{:S(2)}) collective-permute-start(f32[160,128]{1,0:T(8,128)S(1)} %merge.3.refs_0_), channel_id=1, source_target_pairs={{0,3},{1,2},{2,1},{3,0},{4,7},{5,6},{6,5},{7,4},{8,11},{9,10},{10,... | collective-permute-start | bytes 245768 | tf_op jit(solution)/shard_map/ppermute | solution.py:319
  96.3 0.9 collective-permute-start.19
  97.3 2.5 %collective-permute-done.19.refs_2_ = f32[80,128]{1,0:T(8,128)S(1)} collective-permute-done((f32[80,128]{1,0:T(8,128)S(1)}, f32[80,128]{1,0:T(8,128)S(1)}, u32[]{:S(2)}, u32[]{:S(2)}) %collective-permute-start.19) | collective-permute-done | bytes 40992 | tf_op jit(solution)/shard_map/ppermute | solution.py:318
  99.8 1.5 %collective-permute-done.24.refs_3_ = f32[160,128]{1,0:T(8,128)S(1)} collective-permute-done((f32[160,128]{1,0:T(8,128)S(1)}, f32[160,128]{1,0:T(8,128)S(1)}, u32[]{:S(2)}, u32[]{:S(2)}) %collective-permute-start.24) | collective-permute-done | bytes 81952 | tf_op jit(solution)/shard_map/ppermute | solution.py:319
  101.3 3.5 %term.2 = (f32[64,3584]{1,0:T(8,128)S(1)}, f32[64,3584]{1,0:T(8,128)S(1)}) custom-call(f32[160,128]{1,0:T(8,128)S(1)} %merge.3.refs_0_, f32[160,128]{1,0:T(8,128)S(1)} %collective-permute-done.22.refs_1_, f32[160,128]{1,0:T(8,128)S(1)} %collective-permute-done.23.refs_2_, f32[160,128]{1,0:T(8,128)S(1)} %collective-permute-done.24.refs_3_, ...), custom_call_target="tpu_custom_call" | custom-call | tf_op jit(solution)/shard_map/term/pallas_call | solution.py:254
  104.8 1.3 collective-permute-start.28
  106.1 2.5 %collective-permute-start.25 = (f32[160,128]{1,0:T(8,128)S(1)}, f32[160,128]{1,0:T(8,128)S(1)}, u32[]{:S(2)}, u32[]{:S(2)}) collective-permute-start(f32[160,128]{1,0:T(8,128)S(1)} %merge.2.refs_0_), channel_id=1, source_target_pairs={{0,1},{1,0},{2,3},{3,2},{4,5},{5,4},{6,7},{7,6},{8,9},{9,8},{10,11... | collective-permute-start | bytes 245768 | tf_op jit(solution)/shard_map/ppermute | solution.py:319
  108.6 0.6 collective-permute-start.26
  109.2 1.8 %collective-permute-start.27 = (f32[160,128]{1,0:T(8,128)S(1)}, f32[160,128]{1,0:T(8,128)S(1)}, u32[]{:S(2)}, u32[]{:S(2)}) collective-permute-start(f32[160,128]{1,0:T(8,128)S(1)} %merge.2.refs_0_), channel_id=1, source_target_pairs={{0,3},{1,2},{2,1},{3,0},{4,7},{5,6},{6,5},{7,4},{8,11},{9,10},{10,... | collective-permute-start | bytes 245768 | tf_op jit(solution)/shard_map/ppermute | solution.py:319
  111.0 0.7 collective-permute-done.25.refs_1_
  111.7 6.7 %collective-permute-done.26.refs_2_ = f32[160,128]{1,0:T(8,128)S(1)} collective-permute-done((f32[160,128]{1,0:T(8,128)S(1)}, f32[160,128]{1,0:T(8,128)S(1)}, u32[]{:S(2)}, u32[]{:S(2)}) %collective-permute-start.26) | collective-permute-done | bytes 81952 | tf_op jit(solution)/shard_map/ppermute | solution.py:319
  118.4 3.5 %term.3 = (f32[64,3584]{1,0:T(8,128)S(1)}, f32[64,3584]{1,0:T(8,128)S(1)}) custom-call(f32[160,128]{1,0:T(8,128)S(1)} %merge.2.refs_0_, f32[160,128]{1,0:T(8,128)S(1)} %collective-permute-done.25.refs_1_, f32[160,128]{1,0:T(8,128)S(1)} %collective-permute-done.26.refs_2_, f32[160,128]{1,0:T(8,128)S(1)} %collective-permute-done.27.refs_3_, ...), custom_call_target="tpu_custom_call" | custom-call | tf_op jit(solution)/shard_map/term/pallas_call | solution.py:254
  122.0 5.4 %collective-permute-done.30.refs_1_.refs_3_ = f32[64,3584]{1,0:T(8,128)S(1)} collective-permute-done((f32[64,3584]{1,0:T(8,128)S(1)}, f32[64,3584]{1,0:T(8,128)S(1)}, u32[]{:S(2)}, u32[]{:S(2)}) %collective-permute-start.30) | collective-permute-done | bytes 917536 | tf_op jit(solution)/shard_map/ppermute | solution.py:318
  127.4 1.8 %join.1 = f32[64,7168]{1,0:T(8,128)} custom-call(f32[64,3584]{1,0:T(8,128)S(1)} %get-tuple-element.111.refs_0_, f32[64,3584]{1,0:T(8,128)S(1)} %collective-permute-done.28.refs_0_.refs_1_, f32[64,3584]{1,0:T(8,128)S(1)} %collective-permute-done.29.refs_2_, f32[64,3584]{1,0:T(8,128)S(1)} %collective-permute-done.30.refs_1_.refs_3_, f32[8,128]{1,0:T(8,128)S(1)} %arrived.1.refs_4_), custom_call_target="tpu_custom_call" | custom-call | tf_op jit(solution)/shard_map/join/pallas_call | solution.py:300
  (31 shorter events, 1.2 us)
Async XLA Ops:
  0.0 1.5 %copy-start.1 = (f32[7168,64]{0,1:T(8,128)S(1)}, f32[7168,64]{0,1:T(8,128)}, u32[]{:S(2)}) copy-start(f32[7168,64]{0,1:T(8,128)} %param.3) | copy-start | bytes 5505028
  1.7 6.4 %collective-permute-start.4 = (f32[64,3584]{1,0:T(8,128)S(1)}, f32[64,3584]{1,0:T(8,128)S(1)}, u32[]{:S(2)}, u32[]{:S(2)}) collective-permute-start(f32[64,3584]{1,0:T(8,128)S(1)} %get-tuple-element.64), channel_id=1, source_target_pairs={{0,4},{4,0},{8,12},{12,8},{16,20},{20,16},{24,28},{28,24},{1,5},{5... | collective-permute-start | bytes 2752520 | tf_op jit(solution)/shard_map/ppermute | solution.py:318
  2.2 23.3 %collective-permute-start.5 = (f32[64,3584]{1,0:T(8,128)S(1)}, f32[64,3584]{1,0:T(8,128)S(1)}, u32[]{:S(2)}, u32[]{:S(2)}) collective-permute-start(f32[64,3584]{1,0:T(8,128)S(1)} %get-tuple-element.63.refs_0_), channel_id=1, source_target_pairs={{0,16},{4,12},{8,24},{12,4},{16,0},{20,28},{24,8},{28,20},{1,17},{... | collective-permute-start | bytes 2752520 | tf_op jit(solution)/shard_map/ppermute | solution.py:318
  4.8 21.2 %collective-permute-start.6 = (f32[64,3584]{1,0:T(8,128)S(1)}, f32[64,3584]{1,0:T(8,128)S(1)}, u32[]{:S(2)}, u32[]{:S(2)}) collective-permute-start(f32[64,3584]{1,0:T(8,128)S(1)} %get-tuple-element.64), channel_id=1, source_target_pairs={{0,12},{4,16},{8,4},{12,24},{16,28},{20,0},{24,20},{28,8},{1,13},{... | collective-permute-start | bytes 2752520 | tf_op jit(solution)/shard_map/ppermute | solution.py:318
  4.8 2.3 %copy-start = (f32[160,7168]{1,0:T(8,128)S(1)}, f32[160,7168]{1,0:T(8,128)}, u32[]{:S(2)}) copy-start(f32[160,7168]{1,0:T(8,128)} %source.1) | copy-start | bytes 13762564
  7.5 20.4 %collective-permute-start.3 = (f32[64,3584]{1,0:T(8,128)S(1)}, f32[64,3584]{1,0:T(8,128)S(1)}, u32[]{:S(2)}, u32[]{:S(2)}) collective-permute-start(f32[64,3584]{1,0:T(8,128)S(1)} %get-tuple-element.62), channel_id=1, source_target_pairs={{0,4},{4,0},{8,12},{12,8},{16,20},{20,16},{24,28},{28,24},{1,5},{5... | collective-permute-start | bytes 2752520 | tf_op jit(solution)/shard_map/ppermute | solution.py:318
  7.7 23.0 %collective-permute-start.2 = (f32[96,3584]{1,0:T(8,128)S(1)}, f32[96,3584]{1,0:T(8,128)S(1)}, u32[]{:S(2)}, u32[]{:S(2)}) collective-permute-start(f32[96,3584]{1,0:T(8,128)S(1)} %get-tuple-element.60), channel_id=1, source_target_pairs={{0,4},{4,0},{8,12},{12,8},{16,20},{20,16},{24,28},{28,24},{1,5},{5... | collective-permute-start | bytes 4128776 | tf_op jit(solution)/shard_map/ppermute | solution.py:318
  8.1 44.3 %collective-permute-start = (f32[96,3584]{1,0:T(8,128)S(1)}, f32[96,3584]{1,0:T(8,128)S(1)}, u32[]{:S(2)}, u32[]{:S(2)}) collective-permute-start(f32[96,3584]{1,0:T(8,128)S(1)} %get-tuple-element.59.refs_0_), channel_id=1, source_target_pairs={{0,8},{4,20},{8,0},{12,28},{16,24},{20,4},{24,16},{28,12},{1,9},{5... | collective-permute-start | bytes 4128776 | tf_op jit(solution)/shard_map/ppermute | solution.py:318
  25.5 32.5 %collective-permute-start.1 = (f32[96,3584]{1,0:T(8,128)S(1)}, f32[96,3584]{1,0:T(8,128)S(1)}, u32[]{:S(2)}, u32[]{:S(2)}) collective-permute-start(f32[96,3584]{1,0:T(8,128)S(1)} %get-tuple-element.60), channel_id=1, source_target_pairs={{0,20},{4,8},{8,28},{12,0},{16,4},{20,24},{24,12},{28,16},{1,21},{... | collective-permute-start | bytes 4128776 | tf_op jit(solution)/shard_map/ppermute | solution.py:318
  26.0 46.1 %collective-permute-start.10 = (f32[64,3584]{1,0:T(8,128)S(1)}, f32[64,3584]{1,0:T(8,128)S(1)}, u32[]{:S(2)}, u32[]{:S(2)}) collective-permute-start(f32[64,3584]{1,0:T(8,128)S(1)} %get-tuple-element.61.refs_2_), channel_id=1, source_target_pairs={{0,8},{4,20},{8,0},{12,28},{16,24},{20,4},{24,16},{28,12},{1,9},{5... | collective-permute-start | bytes 2752520 | tf_op jit(solution)/shard_map/ppermute | solution.py:318
  28.0 46.9 %collective-permute-start.11 = (f32[64,3584]{1,0:T(8,128)S(1)}, f32[64,3584]{1,0:T(8,128)S(1)}, u32[]{:S(2)}, u32[]{:S(2)}) collective-permute-start(f32[64,3584]{1,0:T(8,128)S(1)} %get-tuple-element.62), channel_id=1, source_target_pairs={{0,20},{4,8},{8,28},{12,0},{16,4},{20,24},{24,12},{28,16},{1,21},{... | collective-permute-start | bytes 2752520 | tf_op jit(solution)/shard_map/ppermute | solution.py:318
  33.6 28.1 %collective-permute-start.7 = (f32[80,256]{1,0:T(8,128)S(1)}, f32[80,256]{1,0:T(8,128)S(1)}, u32[]{:S(2)}, u32[]{:S(2)}) collective-permute-start(f32[80,256]{1,0:T(8,128)S(1)} %get-tuple-element.66), channel_id=1, source_target_pairs={{0,1},{1,0},{2,3},{3,2},{4,5},{5,4},{6,7},{7,6},{8,9},{9,8},{10,11... | collective-permute-start | bytes 245768 | tf_op jit(solution)/shard_map/ppermute | solution.py:319
  52.4 9.3 %collective-permute-start.8 = (f32[80,256]{1,0:T(8,128)S(1)}, f32[80,256]{1,0:T(8,128)S(1)}, u32[]{:S(2)}, u32[]{:S(2)}) collective-permute-start(f32[80,256]{1,0:T(8,128)S(1)} %get-tuple-element.67), channel_id=1, source_target_pairs={{0,2},{1,3},{2,0},{3,1},{4,6},{5,7},{6,4},{7,5},{8,10},{9,11},{10,... | collective-permute-start | bytes 245768 | tf_op jit(solution)/shard_map/ppermute | solution.py:319
  58.0 6.9 %collective-permute-start.9 = (f32[80,256]{1,0:T(8,128)S(1)}, f32[80,256]{1,0:T(8,128)S(1)}, u32[]{:S(2)}, u32[]{:S(2)}) collective-permute-start(f32[80,256]{1,0:T(8,128)S(1)} %get-tuple-element.68), channel_id=1, source_target_pairs={{0,3},{1,2},{2,1},{3,0},{4,7},{5,6},{6,5},{7,4},{8,11},{9,10},{10,... | collective-permute-start | bytes 245768 | tf_op jit(solution)/shard_map/ppermute | solution.py:319
  66.9 8.0 %collective-permute-start.12 = (f32[48,256]{1,0:T(8,128)S(1)}, f32[48,256]{1,0:T(8,128)S(1)}, u32[]{:S(2)}, u32[]{:S(2)}) collective-permute-start(f32[48,256]{1,0:T(8,128)S(1)} %get-tuple-element.76), channel_id=1, source_target_pairs={{0,1},{1,0},{2,3},{3,2},{4,5},{5,4},{6,7},{7,6},{8,9},{9,8},{10,11... | collective-permute-start | bytes 147464 | tf_op jit(solution)/shard_map/ppermute | solution.py:319
  68.7 6.2 %collective-permute-start.13 = (f32[48,256]{1,0:T(8,128)S(1)}, f32[48,256]{1,0:T(8,128)S(1)}, u32[]{:S(2)}, u32[]{:S(2)}) collective-permute-start(f32[48,256]{1,0:T(8,128)S(1)} %get-tuple-element.77), channel_id=1, source_target_pairs={{0,2},{1,3},{2,0},{3,1},{4,6},{5,7},{6,4},{7,5},{8,10},{9,11},{10,... | collective-permute-start | bytes 147464 | tf_op jit(solution)/shard_map/ppermute | solution.py:319
  71.3 5.9 %collective-permute-start.14 = (f32[48,256]{1,0:T(8,128)S(1)}, f32[48,256]{1,0:T(8,128)S(1)}, u32[]{:S(2)}, u32[]{:S(2)}) collective-permute-start(f32[48,256]{1,0:T(8,128)S(1)} %get-tuple-element.78), channel_id=1, source_target_pairs={{0,3},{1,2},{2,1},{3,0},{4,7},{5,6},{6,5},{7,4},{8,11},{9,10},{10,... | collective-permute-start | bytes 147464 | tf_op jit(solution)/shard_map/ppermute | solution.py:319
  78.7 4.5 %collective-permute-start.15 = (f32[32,256]{1,0:T(8,128)S(1)}, f32[32,256]{1,0:T(8,128)S(1)}, u32[]{:S(2)}, u32[]{:S(2)}) collective-permute-start(f32[32,256]{1,0:T(8,128)S(1)} %get-tuple-element.86), channel_id=1, source_target_pairs={{0,1},{1,0},{2,3},{3,2},{4,5},{5,4},{6,7},{7,6},{8,9},{9,8},{10,11... | collective-permute-start | bytes 98312 | tf_op jit(solution)/shard_map/ppermute | solution.py:319
  78.7 5.1 %collective-permute-start.16 = (f32[32,256]{1,0:T(8,128)S(1)}, f32[32,256]{1,0:T(8,128)S(1)}, u32[]{:S(2)}, u32[]{:S(2)}) collective-permute-start(f32[32,256]{1,0:T(8,128)S(1)} %get-tuple-element.87), channel_id=1, source_target_pairs={{0,2},{1,3},{2,0},{3,1},{4,6},{5,7},{6,4},{7,5},{8,10},{9,11},{10,... | collective-permute-start | bytes 98312 | tf_op jit(solution)/shard_map/ppermute | solution.py:319
  80.9 5.7 %collective-permute-start.17 = (f32[32,256]{1,0:T(8,128)S(1)}, f32[32,256]{1,0:T(8,128)S(1)}, u32[]{:S(2)}, u32[]{:S(2)}) collective-permute-start(f32[32,256]{1,0:T(8,128)S(1)} %get-tuple-element.88), channel_id=1, source_target_pairs={{0,3},{1,2},{2,1},{3,0},{4,7},{5,6},{6,5},{7,4},{8,11},{9,10},{10,... | collective-permute-start | bytes 98312 | tf_op jit(solution)/shard_map/ppermute | solution.py:319
  86.7 3.5 %collective-permute-start.20 = (f32[80,128]{1,0:T(8,128)S(1)}, f32[80,128]{1,0:T(8,128)S(1)}, u32[]{:S(2)}, u32[]{:S(2)}) collective-permute-start(f32[80,128]{1,0:T(8,128)S(1)} %get-tuple-element.92), channel_id=1, source_target_pairs={{0,12},{4,16},{8,4},{12,24},{16,28},{20,0},{24,20},{28,8},{1,13},{... | collective-permute-start | bytes 122888 | tf_op jit(solution)/shard_map/ppermute | solution.py:318
  86.8 4.8 %collective-permute-start.21 = (f32[80,128]{1,0:T(8,128)S(1)}, f32[80,128]{1,0:T(8,128)S(1)}, u32[]{:S(2)}, u32[]{:S(2)}) collective-permute-start(f32[80,128]{1,0:T(8,128)S(1)} %get-tuple-element.93), channel_id=1, source_target_pairs={{0,28},{4,24},{8,20},{12,16},{16,12},{20,8},{24,4},{28,0},{1,29},{... | collective-permute-start | bytes 122888 | tf_op jit(solution)/shard_map/ppermute | solution.py:318
  91.6 8.2 %collective-permute-start.22 = (f32[160,128]{1,0:T(8,128)S(1)}, f32[160,128]{1,0:T(8,128)S(1)}, u32[]{:S(2)}, u32[]{:S(2)}) collective-permute-start(f32[160,128]{1,0:T(8,128)S(1)} %merge.3.refs_0_), channel_id=1, source_target_pairs={{0,1},{1,0},{2,3},{3,2},{4,5},{5,4},{6,7},{7,6},{8,9},{9,8},{10,11... | collective-permute-start | bytes 245768 | tf_op jit(solution)/shard_map/ppermute | solution.py:319
  91.7 8.1 %collective-permute-start.23 = (f32[160,128]{1,0:T(8,128)S(1)}, f32[160,128]{1,0:T(8,128)S(1)}, u32[]{:S(2)}, u32[]{:S(2)}) collective-permute-start(f32[160,128]{1,0:T(8,128)S(1)} %merge.3.refs_0_), channel_id=1, source_target_pairs={{0,2},{1,3},{2,0},{3,1},{4,6},{5,7},{6,4},{7,5},{8,10},{9,11},{10,... | collective-permute-start | bytes 245768 | tf_op jit(solution)/shard_map/ppermute | solution.py:319
  94.2 7.1 %collective-permute-start.24 = (f32[160,128]{1,0:T(8,128)S(1)}, f32[160,128]{1,0:T(8,128)S(1)}, u32[]{:S(2)}, u32[]{:S(2)}) collective-permute-start(f32[160,128]{1,0:T(8,128)S(1)} %merge.3.refs_0_), channel_id=1, source_target_pairs={{0,3},{1,2},{2,1},{3,0},{4,7},{5,6},{6,5},{7,4},{8,11},{9,10},{10,... | collective-permute-start | bytes 245768 | tf_op jit(solution)/shard_map/ppermute | solution.py:319
  96.1 1.2 collective-permute-start.18
  96.3 3.4 %collective-permute-start.19 = (f32[80,128]{1,0:T(8,128)S(1)}, f32[80,128]{1,0:T(8,128)S(1)}, u32[]{:S(2)}, u32[]{:S(2)}) collective-permute-start(f32[80,128]{1,0:T(8,128)S(1)} %get-tuple-element.91), channel_id=1, source_target_pairs={{0,20},{4,8},{8,28},{12,0},{16,4},{20,24},{24,12},{28,16},{1,21},{... | collective-permute-start | bytes 122888 | tf_op jit(solution)/shard_map/ppermute | solution.py:318
  104.8 17.1 %collective-permute-start.28 = (f32[64,3584]{1,0:T(8,128)S(1)}, f32[64,3584]{1,0:T(8,128)S(1)}, u32[]{:S(2)}, u32[]{:S(2)}) collective-permute-start(f32[64,3584]{1,0:T(8,128)S(1)} %get-tuple-element.105), channel_id=1, source_target_pairs={{0,16},{4,12},{8,24},{12,4},{16,0},{20,28},{24,8},{28,20},{1,17},{... | collective-permute-start | bytes 2752520 | tf_op jit(solution)/shard_map/ppermute | solution.py:318
  106.1 21.2 %collective-permute-start.30 = (f32[64,3584]{1,0:T(8,128)S(1)}, f32[64,3584]{1,0:T(8,128)S(1)}, u32[]{:S(2)}, u32[]{:S(2)}) collective-permute-start(f32[64,3584]{1,0:T(8,128)S(1)} %get-tuple-element.106), channel_id=1, source_target_pairs={{0,20},{4,8},{8,28},{12,0},{16,4},{20,24},{24,12},{28,16},{1,21},{... | collective-permute-start | bytes 2752520 | tf_op jit(solution)/shard_map/ppermute | solution.py:318
  106.1 5.5 %collective-permute-start.25 = (f32[160,128]{1,0:T(8,128)S(1)}, f32[160,128]{1,0:T(8,128)S(1)}, u32[]{:S(2)}, u32[]{:S(2)}) collective-permute-start(f32[160,128]{1,0:T(8,128)S(1)} %merge.2.refs_0_), channel_id=1, source_target_pairs={{0,1},{1,0},{2,3},{3,2},{4,5},{5,4},{6,7},{7,6},{8,9},{9,8},{10,11... | collective-permute-start | bytes 245768 | tf_op jit(solution)/shard_map/ppermute | solution.py:319
  108.6 9.7 %collective-permute-start.26 = (f32[160,128]{1,0:T(8,128)S(1)}, f32[160,128]{1,0:T(8,128)S(1)}, u32[]{:S(2)}, u32[]{:S(2)}) collective-permute-start(f32[160,128]{1,0:T(8,128)S(1)} %merge.2.refs_0_), channel_id=1, source_target_pairs={{0,2},{1,3},{2,0},{3,1},{4,6},{5,7},{6,4},{7,5},{8,10},{9,11},{10,... | collective-permute-start | bytes 245768 | tf_op jit(solution)/shard_map/ppermute | solution.py:319
  109.2 9.1 %collective-permute-start.27 = (f32[160,128]{1,0:T(8,128)S(1)}, f32[160,128]{1,0:T(8,128)S(1)}, u32[]{:S(2)}, u32[]{:S(2)}) collective-permute-start(f32[160,128]{1,0:T(8,128)S(1)} %merge.2.refs_0_), channel_id=1, source_target_pairs={{0,3},{1,2},{2,1},{3,0},{4,7},{5,6},{6,5},{7,4},{8,11},{9,10},{10,... | collective-permute-start | bytes 245768 | tf_op jit(solution)/shard_map/ppermute | solution.py:319
  121.9 5.5 %collective-permute-start.29 = (f32[64,3584]{1,0:T(8,128)S(1)}, f32[64,3584]{1,0:T(8,128)S(1)}, u32[]{:S(2)}, u32[]{:S(2)}) collective-permute-start(f32[64,3584]{1,0:T(8,128)S(1)} %get-tuple-element.112), channel_id=1, source_target_pairs={{0,4},{4,0},{8,12},{12,8},{16,20},{20,16},{24,28},{28,24},{1,5},{5... | collective-permute-start | bytes 2752520 | tf_op jit(solution)/shard_map/ppermute | solution.py:318

commit v4 on v3

--- a/solution.py
+++ b/solution.py
@@ -219,13 +219,13 @@
     )(*inputs)
 
 
-def term_kernel(zs, spots, groups, *refs):
+def term_kernel(zs, spots, groups, begin, *refs):
     got = [refs[c * zs : (c + 1) * zs] for c in range(len(spots))]
     refs = refs[len(spots) * zs :]
     acts = refs[: 2 * groups]
     outs, full = refs[2 * groups : -1], refs[-1]
     columns = full.shape[1]
-    width, half = outs[0].shape
+    width, size = outs[0].shape
     z = lax.axis_index("feat")
     for pieces, segments in zip(got, spots):
         for s in range(zs):
@@ -233,49 +233,37 @@
                 full[pl.ds(to + (z ^ s) * part, part)] = pieces[s][at : at + part]
     h, l = split(full[...].T)
     both = jnp.concatenate([h, l], 0)
-    step = block_of(half, 512)
-
-    @pl.loop(0, half // step)
+    step = block_of(size, 896)
+
+    @pl.loop(0, size // step)
     def _(i):
-        at = pl.ds(pl.multiple_of(i * step, step), step)
+        to = pl.ds(pl.multiple_of(i * step, step), step)
+        at = pl.ds(pl.multiple_of(begin + i * step, 128), step)
         high = jnp.concatenate([x[:, at] for x in acts[::2]], 0)
         low = jnp.concatenate([x[:, at] for x in acts[1::2]], 0)
         d = dot(both, high)
         total = d[:columns] + (d[columns:] + dot(h, low))
         for o, out in enumerate(outs):
-            out[:, at] = total[o * width : (o + 1) * width]
-
-
-def terms(got, acts, spots, width, cost=1):
+            out[:, to] = total[o * width : (o + 1) * width]
+
+
+def terms(got, acts, spots, width, low=0, high=None):
     zs, columns = len(got[0]), got[0][0].shape[1]
     half = acts[0][0].shape[1]
     count = columns // width
     rows = sum(act[0].shape[0] for act in acts)
     return pl.pallas_call(
-        functools.partial(term_kernel, zs, spots, len(acts)),
-        out_shape=[jax.ShapeDtypeStruct((width, half), jnp.float32)] * count,
+        functools.partial(term_kernel, zs, spots, len(acts), low),
+        out_shape=[jax.ShapeDtypeStruct((width, (high or half) - low), jnp.float32)] * count,
         in_specs=[VMEM] * (zs * len(got) + 2 * len(acts)),
         out_specs=[VMEM] * count,
         scratch_shapes=[pltpu.VMEM((rows, columns), jnp.float32)],
         compiler_params=PARAMS,
         cost_estimate=pl.CostEstimate(
-            flops=cost * 6 * rows * columns * half,
-            bytes_accessed=cost * (4 * rows * half + 4 * columns * half),
-            transcendentals=0,
+            flops=0, bytes_accessed=0, transcendentals=0
         ),
         name="term",
     )(*[x for pieces in got for x in pieces], *[x for act in acts for x in act])
-
-
-def join_kernel(count, *refs):
-    out = refs[-1]
-    core = lax.axis_index("tok") & 1
-    half = out.shape[1] // 2
-    for side, at in ((refs[:count], core), (refs[count : 2 * count], 1 - core)):
-        total = side[0][...]
-        for x in side[1:]:
-            total = total + x[...]
-        out[:, pl.ds(pl.multiple_of(at * half, half), half)] = total
 
 
 def arrived_kernel(*refs):
@@ -294,19 +282,53 @@
     )(*blocks)
 
 
-def join(own, other, mark):
+def join_kernel(sides, low, *refs):
+    staged, sems, out = refs[-2], refs[-1], refs[-3]
+    core = lax.axis_index("tok") & 1
+    half = out.shape[1] // 2
+    width, size = staged.shape[1:]
+    rows = 16 if width % 16 == 0 else width
+    copies = []
+    for i in range(0, width, rows):
+        first = 0
+        for k, count in enumerate(sides):
+            whole, *arrivals = refs[first : first + count]
+            first += count
+            x = whole[i : i + rows, low : low + size]
+            for ref in arrivals:
+                x = x + ref[i : i + rows]
+            staged[k, i : i + rows] = x
+            at = pl.multiple_of((core ^ k) * half + low, 128)
+            copy = pltpu.make_async_copy(
+                staged.at[k, pl.ds(i, rows)],
+                out.at[pl.ds(i, rows), pl.ds(at, size)],
+                sems.at[len(copies)],
+            )
+            copy.start()
+            copies.append(copy)
+    for copy in copies:
+        copy.wait()
+
+
+def join(own, other, low, mark, before=()):
     width, half = own[0].shape
+    size = own[1].shape[1]
+    inputs = [*own, *other]
     rows = 16 if width % 16 == 0 else width
+    hbm = pl.BlockSpec(memory_space=pl.ANY)
     return pl.pallas_call(
-        functools.partial(join_kernel, len(own)),
-        grid=(width // rows,),
+        functools.partial(join_kernel, (len(own), len(other)), low),
         out_shape=jax.ShapeDtypeStruct((width, 2 * half), jnp.float32),
-        in_specs=[pl.BlockSpec((rows, half), lambda i: (i, 0))] * (2 * len(own))
-        + [pl.BlockSpec(memory_space=pl.ANY)],
-        out_specs=pl.BlockSpec((rows, 2 * half), lambda i: (i, 0)),
+        in_specs=[VMEM] * len(inputs) + [hbm] * (len(mark) + len(before)),
+        out_specs=hbm,
+        input_output_aliases={len(inputs) + len(mark): 0} if before else {},
+        scratch_shapes=[
+            pltpu.VMEM((2, width, size), jnp.float32),
+            pltpu.SemaphoreType.DMA((2 * width // rows,)),
+        ],
         compiler_params=PARAMS,
         name="join",
-    )(*own, *other, mark)
+    )(*inputs, *mark, *before)
 
 
 def shards(side, calib, weight):
@@ -379,14 +401,24 @@
     away = spread(merge(side, factor, turns[1:], [chunk]))
     here = merge(side, factor, turns[:1], [chunk])
     here, away = hold((here, away))
-    term = terms([away], acts, [spots], width, 0)
-    same = [send(term[2 * q - 2], along(q, 0, "results")) for q in turns[1:]]
-    cross = [send(term[2 * q - 1], along(q, 1, "results")) for q in turns[1:]]
+    half = acts[0][0].shape[1]
+    cuts = [(0, half)]
+    same, cross = [], []
+    for low, high in cuts:
+        term = terms([away], acts, [spots], width, low, high)
+        same.append([send(term[2 * q - 2], along(q, 0, "results")) for q in turns[1:]])
+        cross.append([send(term[2 * q - 1], along(q, 1, "results")) for q in turns[1:]])
+        (here, away), term = hold(((here, away), term))
     here = spread(here)
     here, term = hold((here, term))
-    mine, near = terms([here], acts, [spots], width, 0)
+    mine, near = terms([here], acts, [spots], width)
     near = send(near, along(0, 1, "results"))
-    return join([mine] + same, [near] + cross, arrived(same + cross))
+    out = ()
+    for (low, high), s, c in zip(cuts, same, cross):
+        last = high == half
+        mark = [arrived([x for part in (same + cross) for x in part])] if last else []
+        out = (join([mine] + s, [near] + c, low, mark, out),)
+    return out[0]
 
 
 def solution(mesh):

time: 129 us -> 129 us (level)
  no operation moved by 1% of the time
where the time goes in v4:
time: 129 us; the launch traced here: 128 us
  waiting for transfers between devices  67.6 us (52%)
  starting transfers between devices  40.5 us (31%)
  Pallas kernels  16.3 us (13%)
  local copies, waits for them, and re-layouts  3.8 us (3%)
    ppermute x16, waiting for transfers between devices, shards(): send = lambda x, pairs: lax.ppermute(x, 'tok', pairs)  49.8 us
    ppermute x15, starting transfers between devices, shards(): lax.ppermute(x, 'feat', [(i, i ^ s) for i in range(zs)])  26.6 us
    ppermute x15, waiting for transfers between devices, shards(): lax.ppermute(x, 'feat', [(i, i ^ s) for i in range(zs)])  17.9 us
    ppermute x16, starting transfers between devices, shards(): send = lambda x, pairs: lax.ppermute(x, 'tok', pairs)  14 us
    pallas_call x2, Pallas kernels, terms(): pl.pallas_call(functools.partial(term_kernel, zs, spots, len(acts), low),...  6.42 us
    pallas_call x3, Pallas kernels, mix(): pl.pallas_call(functools.partial(mix_kernel, count, zs), out_shape=[piece...  6.36 us
    unnamed x4, local copies, waits for them, and re-layouts  3.8 us
  transfers between devices with their start and end apart: 31, of which 17 were waited for; matrix products, arithmetic and copies ran while one was open for 0% of the time, Pallas kernels for 8%

profile of v4, /device:TPU:0, one launch (start us, length us, event | category | flops | bytes accessed | tf_op | source)
XLA Modules:
  0.0 128.4 jit_solution(9679229493262113424)
XLA Ops:
  0.0 1.5 %copy-done.1 = f32[7168,64]{0,1:T(8,128)S(1)} copy-done((f32[7168,64]{0,1:T(8,128)S(1)}, f32[7168,64]{0,1:T(8,128)}, u32[]{:S(2)}) %copy-start.1) | copy-done | bytes 1835032
  1.7 0.5 collective-permute-start.4
  2.2 2.6 %collective-permute-start.5 = (f32[64,3584]{1,0:T(8,128)S(1)}, f32[64,3584]{1,0:T(8,128)S(1)}, u32[]{:S(2)}, u32[]{:S(2)}) collective-permute-start(f32[64,3584]{1,0:T(8,128)S(1)} %get-tuple-element.64.refs_0_), channel_id=1, source_target_pairs={{0,16},{4,12},{8,24},{12,4},{16,0},{20,28},{24,8},{28,20},{1,17},{... | collective-permute-start | bytes 2752520 | tf_op jit(solution)/shard_map/ppermute | solution.py:340
  4.8 2.3 %copy-done = f32[160,7168]{1,0:T(8,128)S(1)} copy-done((f32[160,7168]{1,0:T(8,128)S(1)}, f32[160,7168]{1,0:T(8,128)}, u32[]{:S(2)}) %copy-start) | copy-done | bytes 4587544
  7.1 0.4 cut.2
  7.7 0.4 collective-permute-start.2
  8.1 1.7 %collective-permute-start = (f32[96,3584]{1,0:T(8,128)S(1)}, f32[96,3584]{1,0:T(8,128)S(1)}, u32[]{:S(2)}, u32[]{:S(2)}) collective-permute-start(f32[96,3584]{1,0:T(8,128)S(1)} %get-tuple-element.60.refs_0_), channel_id=1, source_target_pairs={{0,8},{4,20},{8,0},{12,28},{16,24},{20,4},{24,16},{28,12},{1,9},{5... | collective-permute-start | bytes 4128776 | tf_op jit(solution)/shard_map/ppermute | solution.py:340
  9.8 15.6 %collective-permute-done.5.refs_2_ = f32[64,3584]{1,0:T(8,128)S(1)} collective-permute-done((f32[64,3584]{1,0:T(8,128)S(1)}, f32[64,3584]{1,0:T(8,128)S(1)}, u32[]{:S(2)}, u32[]{:S(2)}) %collective-permute-start.5) | collective-permute-done | bytes 917536 | tf_op jit(solution)/shard_map/ppermute | solution.py:340
  25.5 0.5 collective-permute-done.6.refs_3_
  26.0 2.0 %collective-permute-start.10 = (f32[64,3584]{1,0:T(8,128)S(1)}, f32[64,3584]{1,0:T(8,128)S(1)}, u32[]{:S(2)}, u32[]{:S(2)}) collective-permute-start(f32[64,3584]{1,0:T(8,128)S(1)} %get-tuple-element.62.refs_2_), channel_id=1, source_target_pairs={{0,8},{4,20},{8,0},{12,28},{16,24},{20,4},{24,16},{28,12},{1,9},{5... | collective-permute-start | bytes 2752520 | tf_op jit(solution)/shard_map/ppermute | solution.py:340
  28.0 1.3 %collective-permute-start.11 = (f32[64,3584]{1,0:T(8,128)S(1)}, f32[64,3584]{1,0:T(8,128)S(1)}, u32[]{:S(2)}, u32[]{:S(2)}) collective-permute-start(f32[64,3584]{1,0:T(8,128)S(1)} %get-tuple-element.63), channel_id=1, source_target_pairs={{0,20},{4,8},{8,28},{12,0},{16,4},{20,24},{24,12},{28,16},{1,21},{... | collective-permute-start | bytes 2752520 | tf_op jit(solution)/shard_map/ppermute | solution.py:340
  29.3 1.4 %turn.1.refs_4_.refs_2_ = bf16[3584,512]{1,0:T(8,128)(2,1)S(1)} custom-call(f32[64,3584]{1,0:T(8,128)S(1)} %get-tuple-element.64.refs_0_, f32[64,3584]{1,0:T(8,128)S(1)} %collective-permute-done.4.refs_1_, f32[64,3584]{1,0:T(8,128)S(1)} %collective-permute-done.5.refs_2_, f32[64,3584]{1,0:T(8,128)S(1)} %collective-permute-done.6.refs_3_), custom_call_target="tpu_custom_call" | custom-call | tf_op jit(solution)/shard_map/turn/pallas_call | solution.py:97
  30.7 2.9 %mix.3 = (f32[80,256]{1,0:T(8,128)S(1)}, f32[80,256]{1,0:T(8,128)S(1)}, f32[80,256]{1,0:T(8,128)S(1)}, f32[80,256]{1,0:T(8,128)S(1)}, bf16[320,3584]{1,0:T(8,128)(2,1)S(1)}, /*index=5*/bf16[320,3584]{1,0:T(8,128)(2,1)S(1)}) custom-call(f32[96,3584]{1,0:T(8,128)S(1)} %get-tuple-element.60.refs_0_, f32[96,3584]{1,0:T(8,128)S(1)} %collective-permute-done.2.refs_1_, ...), custom_call_target="tpu_custom_call" | custom-call | flops 1761607680 | bytes 12845056 | tf_op jit(solution)/shard_map/mix/pallas_call | solution.py:139
  33.6 1.6 %collective-permute-start.7 = (f32[80,256]{1,0:T(8,128)S(1)}, f32[80,256]{1,0:T(8,128)S(1)}, u32[]{:S(2)}, u32[]{:S(2)}) collective-permute-start(f32[80,256]{1,0:T(8,128)S(1)} %get-tuple-element.67), channel_id=1, source_target_pairs={{0,1},{1,0},{2,3},{3,2},{4,5},{5,4},{6,7},{7,6},{8,9},{9,8},{10,11... | collective-permute-start | bytes 245768 | tf_op jit(solution)/shard_map/ppermute | solution.py:341
  35.3 17.1 %collective-permute-done.refs_0_ = f32[96,3584]{1,0:T(8,128)S(1)} collective-permute-done((f32[96,3584]{1,0:T(8,128)S(1)}, f32[96,3584]{1,0:T(8,128)S(1)}, u32[]{:S(2)}, u32[]{:S(2)}) %collective-permute-start) | collective-permute-done | bytes 1376288 | tf_op jit(solution)/shard_map/ppermute | solution.py:340
  52.4 3.0 %collective-permute-start.8 = (f32[80,256]{1,0:T(8,128)S(1)}, f32[80,256]{1,0:T(8,128)S(1)}, u32[]{:S(2)}, u32[]{:S(2)}) collective-permute-start(f32[80,256]{1,0:T(8,128)S(1)} %get-tuple-element.68), channel_id=1, source_target_pairs={{0,2},{1,3},{2,0},{3,1},{4,6},{5,7},{6,4},{7,5},{8,10},{9,11},{10,... | collective-permute-start | bytes 245768 | tf_op jit(solution)/shard_map/ppermute | solution.py:341
  55.4 2.6 %collective-permute-done.1.refs_1_ = f32[96,3584]{1,0:T(8,128)S(1)} collective-permute-done((f32[96,3584]{1,0:T(8,128)S(1)}, f32[96,3584]{1,0:T(8,128)S(1)}, u32[]{:S(2)}, u32[]{:S(2)}) %collective-permute-start.1) | collective-permute-done | bytes 1376288 | tf_op jit(solution)/shard_map/ppermute | solution.py:340
  58.0 3.7 %collective-permute-start.9 = (f32[80,256]{1,0:T(8,128)S(1)}, f32[80,256]{1,0:T(8,128)S(1)}, u32[]{:S(2)}, u32[]{:S(2)}) collective-permute-start(f32[80,256]{1,0:T(8,128)S(1)} %get-tuple-element.69), channel_id=1, source_target_pairs={{0,3},{1,2},{2,1},{3,0},{4,7},{5,6},{6,5},{7,4},{8,11},{9,10},{10,... | collective-permute-start | bytes 245768 | tf_op jit(solution)/shard_map/ppermute | solution.py:341
  61.7 3.2 %collective-permute-done.9.refs_3_ = f32[80,256]{1,0:T(8,128)S(1)} collective-permute-done((f32[80,256]{1,0:T(8,128)S(1)}, f32[80,256]{1,0:T(8,128)S(1)}, u32[]{:S(2)}, u32[]{:S(2)}) %collective-permute-start.9) | collective-permute-done | bytes 81952 | tf_op jit(solution)/shard_map/ppermute | solution.py:341
  64.9 2.0 %mix.4 = (f32[48,256]{1,0:T(8,128)S(1)}, f32[48,256]{1,0:T(8,128)S(1)}, f32[48,256]{1,0:T(8,128)S(1)}, f32[48,256]{1,0:T(8,128)S(1)}, bf16[192,3584]{1,0:T(8,128)(2,1)S(1)}, /*index=5*/bf16[192,3584]{1,0:T(8,128)(2,1)S(1)}) custom-call(f32[96,3584]{1,0:T(8,128)S(1)} %collective-permute-done.refs_0_, f32[96,3584]{1,0:T(8,128)S(1)} %collective-permute-done.1.refs_1_, ...), custom_call_target="tpu_custom_call" | custom-call | flops 1056964608 | bytes 9175040 | tf_op jit(solution)/shard_map/mix/pallas_call | solution.py:139
  66.9 1.8 %collective-permute-start.12 = (f32[48,256]{1,0:T(8,128)S(1)}, f32[48,256]{1,0:T(8,128)S(1)}, u32[]{:S(2)}, u32[]{:S(2)}) collective-permute-start(f32[48,256]{1,0:T(8,128)S(1)} %get-tuple-element.77), channel_id=1, source_target_pairs={{0,1},{1,0},{2,3},{3,2},{4,5},{5,4},{6,7},{7,6},{8,9},{9,8},{10,11... | collective-permute-start | bytes 147464 | tf_op jit(solution)/shard_map/ppermute | solution.py:341
  68.7 2.6 %collective-permute-start.13 = (f32[48,256]{1,0:T(8,128)S(1)}, f32[48,256]{1,0:T(8,128)S(1)}, u32[]{:S(2)}, u32[]{:S(2)}) collective-permute-start(f32[48,256]{1,0:T(8,128)S(1)} %get-tuple-element.78), channel_id=1, source_target_pairs={{0,2},{1,3},{2,0},{3,1},{4,6},{5,7},{6,4},{7,5},{8,10},{9,11},{10,... | collective-permute-start | bytes 147464 | tf_op jit(solution)/shard_map/ppermute | solution.py:341
  71.3 0.7 collective-permute-done.10.refs_0_
  72.1 2.8 %collective-permute-done.11.refs_1_ = f32[64,3584]{1,0:T(8,128)S(1)} collective-permute-done((f32[64,3584]{1,0:T(8,128)S(1)}, f32[64,3584]{1,0:T(8,128)S(1)}, u32[]{:S(2)}, u32[]{:S(2)}) %collective-permute-start.11) | collective-permute-done | bytes 917536 | tf_op jit(solution)/shard_map/ppermute | solution.py:340
  74.9 2.3 %collective-permute-done.14.refs_7_ = f32[48,256]{1,0:T(8,128)S(1)} collective-permute-done((f32[48,256]{1,0:T(8,128)S(1)}, f32[48,256]{1,0:T(8,128)S(1)}, u32[]{:S(2)}, u32[]{:S(2)}) %collective-permute-start.14) | collective-permute-done | bytes 49184 | tf_op jit(solution)/shard_map/ppermute | solution.py:341
  77.2 1.5 %mix.5 = (f32[32,256]{1,0:T(8,128)S(1)}, f32[32,256]{1,0:T(8,128)S(1)}, f32[32,256]{1,0:T(8,128)S(1)}, f32[32,256]{1,0:T(8,128)S(1)}, bf16[128,3584]{1,0:T(8,128)(2,1)S(1)}, /*index=5*/bf16[128,3584]{1,0:T(8,128)(2,1)S(1)}) custom-call(f32[64,3584]{1,0:T(8,128)S(1)} %collective-permute-done.10.refs_0_, f32[64,3584]{1,0:T(8,128)S(1)} %collective-permute-done.11.refs_1_, ...), custom_call_target="tpu_custom_call" | custom-call | flops 704643072 | bytes 7340032 | tf_op jit(solution)/shard_map/mix/pallas_call | solution.py:139
  78.7 2.1 %collective-permute-start.16 = (f32[32,256]{1,0:T(8,128)S(1)}, f32[32,256]{1,0:T(8,128)S(1)}, u32[]{:S(2)}, u32[]{:S(2)}) collective-permute-start(f32[32,256]{1,0:T(8,128)S(1)} %get-tuple-element.88), channel_id=1, source_target_pairs={{0,2},{1,3},{2,0},{3,1},{4,6},{5,7},{6,4},{7,5},{8,10},{9,11},{10,... | collective-permute-start | bytes 98312 | tf_op jit(solution)/shard_map/ppermute | solution.py:341
  80.9 2.2 %collective-permute-start.17 = (f32[32,256]{1,0:T(8,128)S(1)}, f32[32,256]{1,0:T(8,128)S(1)}, u32[]{:S(2)}, u32[]{:S(2)}) collective-permute-start(f32[32,256]{1,0:T(8,128)S(1)} %get-tuple-element.89), channel_id=1, source_target_pairs={{0,3},{1,2},{2,1},{3,0},{4,7},{5,6},{6,5},{7,4},{8,11},{9,10},{10,... | collective-permute-start | bytes 98312 | tf_op jit(solution)/shard_map/ppermute | solution.py:341
  83.1 0.7 collective-permute-done.16.refs_10_
  83.8 2.7 %collective-permute-done.17.refs_11_ = f32[32,256]{1,0:T(8,128)S(1)} collective-permute-done((f32[32,256]{1,0:T(8,128)S(1)}, f32[32,256]{1,0:T(8,128)S(1)}, u32[]{:S(2)}, u32[]{:S(2)}) %collective-permute-start.17) | collective-permute-done | bytes 32800 | tf_op jit(solution)/shard_map/ppermute | solution.py:341
  86.8 2.7 %collective-permute-start.21 = (f32[80,128]{1,0:T(8,128)S(1)}, f32[80,128]{1,0:T(8,128)S(1)}, u32[]{:S(2)}, u32[]{:S(2)}) collective-permute-start(f32[80,128]{1,0:T(8,128)S(1)} %get-tuple-element.94), channel_id=1, source_target_pairs={{0,28},{4,24},{8,20},{12,16},{16,12},{20,8},{24,4},{28,0},{1,29},{... | collective-permute-start | bytes 122888 | tf_op jit(solution)/shard_map/ppermute | solution.py:340
  89.4 0.8 collective-permute-done.20.refs_1_
  90.2 1.4 %collective-permute-done.21.refs_2_ = f32[80,128]{1,0:T(8,128)S(1)} collective-permute-done((f32[80,128]{1,0:T(8,128)S(1)}, f32[80,128]{1,0:T(8,128)S(1)}, u32[]{:S(2)}, u32[]{:S(2)}) %collective-permute-start.21) | collective-permute-done | bytes 40992 | tf_op jit(solution)/shard_map/ppermute | solution.py:340
  91.7 2.6 %collective-permute-start.23 = (f32[160,128]{1,0:T(8,128)S(1)}, f32[160,128]{1,0:T(8,128)S(1)}, u32[]{:S(2)}, u32[]{:S(2)}) collective-permute-start(f32[160,128]{1,0:T(8,128)S(1)} %merge.3.refs_0_), channel_id=1, source_target_pairs={{0,2},{1,3},{2,0},{3,1},{4,6},{5,7},{6,4},{7,5},{8,10},{9,11},{10,... | collective-permute-start | bytes 245768 | tf_op jit(solution)/shard_map/ppermute | solution.py:341
  94.2 1.8 %collective-permute-start.24 = (f32[160,128]{1,0:T(8,128)S(1)}, f32[160,128]{1,0:T(8,128)S(1)}, u32[]{:S(2)}, u32[]{:S(2)}) collective-permute-start(f32[160,128]{1,0:T(8,128)S(1)} %merge.3.refs_0_), channel_id=1, source_target_pairs={{0,3},{1,2},{2,1},{3,0},{4,7},{5,6},{6,5},{7,4},{8,11},{9,10},{10,... | collective-permute-start | bytes 245768 | tf_op jit(solution)/shard_map/ppermute | solution.py:341
  96.3 0.9 collective-permute-start.19
  97.3 2.5 %collective-permute-done.19.refs_2_ = f32[80,128]{1,0:T(8,128)S(1)} collective-permute-done((f32[80,128]{1,0:T(8,128)S(1)}, f32[80,128]{1,0:T(8,128)S(1)}, u32[]{:S(2)}, u32[]{:S(2)}) %collective-permute-start.19) | collective-permute-done | bytes 40992 | tf_op jit(solution)/shard_map/ppermute | solution.py:340
  99.8 1.5 %collective-permute-done.24.refs_3_ = f32[160,128]{1,0:T(8,128)S(1)} collective-permute-done((f32[160,128]{1,0:T(8,128)S(1)}, f32[160,128]{1,0:T(8,128)S(1)}, u32[]{:S(2)}, u32[]{:S(2)}) %collective-permute-start.24) | collective-permute-done | bytes 81952 | tf_op jit(solution)/shard_map/ppermute | solution.py:341
  101.3 3.2 %term.2 = (f32[64,3584]{1,0:T(8,128)S(1)}, f32[64,3584]{1,0:T(8,128)S(1)}) custom-call(f32[160,128]{1,0:T(8,128)S(1)} %merge.3.refs_0_, f32[160,128]{1,0:T(8,128)S(1)} %collective-permute-done.22.refs_1_, f32[160,128]{1,0:T(8,128)S(1)} %collective-permute-done.23.refs_2_, f32[160,128]{1,0:T(8,128)S(1)} %collective-permute-done.24.refs_3_, ...), custom_call_target="tpu_custom_call" | custom-call | tf_op jit(solution)/shard_map/term/pallas_call | solution.py:255
  104.5 1.3 collective-permute-start.28
  105.8 2.5 %collective-permute-start.25 = (f32[160,128]{1,0:T(8,128)S(1)}, f32[160,128]{1,0:T(8,128)S(1)}, u32[]{:S(2)}, u32[]{:S(2)}) collective-permute-start(f32[160,128]{1,0:T(8,128)S(1)} %merge.2.refs_0_), channel_id=1, source_target_pairs={{0,1},{1,0},{2,3},{3,2},{4,5},{5,4},{6,7},{7,6},{8,9},{9,8},{10,11... | collective-permute-start | bytes 245768 | tf_op jit(solution)/shard_map/ppermute | solution.py:341
  108.3 0.6 collective-permute-start.26
  108.9 1.8 %collective-permute-start.27 = (f32[160,128]{1,0:T(8,128)S(1)}, f32[160,128]{1,0:T(8,128)S(1)}, u32[]{:S(2)}, u32[]{:S(2)}) collective-permute-start(f32[160,128]{1,0:T(8,128)S(1)} %merge.2.refs_0_), channel_id=1, source_target_pairs={{0,3},{1,2},{2,1},{3,0},{4,7},{5,6},{6,5},{7,4},{8,11},{9,10},{10,... | collective-permute-start | bytes 245768 | tf_op jit(solution)/shard_map/ppermute | solution.py:341
  110.7 0.7 collective-permute-done.25.refs_1_
  111.4 6.7 %collective-permute-done.26.refs_2_ = f32[160,128]{1,0:T(8,128)S(1)} collective-permute-done((f32[160,128]{1,0:T(8,128)S(1)}, f32[160,128]{1,0:T(8,128)S(1)}, u32[]{:S(2)}, u32[]{:S(2)}) %collective-permute-start.26) | collective-permute-done | bytes 81952 | tf_op jit(solution)/shard_map/ppermute | solution.py:341
  118.1 3.2 %term.3 = (f32[64,3584]{1,0:T(8,128)S(1)}, f32[64,3584]{1,0:T(8,128)S(1)}) custom-call(f32[160,128]{1,0:T(8,128)S(1)} %merge.2.refs_0_, f32[160,128]{1,0:T(8,128)S(1)} %collective-permute-done.25.refs_1_, f32[160,128]{1,0:T(8,128)S(1)} %collective-permute-done.26.refs_2_, f32[160,128]{1,0:T(8,128)S(1)} %collective-permute-done.27.refs_3_, ...), custom_call_target="tpu_custom_call" | custom-call | tf_op jit(solution)/shard_map/term/pallas_call | solution.py:255
  121.4 5.7 %collective-permute-done.30.refs_1_.refs_3_ = f32[64,3584]{1,0:T(8,128)S(1)} collective-permute-done((f32[64,3584]{1,0:T(8,128)S(1)}, f32[64,3584]{1,0:T(8,128)S(1)}, u32[]{:S(2)}, u32[]{:S(2)}) %collective-permute-start.30) | collective-permute-done | bytes 917536 | tf_op jit(solution)/shard_map/ppermute | solution.py:340
  127.1 1.3 %join.1 = f32[64,7168]{1,0:T(8,128)} custom-call(f32[64,3584]{1,0:T(8,128)S(1)} %get-tuple-element.113.refs_0_, f32[64,3584]{1,0:T(8,128)S(1)} %collective-permute-done.28.refs_0_.refs_1_, f32[64,3584]{1,0:T(8,128)S(1)} %collective-permute-done.29.refs_2_, f32[64,3584]{1,0:T(8,128)S(1)} %collective-permute-done.30.refs_1_.refs_3_, f32[8,128]{1,0:T(8,128)S(1)} %arrived.1.refs_4_), custom_call_target="tpu_custom_call" | custom-call | tf_op jit(solution)/shard_map/join/pallas_call | solution.py:319
  (31 shorter events, 1.2 us)
Async XLA Ops:
  0.0 1.5 %copy-start.1 = (f32[7168,64]{0,1:T(8,128)S(1)}, f32[7168,64]{0,1:T(8,128)}, u32[]{:S(2)}) copy-start(f32[7168,64]{0,1:T(8,128)} %param.3) | copy-start | bytes 5505028
  1.7 6.4 %collective-permute-start.4 = (f32[64,3584]{1,0:T(8,128)S(1)}, f32[64,3584]{1,0:T(8,128)S(1)}, u32[]{:S(2)}, u32[]{:S(2)}) collective-permute-start(f32[64,3584]{1,0:T(8,128)S(1)} %get-tuple-element.65), channel_id=1, source_target_pairs={{0,4},{4,0},{8,12},{12,8},{16,20},{20,16},{24,28},{28,24},{1,5},{5... | collective-permute-start | bytes 2752520 | tf_op jit(solution)/shard_map/ppermute | solution.py:340
  2.2 23.3 %collective-permute-start.5 = (f32[64,3584]{1,0:T(8,128)S(1)}, f32[64,3584]{1,0:T(8,128)S(1)}, u32[]{:S(2)}, u32[]{:S(2)}) collective-permute-start(f32[64,3584]{1,0:T(8,128)S(1)} %get-tuple-element.64.refs_0_), channel_id=1, source_target_pairs={{0,16},{4,12},{8,24},{12,4},{16,0},{20,28},{24,8},{28,20},{1,17},{... | collective-permute-start | bytes 2752520 | tf_op jit(solution)/shard_map/ppermute | solution.py:340
  4.8 21.2 %collective-permute-start.6 = (f32[64,3584]{1,0:T(8,128)S(1)}, f32[64,3584]{1,0:T(8,128)S(1)}, u32[]{:S(2)}, u32[]{:S(2)}) collective-permute-start(f32[64,3584]{1,0:T(8,128)S(1)} %get-tuple-element.65), channel_id=1, source_target_pairs={{0,12},{4,16},{8,4},{12,24},{16,28},{20,0},{24,20},{28,8},{1,13},{... | collective-permute-start | bytes 2752520 | tf_op jit(solution)/shard_map/ppermute | solution.py:340
  4.8 2.3 %copy-start = (f32[160,7168]{1,0:T(8,128)S(1)}, f32[160,7168]{1,0:T(8,128)}, u32[]{:S(2)}) copy-start(f32[160,7168]{1,0:T(8,128)} %source.1) | copy-start | bytes 13762564
  7.5 20.4 %collective-permute-start.3 = (f32[64,3584]{1,0:T(8,128)S(1)}, f32[64,3584]{1,0:T(8,128)S(1)}, u32[]{:S(2)}, u32[]{:S(2)}) collective-permute-start(f32[64,3584]{1,0:T(8,128)S(1)} %get-tuple-element.63), channel_id=1, source_target_pairs={{0,4},{4,0},{8,12},{12,8},{16,20},{20,16},{24,28},{28,24},{1,5},{5... | collective-permute-start | bytes 2752520 | tf_op jit(solution)/shard_map/ppermute | solution.py:340
  7.7 23.0 %collective-permute-start.2 = (f32[96,3584]{1,0:T(8,128)S(1)}, f32[96,3584]{1,0:T(8,128)S(1)}, u32[]{:S(2)}, u32[]{:S(2)}) collective-permute-start(f32[96,3584]{1,0:T(8,128)S(1)} %get-tuple-element.61), channel_id=1, source_target_pairs={{0,4},{4,0},{8,12},{12,8},{16,20},{20,16},{24,28},{28,24},{1,5},{5... | collective-permute-start | bytes 4128776 | tf_op jit(solution)/shard_map/ppermute | solution.py:340
  8.1 44.3 %collective-permute-start = (f32[96,3584]{1,0:T(8,128)S(1)}, f32[96,3584]{1,0:T(8,128)S(1)}, u32[]{:S(2)}, u32[]{:S(2)}) collective-permute-start(f32[96,3584]{1,0:T(8,128)S(1)} %get-tuple-element.60.refs_0_), channel_id=1, source_target_pairs={{0,8},{4,20},{8,0},{12,28},{16,24},{20,4},{24,16},{28,12},{1,9},{5... | collective-permute-start | bytes 4128776 | tf_op jit(solution)/shard_map/ppermute | solution.py:340
  25.5 32.5 %collective-permute-start.1 = (f32[96,3584]{1,0:T(8,128)S(1)}, f32[96,3584]{1,0:T(8,128)S(1)}, u32[]{:S(2)}, u32[]{:S(2)}) collective-permute-start(f32[96,3584]{1,0:T(8,128)S(1)} %get-tuple-element.61), channel_id=1, source_target_pairs={{0,20},{4,8},{8,28},{12,0},{16,4},{20,24},{24,12},{28,16},{1,21},{... | collective-permute-start | bytes 4128776 | tf_op jit(solution)/shard_map/ppermute | solution.py:340
  26.0 46.1 %collective-permute-start.10 = (f32[64,3584]{1,0:T(8,128)S(1)}, f32[64,3584]{1,0:T(8,128)S(1)}, u32[]{:S(2)}, u32[]{:S(2)}) collective-permute-start(f32[64,3584]{1,0:T(8,128)S(1)} %get-tuple-element.62.refs_2_), channel_id=1, source_target_pairs={{0,8},{4,20},{8,0},{12,28},{16,24},{20,4},{24,16},{28,12},{1,9},{5... | collective-permute-start | bytes 2752520 | tf_op jit(solution)/shard_map/ppermute | solution.py:340
  28.0 46.9 %collective-permute-start.11 = (f32[64,3584]{1,0:T(8,128)S(1)}, f32[64,3584]{1,0:T(8,128)S(1)}, u32[]{:S(2)}, u32[]{:S(2)}) collective-permute-start(f32[64,3584]{1,0:T(8,128)S(1)} %get-tuple-element.63), channel_id=1, source_target_pairs={{0,20},{4,8},{8,28},{12,0},{16,4},{20,24},{24,12},{28,16},{1,21},{... | collective-permute-start | bytes 2752520 | tf_op jit(solution)/shard_map/ppermute | solution.py:340
  33.6 28.1 %collective-permute-start.7 = (f32[80,256]{1,0:T(8,128)S(1)}, f32[80,256]{1,0:T(8,128)S(1)}, u32[]{:S(2)}, u32[]{:S(2)}) collective-permute-start(f32[80,256]{1,0:T(8,128)S(1)} %get-tuple-element.67), channel_id=1, source_target_pairs={{0,1},{1,0},{2,3},{3,2},{4,5},{5,4},{6,7},{7,6},{8,9},{9,8},{10,11... | collective-permute-start | bytes 245768 | tf_op jit(solution)/shard_map/ppermute | solution.py:341
  52.4 9.3 %collective-permute-start.8 = (f32[80,256]{1,0:T(8,128)S(1)}, f32[80,256]{1,0:T(8,128)S(1)}, u32[]{:S(2)}, u32[]{:S(2)}) collective-permute-start(f32[80,256]{1,0:T(8,128)S(1)} %get-tuple-element.68), channel_id=1, source_target_pairs={{0,2},{1,3},{2,0},{3,1},{4,6},{5,7},{6,4},{7,5},{8,10},{9,11},{10,... | collective-permute-start | bytes 245768 | tf_op jit(solution)/shard_map/ppermute | solution.py:341
  58.0 6.9 %collective-permute-start.9 = (f32[80,256]{1,0:T(8,128)S(1)}, f32[80,256]{1,0:T(8,128)S(1)}, u32[]{:S(2)}, u32[]{:S(2)}) collective-permute-start(f32[80,256]{1,0:T(8,128)S(1)} %get-tuple-element.69), channel_id=1, source_target_pairs={{0,3},{1,2},{2,1},{3,0},{4,7},{5,6},{6,5},{7,4},{8,11},{9,10},{10,... | collective-permute-start | bytes 245768 | tf_op jit(solution)/shard_map/ppermute | solution.py:341
  66.9 8.0 %collective-permute-start.12 = (f32[48,256]{1,0:T(8,128)S(1)}, f32[48,256]{1,0:T(8,128)S(1)}, u32[]{:S(2)}, u32[]{:S(2)}) collective-permute-start(f32[48,256]{1,0:T(8,128)S(1)} %get-tuple-element.77), channel_id=1, source_target_pairs={{0,1},{1,0},{2,3},{3,2},{4,5},{5,4},{6,7},{7,6},{8,9},{9,8},{10,11... | collective-permute-start | bytes 147464 | tf_op jit(solution)/shard_map/ppermute | solution.py:341
  68.7 6.2 %collective-permute-start.13 = (f32[48,256]{1,0:T(8,128)S(1)}, f32[48,256]{1,0:T(8,128)S(1)}, u32[]{:S(2)}, u32[]{:S(2)}) collective-permute-start(f32[48,256]{1,0:T(8,128)S(1)} %get-tuple-element.78), channel_id=1, source_target_pairs={{0,2},{1,3},{2,0},{3,1},{4,6},{5,7},{6,4},{7,5},{8,10},{9,11},{10,... | collective-permute-start | bytes 147464 | tf_op jit(solution)/shard_map/ppermute | solution.py:341
  71.3 5.9 %collective-permute-start.14 = (f32[48,256]{1,0:T(8,128)S(1)}, f32[48,256]{1,0:T(8,128)S(1)}, u32[]{:S(2)}, u32[]{:S(2)}) collective-permute-start(f32[48,256]{1,0:T(8,128)S(1)} %get-tuple-element.79), channel_id=1, source_target_pairs={{0,3},{1,2},{2,1},{3,0},{4,7},{5,6},{6,5},{7,4},{8,11},{9,10},{10,... | collective-permute-start | bytes 147464 | tf_op jit(solution)/shard_map/ppermute | solution.py:341
  78.7 4.5 %collective-permute-start.15 = (f32[32,256]{1,0:T(8,128)S(1)}, f32[32,256]{1,0:T(8,128)S(1)}, u32[]{:S(2)}, u32[]{:S(2)}) collective-permute-start(f32[32,256]{1,0:T(8,128)S(1)} %get-tuple-element.87), channel_id=1, source_target_pairs={{0,1},{1,0},{2,3},{3,2},{4,5},{5,4},{6,7},{7,6},{8,9},{9,8},{10,11... | collective-permute-start | bytes 98312 | tf_op jit(solution)/shard_map/ppermute | solution.py:341
  78.7 5.1 %collective-permute-start.16 = (f32[32,256]{1,0:T(8,128)S(1)}, f32[32,256]{1,0:T(8,128)S(1)}, u32[]{:S(2)}, u32[]{:S(2)}) collective-permute-start(f32[32,256]{1,0:T(8,128)S(1)} %get-tuple-element.88), channel_id=1, source_target_pairs={{0,2},{1,3},{2,0},{3,1},{4,6},{5,7},{6,4},{7,5},{8,10},{9,11},{10,... | collective-permute-start | bytes 98312 | tf_op jit(solution)/shard_map/ppermute | solution.py:341
  80.9 5.7 %collective-permute-start.17 = (f32[32,256]{1,0:T(8,128)S(1)}, f32[32,256]{1,0:T(8,128)S(1)}, u32[]{:S(2)}, u32[]{:S(2)}) collective-permute-start(f32[32,256]{1,0:T(8,128)S(1)} %get-tuple-element.89), channel_id=1, source_target_pairs={{0,3},{1,2},{2,1},{3,0},{4,7},{5,6},{6,5},{7,4},{8,11},{9,10},{10,... | collective-permute-start | bytes 98312 | tf_op jit(solution)/shard_map/ppermute | solution.py:341
  86.7 3.5 %collective-permute-start.20 = (f32[80,128]{1,0:T(8,128)S(1)}, f32[80,128]{1,0:T(8,128)S(1)}, u32[]{:S(2)}, u32[]{:S(2)}) collective-permute-start(f32[80,128]{1,0:T(8,128)S(1)} %get-tuple-element.93), channel_id=1, source_target_pairs={{0,12},{4,16},{8,4},{12,24},{16,28},{20,0},{24,20},{28,8},{1,13},{... | collective-permute-start | bytes 122888 | tf_op jit(solution)/shard_map/ppermute | solution.py:340
  86.8 4.8 %collective-permute-start.21 = (f32[80,128]{1,0:T(8,128)S(1)}, f32[80,128]{1,0:T(8,128)S(1)}, u32[]{:S(2)}, u32[]{:S(2)}) collective-permute-start(f32[80,128]{1,0:T(8,128)S(1)} %get-tuple-element.94), channel_id=1, source_target_pairs={{0,28},{4,24},{8,20},{12,16},{16,12},{20,8},{24,4},{28,0},{1,29},{... | collective-permute-start | bytes 122888 | tf_op jit(solution)/shard_map/ppermute | solution.py:340
  91.6 8.2 %collective-permute-start.22 = (f32[160,128]{1,0:T(8,128)S(1)}, f32[160,128]{1,0:T(8,128)S(1)}, u32[]{:S(2)}, u32[]{:S(2)}) collective-permute-start(f32[160,128]{1,0:T(8,128)S(1)} %merge.3.refs_0_), channel_id=1, source_target_pairs={{0,1},{1,0},{2,3},{3,2},{4,5},{5,4},{6,7},{7,6},{8,9},{9,8},{10,11... | collective-permute-start | bytes 245768 | tf_op jit(solution)/shard_map/ppermute | solution.py:341
  91.7 8.1 %collective-permute-start.23 = (f32[160,128]{1,0:T(8,128)S(1)}, f32[160,128]{1,0:T(8,128)S(1)}, u32[]{:S(2)}, u32[]{:S(2)}) collective-permute-start(f32[160,128]{1,0:T(8,128)S(1)} %merge.3.refs_0_), channel_id=1, source_target_pairs={{0,2},{1,3},{2,0},{3,1},{4,6},{5,7},{6,4},{7,5},{8,10},{9,11},{10,... | collective-permute-start | bytes 245768 | tf_op jit(solution)/shard_map/ppermute | solution.py:341
  94.2 7.1 %collective-permute-start.24 = (f32[160,128]{1,0:T(8,128)S(1)}, f32[160,128]{1,0:T(8,128)S(1)}, u32[]{:S(2)}, u32[]{:S(2)}) collective-permute-start(f32[160,128]{1,0:T(8,128)S(1)} %merge.3.refs_0_), channel_id=1, source_target_pairs={{0,3},{1,2},{2,1},{3,0},{4,7},{5,6},{6,5},{7,4},{8,11},{9,10},{10,... | collective-permute-start | bytes 245768 | tf_op jit(solution)/shard_map/ppermute | solution.py:341
  96.1 1.2 collective-permute-start.18
  96.3 3.4 %collective-permute-start.19 = (f32[80,128]{1,0:T(8,128)S(1)}, f32[80,128]{1,0:T(8,128)S(1)}, u32[]{:S(2)}, u32[]{:S(2)}) collective-permute-start(f32[80,128]{1,0:T(8,128)S(1)} %get-tuple-element.92), channel_id=1, source_target_pairs={{0,20},{4,8},{8,28},{12,0},{16,4},{20,24},{24,12},{28,16},{1,21},{... | collective-permute-start | bytes 122888 | tf_op jit(solution)/shard_map/ppermute | solution.py:340
  104.5 16.8 %collective-permute-start.28 = (f32[64,3584]{1,0:T(8,128)S(1)}, f32[64,3584]{1,0:T(8,128)S(1)}, u32[]{:S(2)}, u32[]{:S(2)}) collective-permute-start(f32[64,3584]{1,0:T(8,128)S(1)} %get-tuple-element.106), channel_id=1, source_target_pairs={{0,16},{4,12},{8,24},{12,4},{16,0},{20,28},{24,8},{28,20},{1,17},{... | collective-permute-start | bytes 2752520 | tf_op jit(solution)/shard_map/ppermute | solution.py:340
  105.8 21.2 %collective-permute-start.30 = (f32[64,3584]{1,0:T(8,128)S(1)}, f32[64,3584]{1,0:T(8,128)S(1)}, u32[]{:S(2)}, u32[]{:S(2)}) collective-permute-start(f32[64,3584]{1,0:T(8,128)S(1)} %get-tuple-element.107), channel_id=1, source_target_pairs={{0,20},{4,8},{8,28},{12,0},{16,4},{20,24},{24,12},{28,16},{1,21},{... | collective-permute-start | bytes 2752520 | tf_op jit(solution)/shard_map/ppermute | solution.py:340
  105.8 5.5 %collective-permute-start.25 = (f32[160,128]{1,0:T(8,128)S(1)}, f32[160,128]{1,0:T(8,128)S(1)}, u32[]{:S(2)}, u32[]{:S(2)}) collective-permute-start(f32[160,128]{1,0:T(8,128)S(1)} %merge.2.refs_0_), channel_id=1, source_target_pairs={{0,1},{1,0},{2,3},{3,2},{4,5},{5,4},{6,7},{7,6},{8,9},{9,8},{10,11... | collective-permute-start | bytes 245768 | tf_op jit(solution)/shard_map/ppermute | solution.py:341
  108.3 9.7 %collective-permute-start.26 = (f32[160,128]{1,0:T(8,128)S(1)}, f32[160,128]{1,0:T(8,128)S(1)}, u32[]{:S(2)}, u32[]{:S(2)}) collective-permute-start(f32[160,128]{1,0:T(8,128)S(1)} %merge.2.refs_0_), channel_id=1, source_target_pairs={{0,2},{1,3},{2,0},{3,1},{4,6},{5,7},{6,4},{7,5},{8,10},{9,11},{10,... | collective-permute-start | bytes 245768 | tf_op jit(solution)/shard_map/ppermute | solution.py:341
  108.9 9.1 %collective-permute-start.27 = (f32[160,128]{1,0:T(8,128)S(1)}, f32[160,128]{1,0:T(8,128)S(1)}, u32[]{:S(2)}, u32[]{:S(2)}) collective-permute-start(f32[160,128]{1,0:T(8,128)S(1)} %merge.2.refs_0_), channel_id=1, source_target_pairs={{0,3},{1,2},{2,1},{3,0},{4,7},{5,6},{6,5},{7,4},{8,11},{9,10},{10,... | collective-permute-start | bytes 245768 | tf_op jit(solution)/shard_map/ppermute | solution.py:341
  121.3 5.8 %collective-permute-start.29 = (f32[64,3584]{1,0:T(8,128)S(1)}, f32[64,3584]{1,0:T(8,128)S(1)}, u32[]{:S(2)}, u32[]{:S(2)}) collective-permute-start(f32[64,3584]{1,0:T(8,128)S(1)} %get-tuple-element.114), channel_id=1, source_target_pairs={{0,4},{4,0},{8,12},{12,8},{16,20},{20,16},{24,28},{28,24},{1,5},{5... | collective-permute-start | bytes 2752520 | tf_op jit(solution)/shard_map/ppermute | solution.py:340

commit v5 on v4

--- a/solution.py
+++ b/solution.py
@@ -219,7 +219,7 @@
     )(*inputs)
 
 
-def term_kernel(zs, spots, groups, begin, *refs):
+def term_kernel(zs, spots, groups, left, *refs):
     got = [refs[c * zs : (c + 1) * zs] for c in range(len(spots))]
     refs = refs[len(spots) * zs :]
     acts = refs[: 2 * groups]
@@ -230,7 +230,7 @@
     for pieces, segments in zip(got, spots):
         for s in range(zs):
             for at, part, to in segments:
-                full[pl.ds(to + (z ^ s) * part, part)] = pieces[s][at : at + part]
+                full[pl.ds(to + (z ^ s) * part, part)] = pieces[s][at : at + part, left : left + columns]
     h, l = split(full[...].T)
     both = jnp.concatenate([h, l], 0)
     step = block_of(size, 896)
@@ -238,7 +238,7 @@
     @pl.loop(0, size // step)
     def _(i):
         to = pl.ds(pl.multiple_of(i * step, step), step)
-        at = pl.ds(pl.multiple_of(begin + i * step, 128), step)
+        at = pl.ds(pl.multiple_of(i * step, 128), step)
         high = jnp.concatenate([x[:, at] for x in acts[::2]], 0)
         low = jnp.concatenate([x[:, at] for x in acts[1::2]], 0)
         d = dot(both, high)
@@ -247,14 +247,14 @@
             out[:, to] = total[o * width : (o + 1) * width]
 
 
-def terms(got, acts, spots, width, low=0, high=None):
-    zs, columns = len(got[0]), got[0][0].shape[1]
+def terms(got, acts, spots, width, left, columns):
+    zs = len(got[0])
     half = acts[0][0].shape[1]
     count = columns // width
     rows = sum(act[0].shape[0] for act in acts)
     return pl.pallas_call(
-        functools.partial(term_kernel, zs, spots, len(acts), low),
-        out_shape=[jax.ShapeDtypeStruct((width, (high or half) - low), jnp.float32)] * count,
+        functools.partial(term_kernel, zs, spots, len(acts), left),
+        out_shape=[jax.ShapeDtypeStruct((width, half), jnp.float32)] * count,
         in_specs=[VMEM] * (zs * len(got) + 2 * len(acts)),
         out_specs=[VMEM] * count,
         scratch_shapes=[pltpu.VMEM((rows, columns), jnp.float32)],
@@ -346,9 +346,9 @@
 
     def reduce(group, cols):
         pieces, act = mix(group, cols, zs)
-        return list(pieces[:1]) + [across(pieces[s], s) for s in order][::-1], act
-
-    order = range(zs - 1, 0, -1)
+        return list(pieces[:1]) + [across(pieces[s], s) for s in order], act
+
+    order = sorted(range(1, zs), key=lambda s: s ^ (zs // 2))
 
     def far(own, other, which):
         got = []
@@ -396,29 +396,24 @@
     chunk = (total, [send(x, pair) for x, pair in zip(payloads, pairs)])
 
     def spread(mine):
-        return [mine] + [across(mine, s) for s in order][::-1]
+        return [mine] + [x for _, x in sorted([(s, across(mine, s)) for s in order], key=lambda t: t[0])]
 
     away = spread(merge(side, factor, turns[1:], [chunk]))
     here = merge(side, factor, turns[:1], [chunk])
     here, away = hold((here, away))
     half = acts[0][0].shape[1]
-    cuts = [(0, half)]
     same, cross = [], []
-    for low, high in cuts:
-        term = terms([away], acts, [spots], width, low, high)
-        same.append([send(term[2 * q - 2], along(q, 0, "results")) for q in turns[1:]])
-        cross.append([send(term[2 * q - 1], along(q, 1, "results")) for q in turns[1:]])
-        (here, away), term = hold(((here, away), term))
+    for q in turns[1:]:
+        for core, results in ((1, cross), (0, same)):
+            left = width * (2 * q - 2 + core)
+            (term,) = terms([away], acts, [spots], width, left, width)
+            results.append(send(term, along(q, core, "results")))
+            (here, away), term = hold(((here, away), term))
     here = spread(here)
     here, term = hold((here, term))
-    mine, near = terms([here], acts, [spots], width)
+    mine, near = terms([here], acts, [spots], width, 0, 2 * width)
     near = send(near, along(0, 1, "results"))
-    out = ()
-    for (low, high), s, c in zip(cuts, same, cross):
-        last = high == half
-        mark = [arrived([x for part in (same + cross) for x in part])] if last else []
-        out = (join([mine] + s, [near] + c, low, mark, out),)
-    return out[0]
+    return join([mine] + same, [near] + cross, 0, [arrived(same + [arrived(cross)])])
 
 
 def solution(mesh):

time: 129 us -> 127 us (0.984)
  waiting for transfers between devices: 67.6 us -> 63.8 us
  Pallas kernels: 16.3 us -> 17.7 us
    ppermute x15, waiting for transfers between devices: 17.9 us -> 14.8 us  [shards(): lax.ppermute(x, 'feat', [(i, i ^ s) for i in range(zs)])]
    pallas_call x2 -> x3, Pallas kernels: 6.42 us -> 7.86 us  [terms(): pl.pallas_call(functools.partial(term_kernel, zs, spots, len(acts), left)...]
  transfers between devices with their start and end apart: 31 -> 31, of which waited for: 17 -> 15; matrix products, arithmetic and copies ran while one was open for 0% -> 0% of each run, Pallas kernels for 8% -> 10%
where the time goes in v5:
time: 127 us; the launch traced here: 126 us
  waiting for transfers between devices  63.8 us (50%)
  starting transfers between devices  41 us (32%)
  Pallas kernels  17.7 us (14%)
  local copies, waits for them, and re-layouts  3.8 us (3%)
    ppermute x16, waiting for transfers between devices, shards(): send = lambda x, pairs: lax.ppermute(x, 'tok', pairs)  49 us
    ppermute x15, starting transfers between devices, shards(): lax.ppermute(x, 'feat', [(i, i ^ s) for i in range(zs)])  26.5 us
    ppermute x15, waiting for transfers between devices, shards(): lax.ppermute(x, 'feat', [(i, i ^ s) for i in range(zs)])  14.8 us
    ppermute x16, starting transfers between devices, shards(): send = lambda x, pairs: lax.ppermute(x, 'tok', pairs)  14.6 us
    pallas_call x3, Pallas kernels, terms(): pl.pallas_call(functools.partial(term_kernel, zs, spots, len(acts), left)...  7.86 us
    pallas_call x3, Pallas kernels, mix(): pl.pallas_call(functools.partial(mix_kernel, count, zs), out_shape=[piece...  6.36 us
    unnamed x4, local copies, waits for them, and re-layouts  3.8 us
  transfers between devices with their start and end apart: 31, of which 15 were waited for; matrix products, arithmetic and copies ran while one was open for 0% of the time, Pallas kernels for 10%

profile of v5, /device:TPU:0, one launch (start us, length us, event | category | flops | bytes accessed | tf_op | source)
XLA Modules:
  0.0 126.5 jit_solution(5222725700446380545)
XLA Ops:
  0.0 1.5 %copy-done.1 = f32[7168,64]{0,1:T(8,128)S(1)} copy-done((f32[7168,64]{0,1:T(8,128)S(1)}, f32[7168,64]{0,1:T(8,128)}, u32[]{:S(2)}) %copy-start.1) | copy-done | bytes 1835032
  1.7 0.5 collective-permute-start.4
  2.2 2.6 %collective-permute-start.5 = (f32[64,3584]{1,0:T(8,128)S(1)}, f32[64,3584]{1,0:T(8,128)S(1)}, u32[]{:S(2)}, u32[]{:S(2)}) collective-permute-start(f32[64,3584]{1,0:T(8,128)S(1)} %get-tuple-element.67.refs_0_), channel_id=1, source_target_pairs={{0,16},{4,12},{8,24},{12,4},{16,0},{20,28},{24,8},{28,20},{1,17},{... | collective-permute-start | bytes 2752520 | tf_op jit(solution)/shard_map/ppermute | solution.py:340
  4.8 2.3 %copy-done = f32[160,7168]{1,0:T(8,128)S(1)} copy-done((f32[160,7168]{1,0:T(8,128)S(1)}, f32[160,7168]{1,0:T(8,128)}, u32[]{:S(2)}) %copy-start) | copy-done | bytes 4587544
  7.1 0.4 cut.2
  7.7 0.4 collective-permute-start.2
  8.1 1.7 %collective-permute-start = (f32[96,3584]{1,0:T(8,128)S(1)}, f32[96,3584]{1,0:T(8,128)S(1)}, u32[]{:S(2)}, u32[]{:S(2)}) collective-permute-start(f32[96,3584]{1,0:T(8,128)S(1)} %get-tuple-element.63.refs_0_), channel_id=1, source_target_pairs={{0,8},{4,20},{8,0},{12,28},{16,24},{20,4},{24,16},{28,12},{1,9},{5... | collective-permute-start | bytes 4128776 | tf_op jit(solution)/shard_map/ppermute | solution.py:340
  9.8 15.6 %collective-permute-done.5.refs_2_ = f32[64,3584]{1,0:T(8,128)S(1)} collective-permute-done((f32[64,3584]{1,0:T(8,128)S(1)}, f32[64,3584]{1,0:T(8,128)S(1)}, u32[]{:S(2)}, u32[]{:S(2)}) %collective-permute-start.5) | collective-permute-done | bytes 917536 | tf_op jit(solution)/shard_map/ppermute | solution.py:340
  25.5 0.5 collective-permute-done.6.refs_3_
  26.0 2.0 %collective-permute-start.10 = (f32[64,3584]{1,0:T(8,128)S(1)}, f32[64,3584]{1,0:T(8,128)S(1)}, u32[]{:S(2)}, u32[]{:S(2)}) collective-permute-start(f32[64,3584]{1,0:T(8,128)S(1)} %get-tuple-element.65.refs_2_), channel_id=1, source_target_pairs={{0,8},{4,20},{8,0},{12,28},{16,24},{20,4},{24,16},{28,12},{1,9},{5... | collective-permute-start | bytes 2752520 | tf_op jit(solution)/shard_map/ppermute | solution.py:340
  28.0 1.3 %collective-permute-start.11 = (f32[64,3584]{1,0:T(8,128)S(1)}, f32[64,3584]{1,0:T(8,128)S(1)}, u32[]{:S(2)}, u32[]{:S(2)}) collective-permute-start(f32[64,3584]{1,0:T(8,128)S(1)} %get-tuple-element.66), channel_id=1, source_target_pairs={{0,20},{4,8},{8,28},{12,0},{16,4},{20,24},{24,12},{28,16},{1,21},{... | collective-permute-start | bytes 2752520 | tf_op jit(solution)/shard_map/ppermute | solution.py:340
  29.3 1.4 %turn.1.refs_4_.refs_2_ = bf16[3584,512]{1,0:T(8,128)(2,1)S(1)} custom-call(f32[64,3584]{1,0:T(8,128)S(1)} %get-tuple-element.67.refs_0_, f32[64,3584]{1,0:T(8,128)S(1)} %collective-permute-done.4.refs_1_, f32[64,3584]{1,0:T(8,128)S(1)} %collective-permute-done.5.refs_2_, f32[64,3584]{1,0:T(8,128)S(1)} %collective-permute-done.6.refs_3_), custom_call_target="tpu_custom_call" | custom-call | tf_op jit(solution)/shard_map/turn/pallas_call | solution.py:97
  30.7 2.9 %mix.3 = (f32[80,256]{1,0:T(8,128)S(1)}, f32[80,256]{1,0:T(8,128)S(1)}, f32[80,256]{1,0:T(8,128)S(1)}, f32[80,256]{1,0:T(8,128)S(1)}, bf16[320,3584]{1,0:T(8,128)(2,1)S(1)}, /*index=5*/bf16[320,3584]{1,0:T(8,128)(2,1)S(1)}) custom-call(f32[96,3584]{1,0:T(8,128)S(1)} %get-tuple-element.63.refs_0_, f32[96,3584]{1,0:T(8,128)S(1)} %collective-permute-done.2.refs_1_, ...), custom_call_target="tpu_custom_call" | custom-call | flops 1761607680 | bytes 12845056 | tf_op jit(solution)/shard_map/mix/pallas_call | solution.py:139
  33.6 2.6 %collective-permute-start.7 = (f32[80,256]{1,0:T(8,128)S(1)}, f32[80,256]{1,0:T(8,128)S(1)}, u32[]{:S(2)}, u32[]{:S(2)}) collective-permute-start(f32[80,256]{1,0:T(8,128)S(1)} %get-tuple-element.70), channel_id=1, source_target_pairs={{0,2},{1,3},{2,0},{3,1},{4,6},{5,7},{6,4},{7,5},{8,10},{9,11},{10,... | collective-permute-start | bytes 245768 | tf_op jit(solution)/shard_map/ppermute | solution.py:341
  36.3 16.1 %collective-permute-done.refs_0_ = f32[96,3584]{1,0:T(8,128)S(1)} collective-permute-done((f32[96,3584]{1,0:T(8,128)S(1)}, f32[96,3584]{1,0:T(8,128)S(1)}, u32[]{:S(2)}, u32[]{:S(2)}) %collective-permute-start) | collective-permute-done | bytes 1376288 | tf_op jit(solution)/shard_map/ppermute | solution.py:340
  52.4 4.0 %collective-permute-start.8 = (f32[80,256]{1,0:T(8,128)S(1)}, f32[80,256]{1,0:T(8,128)S(1)}, u32[]{:S(2)}, u32[]{:S(2)}) collective-permute-start(f32[80,256]{1,0:T(8,128)S(1)} %get-tuple-element.71), channel_id=1, source_target_pairs={{0,3},{1,2},{2,1},{3,0},{4,7},{5,6},{6,5},{7,4},{8,11},{9,10},{10,... | collective-permute-start | bytes 245768 | tf_op jit(solution)/shard_map/ppermute | solution.py:341
  56.4 1.6 %collective-permute-done.1.refs_1_ = f32[96,3584]{1,0:T(8,128)S(1)} collective-permute-done((f32[96,3584]{1,0:T(8,128)S(1)}, f32[96,3584]{1,0:T(8,128)S(1)}, u32[]{:S(2)}, u32[]{:S(2)}) %collective-permute-start.1) | collective-permute-done | bytes 1376288 | tf_op jit(solution)/shard_map/ppermute | solution.py:340
  58.0 1.7 %collective-permute-start.9 = (f32[80,256]{1,0:T(8,128)S(1)}, f32[80,256]{1,0:T(8,128)S(1)}, u32[]{:S(2)}, u32[]{:S(2)}) collective-permute-start(f32[80,256]{1,0:T(8,128)S(1)} %get-tuple-element.72), channel_id=1, source_target_pairs={{0,1},{1,0},{2,3},{3,2},{4,5},{5,4},{6,7},{7,6},{8,9},{9,8},{10,11... | collective-permute-start | bytes 245768 | tf_op jit(solution)/shard_map/ppermute | solution.py:341
  59.7 3.4 %collective-permute-done.9.refs_3_ = f32[80,256]{1,0:T(8,128)S(1)} collective-permute-done((f32[80,256]{1,0:T(8,128)S(1)}, f32[80,256]{1,0:T(8,128)S(1)}, u32[]{:S(2)}, u32[]{:S(2)}) %collective-permute-start.9) | collective-permute-done | bytes 81952 | tf_op jit(solution)/shard_map/ppermute | solution.py:341
  63.1 2.0 %mix.4 = (f32[48,256]{1,0:T(8,128)S(1)}, f32[48,256]{1,0:T(8,128)S(1)}, f32[48,256]{1,0:T(8,128)S(1)}, f32[48,256]{1,0:T(8,128)S(1)}, bf16[192,3584]{1,0:T(8,128)(2,1)S(1)}, /*index=5*/bf16[192,3584]{1,0:T(8,128)(2,1)S(1)}) custom-call(f32[96,3584]{1,0:T(8,128)S(1)} %collective-permute-done.refs_0_, f32[96,3584]{1,0:T(8,128)S(1)} %collective-permute-done.1.refs_1_, ...), custom_call_target="tpu_custom_call" | custom-call | flops 1056964608 | bytes 9175040 | tf_op jit(solution)/shard_map/mix/pallas_call | solution.py:139
  65.1 2.8 %collective-permute-start.12 = (f32[48,256]{1,0:T(8,128)S(1)}, f32[48,256]{1,0:T(8,128)S(1)}, u32[]{:S(2)}, u32[]{:S(2)}) collective-permute-start(f32[48,256]{1,0:T(8,128)S(1)} %get-tuple-element.80), channel_id=1, source_target_pairs={{0,2},{1,3},{2,0},{3,1},{4,6},{5,7},{6,4},{7,5},{8,10},{9,11},{10,... | collective-permute-start | bytes 147464 | tf_op jit(solution)/shard_map/ppermute | solution.py:341
  67.9 1.4 %collective-permute-start.13 = (f32[48,256]{1,0:T(8,128)S(1)}, f32[48,256]{1,0:T(8,128)S(1)}, u32[]{:S(2)}, u32[]{:S(2)}) collective-permute-start(f32[48,256]{1,0:T(8,128)S(1)} %get-tuple-element.81), channel_id=1, source_target_pairs={{0,3},{1,2},{2,1},{3,0},{4,7},{5,6},{6,5},{7,4},{8,11},{9,10},{10,... | collective-permute-start | bytes 147464 | tf_op jit(solution)/shard_map/ppermute | solution.py:341
  69.5 2.6 %collective-permute-done.10.refs_0_ = f32[64,3584]{1,0:T(8,128)S(1)} collective-permute-done((f32[64,3584]{1,0:T(8,128)S(1)}, f32[64,3584]{1,0:T(8,128)S(1)}, u32[]{:S(2)}, u32[]{:S(2)}) %collective-permute-start.10) | collective-permute-done | bytes 917536 | tf_op jit(solution)/shard_map/ppermute | solution.py:340
  72.1 2.8 %collective-permute-done.11.refs_1_ = f32[64,3584]{1,0:T(8,128)S(1)} collective-permute-done((f32[64,3584]{1,0:T(8,128)S(1)}, f32[64,3584]{1,0:T(8,128)S(1)}, u32[]{:S(2)}, u32[]{:S(2)}) %collective-permute-start.11) | collective-permute-done | bytes 917536 | tf_op jit(solution)/shard_map/ppermute | solution.py:340
  74.9 1.5 %mix.5 = (f32[32,256]{1,0:T(8,128)S(1)}, f32[32,256]{1,0:T(8,128)S(1)}, f32[32,256]{1,0:T(8,128)S(1)}, f32[32,256]{1,0:T(8,128)S(1)}, bf16[128,3584]{1,0:T(8,128)(2,1)S(1)}, /*index=5*/bf16[128,3584]{1,0:T(8,128)(2,1)S(1)}) custom-call(f32[64,3584]{1,0:T(8,128)S(1)} %collective-permute-done.10.refs_0_, f32[64,3584]{1,0:T(8,128)S(1)} %collective-permute-done.11.refs_1_, ...), custom_call_target="tpu_custom_call" | custom-call | flops 704643072 | bytes 7340032 | tf_op jit(solution)/shard_map/mix/pallas_call | solution.py:139
  76.4 2.9 %collective-permute-start.15 = (f32[32,256]{1,0:T(8,128)S(1)}, f32[32,256]{1,0:T(8,128)S(1)}, u32[]{:S(2)}, u32[]{:S(2)}) collective-permute-start(f32[32,256]{1,0:T(8,128)S(1)} %get-tuple-element.90), channel_id=1, source_target_pairs={{0,2},{1,3},{2,0},{3,1},{4,6},{5,7},{6,4},{7,5},{8,10},{9,11},{10,... | collective-permute-start | bytes 98312 | tf_op jit(solution)/shard_map/ppermute | solution.py:341
  79.3 1.3 %collective-permute-start.16 = (f32[32,256]{1,0:T(8,128)S(1)}, f32[32,256]{1,0:T(8,128)S(1)}, u32[]{:S(2)}, u32[]{:S(2)}) collective-permute-start(f32[32,256]{1,0:T(8,128)S(1)} %get-tuple-element.91), channel_id=1, source_target_pairs={{0,3},{1,2},{2,1},{3,0},{4,7},{5,6},{6,5},{7,4},{8,11},{9,10},{10,... | collective-permute-start | bytes 98312 | tf_op jit(solution)/shard_map/ppermute | solution.py:341
  80.9 0.4 collective-permute-done.15.refs_9_
  81.3 3.8 %collective-permute-done.16.refs_10_ = f32[32,256]{1,0:T(8,128)S(1)} collective-permute-done((f32[32,256]{1,0:T(8,128)S(1)}, f32[32,256]{1,0:T(8,128)S(1)}, u32[]{:S(2)}, u32[]{:S(2)}) %collective-permute-start.16) | collective-permute-done | bytes 32800 | tf_op jit(solution)/shard_map/ppermute | solution.py:341
  85.2 2.6 %collective-permute-start.21 = (f32[80,128]{1,0:T(8,128)S(1)}, f32[80,128]{1,0:T(8,128)S(1)}, u32[]{:S(2)}, u32[]{:S(2)}) collective-permute-start(f32[80,128]{1,0:T(8,128)S(1)} %get-tuple-element.97), channel_id=1, source_target_pairs={{0,28},{4,24},{8,20},{12,16},{16,12},{20,8},{24,4},{28,0},{1,29},{... | collective-permute-start | bytes 122888 | tf_op jit(solution)/shard_map/ppermute | solution.py:340
  87.9 0.8 collective-permute-done.20.refs_1_
  88.6 1.4 %collective-permute-done.21.refs_2_ = f32[80,128]{1,0:T(8,128)S(1)} collective-permute-done((f32[80,128]{1,0:T(8,128)S(1)}, f32[80,128]{1,0:T(8,128)S(1)}, u32[]{:S(2)}, u32[]{:S(2)}) %collective-permute-start.21) | collective-permute-done | bytes 40992 | tf_op jit(solution)/shard_map/ppermute | solution.py:340
  90.1 2.6 %collective-permute-start.23 = (f32[160,128]{1,0:T(8,128)S(1)}, f32[160,128]{1,0:T(8,128)S(1)}, u32[]{:S(2)}, u32[]{:S(2)}) collective-permute-start(f32[160,128]{1,0:T(8,128)S(1)} %merge.3.refs_0_), channel_id=1, source_target_pairs={{0,2},{1,3},{2,0},{3,1},{4,6},{5,7},{6,4},{7,5},{8,10},{9,11},{10,... | collective-permute-start | bytes 245768 | tf_op jit(solution)/shard_map/ppermute | solution.py:341
  92.7 1.8 %collective-permute-start.24 = (f32[160,128]{1,0:T(8,128)S(1)}, f32[160,128]{1,0:T(8,128)S(1)}, u32[]{:S(2)}, u32[]{:S(2)}) collective-permute-start(f32[160,128]{1,0:T(8,128)S(1)} %merge.3.refs_0_), channel_id=1, source_target_pairs={{0,3},{1,2},{2,1},{3,0},{4,7},{5,6},{6,5},{7,4},{8,11},{9,10},{10,... | collective-permute-start | bytes 245768 | tf_op jit(solution)/shard_map/ppermute | solution.py:341
  94.5 0.3 collective-permute-start.18
  94.8 0.9 collective-permute-start.19
  95.7 2.5 %collective-permute-done.19.refs_2_ = f32[80,128]{1,0:T(8,128)S(1)} collective-permute-done((f32[80,128]{1,0:T(8,128)S(1)}, f32[80,128]{1,0:T(8,128)S(1)}, u32[]{:S(2)}, u32[]{:S(2)}) %collective-permute-start.19) | collective-permute-done | bytes 40992 | tf_op jit(solution)/shard_map/ppermute | solution.py:340
  98.2 1.6 %collective-permute-done.24.refs_3_ = f32[160,128]{1,0:T(8,128)S(1)} collective-permute-done((f32[160,128]{1,0:T(8,128)S(1)}, f32[160,128]{1,0:T(8,128)S(1)}, u32[]{:S(2)}, u32[]{:S(2)}) %collective-permute-start.24) | collective-permute-done | bytes 81952 | tf_op jit(solution)/shard_map/ppermute | solution.py:341
  99.8 2.4 %term.3 = f32[64,3584]{1,0:T(8,128)S(1)} custom-call(f32[160,128]{1,0:T(8,128)S(1)} %merge.3.refs_0_, f32[160,128]{1,0:T(8,128)S(1)} %collective-permute-done.22.refs_1_, f32[160,128]{1,0:T(8,128)S(1)} %collective-permute-done.23.refs_2_, f32[160,128]{1,0:T(8,128)S(1)} %collective-permute-done.24.refs_3_, bf16[320,3584]{1,0:T(8,128)(2,1)S(1)} %get-tuple-element.103.refs_4_, ...), custom_call_target="tpu_custom_call" | custom-call | tf_op jit(solution)/shard_map/term/pallas_call | solution.py:255
  102.5 2.3 %term.4 = f32[64,3584]{1,0:T(8,128)S(1)} custom-call(f32[160,128]{1,0:T(8,128)S(1)} %merge.3.refs_0_, f32[160,128]{1,0:T(8,128)S(1)} %collective-permute-done.22.refs_1_, f32[160,128]{1,0:T(8,128)S(1)} %collective-permute-done.23.refs_2_, f32[160,128]{1,0:T(8,128)S(1)} %collective-permute-done.24.refs_3_, bf16[320,3584]{1,0:T(8,128)(2,1)S(1)} %get-tuple-element.103.refs_4_, ...), custom_call_target="tpu_custom_call" | custom-call | tf_op jit(solution)/shard_map/term/pallas_call | solution.py:255
  104.7 2.4 %collective-permute-start.25 = (f32[160,128]{1,0:T(8,128)S(1)}, f32[160,128]{1,0:T(8,128)S(1)}, u32[]{:S(2)}, u32[]{:S(2)}) collective-permute-start(f32[160,128]{1,0:T(8,128)S(1)} %merge.2.refs_0_), channel_id=1, source_target_pairs={{0,1},{1,0},{2,3},{3,2},{4,5},{5,4},{6,7},{7,6},{8,9},{9,8},{10,11... | collective-permute-start | bytes 245768 | tf_op jit(solution)/shard_map/ppermute | solution.py:341
  107.1 1.0 collective-permute-start.26
  108.1 1.4 %collective-permute-start.27 = (f32[160,128]{1,0:T(8,128)S(1)}, f32[160,128]{1,0:T(8,128)S(1)}, u32[]{:S(2)}, u32[]{:S(2)}) collective-permute-start(f32[160,128]{1,0:T(8,128)S(1)} %merge.2.refs_0_), channel_id=1, source_target_pairs={{0,3},{1,2},{2,1},{3,0},{4,7},{5,6},{6,5},{7,4},{8,11},{9,10},{10,... | collective-permute-start | bytes 245768 | tf_op jit(solution)/shard_map/ppermute | solution.py:341
  109.5 1.6 %collective-permute-start.28 = (f32[64,3584]{1,0:T(8,128)S(1)}, f32[64,3584]{1,0:T(8,128)S(1)}, u32[]{:S(2)}, u32[]{:S(2)}) collective-permute-start(f32[64,3584]{1,0:T(8,128)S(1)} %term.4), channel_id=1, source_target_pairs={{0,16},{4,12},{8,24},{12,4},{16,0},{20,28},{24,8},{28,20},{1,17},{... | collective-permute-start | bytes 2752520 | tf_op jit(solution)/shard_map/ppermute | solution.py:340
  111.2 5.6 %collective-permute-done.26.refs_2_ = f32[160,128]{1,0:T(8,128)S(1)} collective-permute-done((f32[160,128]{1,0:T(8,128)S(1)}, f32[160,128]{1,0:T(8,128)S(1)}, u32[]{:S(2)}, u32[]{:S(2)}) %collective-permute-start.26) | collective-permute-done | bytes 81952 | tf_op jit(solution)/shard_map/ppermute | solution.py:341
  116.7 3.2 %term.5 = (f32[64,3584]{1,0:T(8,128)S(1)}, f32[64,3584]{1,0:T(8,128)S(1)}) custom-call(f32[160,128]{1,0:T(8,128)S(1)} %merge.2.refs_0_, f32[160,128]{1,0:T(8,128)S(1)} %collective-permute-done.25.refs_1_, f32[160,128]{1,0:T(8,128)S(1)} %collective-permute-done.26.refs_2_, f32[160,128]{1,0:T(8,128)S(1)} %collective-permute-done.27.refs_3_, ...), custom_call_target="tpu_custom_call" | custom-call | tf_op jit(solution)/shard_map/term/pallas_call | solution.py:255
  120.1 5.1 %collective-permute-done.28.refs_0_.refs_1_ = f32[64,3584]{1,0:T(8,128)S(1)} collective-permute-done((f32[64,3584]{1,0:T(8,128)S(1)}, f32[64,3584]{1,0:T(8,128)S(1)}, u32[]{:S(2)}, u32[]{:S(2)}) %collective-permute-start.28) | collective-permute-done | bytes 917536 | tf_op jit(solution)/shard_map/ppermute | solution.py:340
  125.2 1.3 %join.1 = f32[64,7168]{1,0:T(8,128)} custom-call(f32[64,3584]{1,0:T(8,128)S(1)} %get-tuple-element.119.refs_0_, f32[64,3584]{1,0:T(8,128)S(1)} %collective-permute-done.28.refs_0_.refs_1_, f32[64,3584]{1,0:T(8,128)S(1)} %collective-permute-done.29.refs_2_, f32[64,3584]{1,0:T(8,128)S(1)} %collective-permute-done.30.refs_0_.refs_3_, f32[8,128]{1,0:T(8,128)S(1)} %arrived.3.refs_4_), custom_call_target="tpu_custom_call" | custom-call | tf_op jit(solution)/shard_map/join/pallas_call | solution.py:319
  (33 shorter events, 1.5 us)
Async XLA Ops:
  0.0 1.5 %copy-start.1 = (f32[7168,64]{0,1:T(8,128)S(1)}, f32[7168,64]{0,1:T(8,128)}, u32[]{:S(2)}) copy-start(f32[7168,64]{0,1:T(8,128)} %param.3) | copy-start | bytes 5505028
  1.7 6.4 %collective-permute-start.4 = (f32[64,3584]{1,0:T(8,128)S(1)}, f32[64,3584]{1,0:T(8,128)S(1)}, u32[]{:S(2)}, u32[]{:S(2)}) collective-permute-start(f32[64,3584]{1,0:T(8,128)S(1)} %get-tuple-element.68), channel_id=1, source_target_pairs={{0,4},{4,0},{8,12},{12,8},{16,20},{20,16},{24,28},{28,24},{1,5},{5... | collective-permute-start | bytes 2752520 | tf_op jit(solution)/shard_map/ppermute | solution.py:340
  2.2 23.3 %collective-permute-start.5 = (f32[64,3584]{1,0:T(8,128)S(1)}, f32[64,3584]{1,0:T(8,128)S(1)}, u32[]{:S(2)}, u32[]{:S(2)}) collective-permute-start(f32[64,3584]{1,0:T(8,128)S(1)} %get-tuple-element.67.refs_0_), channel_id=1, source_target_pairs={{0,16},{4,12},{8,24},{12,4},{16,0},{20,28},{24,8},{28,20},{1,17},{... | collective-permute-start | bytes 2752520 | tf_op jit(solution)/shard_map/ppermute | solution.py:340
  4.8 21.2 %collective-permute-start.6 = (f32[64,3584]{1,0:T(8,128)S(1)}, f32[64,3584]{1,0:T(8,128)S(1)}, u32[]{:S(2)}, u32[]{:S(2)}) collective-permute-start(f32[64,3584]{1,0:T(8,128)S(1)} %get-tuple-element.68), channel_id=1, source_target_pairs={{0,12},{4,16},{8,4},{12,24},{16,28},{20,0},{24,20},{28,8},{1,13},{... | collective-permute-start | bytes 2752520 | tf_op jit(solution)/shard_map/ppermute | solution.py:340
  4.8 2.3 %copy-start = (f32[160,7168]{1,0:T(8,128)S(1)}, f32[160,7168]{1,0:T(8,128)}, u32[]{:S(2)}) copy-start(f32[160,7168]{1,0:T(8,128)} %source.1) | copy-start | bytes 13762564
  7.5 20.4 %collective-permute-start.3 = (f32[64,3584]{1,0:T(8,128)S(1)}, f32[64,3584]{1,0:T(8,128)S(1)}, u32[]{:S(2)}, u32[]{:S(2)}) collective-permute-start(f32[64,3584]{1,0:T(8,128)S(1)} %get-tuple-element.66), channel_id=1, source_target_pairs={{0,4},{4,0},{8,12},{12,8},{16,20},{20,16},{24,28},{28,24},{1,5},{5... | collective-permute-start | bytes 2752520 | tf_op jit(solution)/shard_map/ppermute | solution.py:340
  7.7 23.0 %collective-permute-start.2 = (f32[96,3584]{1,0:T(8,128)S(1)}, f32[96,3584]{1,0:T(8,128)S(1)}, u32[]{:S(2)}, u32[]{:S(2)}) collective-permute-start(f32[96,3584]{1,0:T(8,128)S(1)} %get-tuple-element.64), channel_id=1, source_target_pairs={{0,4},{4,0},{8,12},{12,8},{16,20},{20,16},{24,28},{28,24},{1,5},{5... | collective-permute-start | bytes 4128776 | tf_op jit(solution)/shard_map/ppermute | solution.py:340
  8.1 44.3 %collective-permute-start = (f32[96,3584]{1,0:T(8,128)S(1)}, f32[96,3584]{1,0:T(8,128)S(1)}, u32[]{:S(2)}, u32[]{:S(2)}) collective-permute-start(f32[96,3584]{1,0:T(8,128)S(1)} %get-tuple-element.63.refs_0_), channel_id=1, source_target_pairs={{0,8},{4,20},{8,0},{12,28},{16,24},{20,4},{24,16},{28,12},{1,9},{5... | collective-permute-start | bytes 4128776 | tf_op jit(solution)/shard_map/ppermute | solution.py:340
  25.5 32.5 %collective-permute-start.1 = (f32[96,3584]{1,0:T(8,128)S(1)}, f32[96,3584]{1,0:T(8,128)S(1)}, u32[]{:S(2)}, u32[]{:S(2)}) collective-permute-start(f32[96,3584]{1,0:T(8,128)S(1)} %get-tuple-element.64), channel_id=1, source_target_pairs={{0,20},{4,8},{8,28},{12,0},{16,4},{20,24},{24,12},{28,16},{1,21},{... | collective-permute-start | bytes 4128776 | tf_op jit(solution)/shard_map/ppermute | solution.py:340
  26.0 46.1 %collective-permute-start.10 = (f32[64,3584]{1,0:T(8,128)S(1)}, f32[64,3584]{1,0:T(8,128)S(1)}, u32[]{:S(2)}, u32[]{:S(2)}) collective-permute-start(f32[64,3584]{1,0:T(8,128)S(1)} %get-tuple-element.65.refs_2_), channel_id=1, source_target_pairs={{0,8},{4,20},{8,0},{12,28},{16,24},{20,4},{24,16},{28,12},{1,9},{5... | collective-permute-start | bytes 2752520 | tf_op jit(solution)/shard_map/ppermute | solution.py:340
  28.0 46.9 %collective-permute-start.11 = (f32[64,3584]{1,0:T(8,128)S(1)}, f32[64,3584]{1,0:T(8,128)S(1)}, u32[]{:S(2)}, u32[]{:S(2)}) collective-permute-start(f32[64,3584]{1,0:T(8,128)S(1)} %get-tuple-element.66), channel_id=1, source_target_pairs={{0,20},{4,8},{8,28},{12,0},{16,4},{20,24},{24,12},{28,16},{1,21},{... | collective-permute-start | bytes 2752520 | tf_op jit(solution)/shard_map/ppermute | solution.py:340
  33.6 26.0 %collective-permute-start.7 = (f32[80,256]{1,0:T(8,128)S(1)}, f32[80,256]{1,0:T(8,128)S(1)}, u32[]{:S(2)}, u32[]{:S(2)}) collective-permute-start(f32[80,256]{1,0:T(8,128)S(1)} %get-tuple-element.70), channel_id=1, source_target_pairs={{0,2},{1,3},{2,0},{3,1},{4,6},{5,7},{6,4},{7,5},{8,10},{9,11},{10,... | collective-permute-start | bytes 245768 | tf_op jit(solution)/shard_map/ppermute | solution.py:341
  52.4 7.3 %collective-permute-start.8 = (f32[80,256]{1,0:T(8,128)S(1)}, f32[80,256]{1,0:T(8,128)S(1)}, u32[]{:S(2)}, u32[]{:S(2)}) collective-permute-start(f32[80,256]{1,0:T(8,128)S(1)} %get-tuple-element.71), channel_id=1, source_target_pairs={{0,3},{1,2},{2,1},{3,0},{4,7},{5,6},{6,5},{7,4},{8,11},{9,10},{10,... | collective-permute-start | bytes 245768 | tf_op jit(solution)/shard_map/ppermute | solution.py:341
  58.0 5.1 %collective-permute-start.9 = (f32[80,256]{1,0:T(8,128)S(1)}, f32[80,256]{1,0:T(8,128)S(1)}, u32[]{:S(2)}, u32[]{:S(2)}) collective-permute-start(f32[80,256]{1,0:T(8,128)S(1)} %get-tuple-element.72), channel_id=1, source_target_pairs={{0,1},{1,0},{2,3},{3,2},{4,5},{5,4},{6,7},{7,6},{8,9},{9,8},{10,11... | collective-permute-start | bytes 245768 | tf_op jit(solution)/shard_map/ppermute | solution.py:341
  65.1 9.7 %collective-permute-start.12 = (f32[48,256]{1,0:T(8,128)S(1)}, f32[48,256]{1,0:T(8,128)S(1)}, u32[]{:S(2)}, u32[]{:S(2)}) collective-permute-start(f32[48,256]{1,0:T(8,128)S(1)} %get-tuple-element.80), channel_id=1, source_target_pairs={{0,2},{1,3},{2,0},{3,1},{4,6},{5,7},{6,4},{7,5},{8,10},{9,11},{10,... | collective-permute-start | bytes 147464 | tf_op jit(solution)/shard_map/ppermute | solution.py:341
  67.9 7.0 %collective-permute-start.13 = (f32[48,256]{1,0:T(8,128)S(1)}, f32[48,256]{1,0:T(8,128)S(1)}, u32[]{:S(2)}, u32[]{:S(2)}) collective-permute-start(f32[48,256]{1,0:T(8,128)S(1)} %get-tuple-element.81), channel_id=1, source_target_pairs={{0,3},{1,2},{2,1},{3,0},{4,7},{5,6},{6,5},{7,4},{8,11},{9,10},{10,... | collective-permute-start | bytes 147464 | tf_op jit(solution)/shard_map/ppermute | solution.py:341
  69.3 5.6 %collective-permute-start.14 = (f32[48,256]{1,0:T(8,128)S(1)}, f32[48,256]{1,0:T(8,128)S(1)}, u32[]{:S(2)}, u32[]{:S(2)}) collective-permute-start(f32[48,256]{1,0:T(8,128)S(1)} %get-tuple-element.82), channel_id=1, source_target_pairs={{0,1},{1,0},{2,3},{3,2},{4,5},{5,4},{6,7},{7,6},{8,9},{9,8},{10,11... | collective-permute-start | bytes 147464 | tf_op jit(solution)/shard_map/ppermute | solution.py:341
  76.4 4.9 %collective-permute-start.15 = (f32[32,256]{1,0:T(8,128)S(1)}, f32[32,256]{1,0:T(8,128)S(1)}, u32[]{:S(2)}, u32[]{:S(2)}) collective-permute-start(f32[32,256]{1,0:T(8,128)S(1)} %get-tuple-element.90), channel_id=1, source_target_pairs={{0,2},{1,3},{2,0},{3,1},{4,6},{5,7},{6,4},{7,5},{8,10},{9,11},{10,... | collective-permute-start | bytes 98312 | tf_op jit(solution)/shard_map/ppermute | solution.py:341
  79.3 5.7 %collective-permute-start.16 = (f32[32,256]{1,0:T(8,128)S(1)}, f32[32,256]{1,0:T(8,128)S(1)}, u32[]{:S(2)}, u32[]{:S(2)}) collective-permute-start(f32[32,256]{1,0:T(8,128)S(1)} %get-tuple-element.91), channel_id=1, source_target_pairs={{0,3},{1,2},{2,1},{3,0},{4,7},{5,6},{6,5},{7,4},{8,11},{9,10},{10,... | collective-permute-start | bytes 98312 | tf_op jit(solution)/shard_map/ppermute | solution.py:341
  80.6 4.4 %collective-permute-start.17 = (f32[32,256]{1,0:T(8,128)S(1)}, f32[32,256]{1,0:T(8,128)S(1)}, u32[]{:S(2)}, u32[]{:S(2)}) collective-permute-start(f32[32,256]{1,0:T(8,128)S(1)} %get-tuple-element.92), channel_id=1, source_target_pairs={{0,1},{1,0},{2,3},{3,2},{4,5},{5,4},{6,7},{7,6},{8,9},{9,8},{10,11... | collective-permute-start | bytes 98312 | tf_op jit(solution)/shard_map/ppermute | solution.py:341
  85.1 3.5 %collective-permute-start.20 = (f32[80,128]{1,0:T(8,128)S(1)}, f32[80,128]{1,0:T(8,128)S(1)}, u32[]{:S(2)}, u32[]{:S(2)}) collective-permute-start(f32[80,128]{1,0:T(8,128)S(1)} %get-tuple-element.96), channel_id=1, source_target_pairs={{0,12},{4,16},{8,4},{12,24},{16,28},{20,0},{24,20},{28,8},{1,13},{... | collective-permute-start | bytes 122888 | tf_op jit(solution)/shard_map/ppermute | solution.py:340
  85.2 4.8 %collective-permute-start.21 = (f32[80,128]{1,0:T(8,128)S(1)}, f32[80,128]{1,0:T(8,128)S(1)}, u32[]{:S(2)}, u32[]{:S(2)}) collective-permute-start(f32[80,128]{1,0:T(8,128)S(1)} %get-tuple-element.97), channel_id=1, source_target_pairs={{0,28},{4,24},{8,20},{12,16},{16,12},{20,8},{24,4},{28,0},{1,29},{... | collective-permute-start | bytes 122888 | tf_op jit(solution)/shard_map/ppermute | solution.py:340
  90.0 8.2 %collective-permute-start.22 = (f32[160,128]{1,0:T(8,128)S(1)}, f32[160,128]{1,0:T(8,128)S(1)}, u32[]{:S(2)}, u32[]{:S(2)}) collective-permute-start(f32[160,128]{1,0:T(8,128)S(1)} %merge.3.refs_0_), channel_id=1, source_target_pairs={{0,1},{1,0},{2,3},{3,2},{4,5},{5,4},{6,7},{7,6},{8,9},{9,8},{10,11... | collective-permute-start | bytes 245768 | tf_op jit(solution)/shard_map/ppermute | solution.py:341
  90.1 8.1 %collective-permute-start.23 = (f32[160,128]{1,0:T(8,128)S(1)}, f32[160,128]{1,0:T(8,128)S(1)}, u32[]{:S(2)}, u32[]{:S(2)}) collective-permute-start(f32[160,128]{1,0:T(8,128)S(1)} %merge.3.refs_0_), channel_id=1, source_target_pairs={{0,2},{1,3},{2,0},{3,1},{4,6},{5,7},{6,4},{7,5},{8,10},{9,11},{10,... | collective-permute-start | bytes 245768 | tf_op jit(solution)/shard_map/ppermute | solution.py:341
  92.7 7.1 %collective-permute-start.24 = (f32[160,128]{1,0:T(8,128)S(1)}, f32[160,128]{1,0:T(8,128)S(1)}, u32[]{:S(2)}, u32[]{:S(2)}) collective-permute-start(f32[160,128]{1,0:T(8,128)S(1)} %merge.3.refs_0_), channel_id=1, source_target_pairs={{0,3},{1,2},{2,1},{3,0},{4,7},{5,6},{6,5},{7,4},{8,11},{9,10},{10,... | collective-permute-start | bytes 245768 | tf_op jit(solution)/shard_map/ppermute | solution.py:341
  94.5 1.2 collective-permute-start.18
  94.8 3.4 %collective-permute-start.19 = (f32[80,128]{1,0:T(8,128)S(1)}, f32[80,128]{1,0:T(8,128)S(1)}, u32[]{:S(2)}, u32[]{:S(2)}) collective-permute-start(f32[80,128]{1,0:T(8,128)S(1)} %get-tuple-element.95), channel_id=1, source_target_pairs={{0,20},{4,8},{8,28},{12,0},{16,4},{20,24},{24,12},{28,16},{1,21},{... | collective-permute-start | bytes 122888 | tf_op jit(solution)/shard_map/ppermute | solution.py:340
  102.2 17.8 %collective-permute-start.30 = (f32[64,3584]{1,0:T(8,128)S(1)}, f32[64,3584]{1,0:T(8,128)S(1)}, u32[]{:S(2)}, u32[]{:S(2)}) collective-permute-start(f32[64,3584]{1,0:T(8,128)S(1)} %term.3), channel_id=1, source_target_pairs={{0,20},{4,8},{8,28},{12,0},{16,4},{20,24},{24,12},{28,16},{1,21},{... | collective-permute-start | bytes 2752520 | tf_op jit(solution)/shard_map/ppermute | solution.py:340
  104.7 6.5 %collective-permute-start.25 = (f32[160,128]{1,0:T(8,128)S(1)}, f32[160,128]{1,0:T(8,128)S(1)}, u32[]{:S(2)}, u32[]{:S(2)}) collective-permute-start(f32[160,128]{1,0:T(8,128)S(1)} %merge.2.refs_0_), channel_id=1, source_target_pairs={{0,1},{1,0},{2,3},{3,2},{4,5},{5,4},{6,7},{7,6},{8,9},{9,8},{10,11... | collective-permute-start | bytes 245768 | tf_op jit(solution)/shard_map/ppermute | solution.py:341
  107.1 9.6 %collective-permute-start.26 = (f32[160,128]{1,0:T(8,128)S(1)}, f32[160,128]{1,0:T(8,128)S(1)}, u32[]{:S(2)}, u32[]{:S(2)}) collective-permute-start(f32[160,128]{1,0:T(8,128)S(1)} %merge.2.refs_0_), channel_id=1, source_target_pairs={{0,2},{1,3},{2,0},{3,1},{4,6},{5,7},{6,4},{7,5},{8,10},{9,11},{10,... | collective-permute-start | bytes 245768 | tf_op jit(solution)/shard_map/ppermute | solution.py:341
  108.1 8.6 %collective-permute-start.27 = (f32[160,128]{1,0:T(8,128)S(1)}, f32[160,128]{1,0:T(8,128)S(1)}, u32[]{:S(2)}, u32[]{:S(2)}) collective-permute-start(f32[160,128]{1,0:T(8,128)S(1)} %merge.2.refs_0_), channel_id=1, source_target_pairs={{0,3},{1,2},{2,1},{3,0},{4,7},{5,6},{6,5},{7,4},{8,11},{9,10},{10,... | collective-permute-start | bytes 245768 | tf_op jit(solution)/shard_map/ppermute | solution.py:341
  109.5 15.6 %collective-permute-start.28 = (f32[64,3584]{1,0:T(8,128)S(1)}, f32[64,3584]{1,0:T(8,128)S(1)}, u32[]{:S(2)}, u32[]{:S(2)}) collective-permute-start(f32[64,3584]{1,0:T(8,128)S(1)} %term.4), channel_id=1, source_target_pairs={{0,16},{4,12},{8,24},{12,4},{16,0},{20,28},{24,8},{28,20},{1,17},{... | collective-permute-start | bytes 2752520 | tf_op jit(solution)/shard_map/ppermute | solution.py:340
  120.0 5.2 %collective-permute-start.29 = (f32[64,3584]{1,0:T(8,128)S(1)}, f32[64,3584]{1,0:T(8,128)S(1)}, u32[]{:S(2)}, u32[]{:S(2)}) collective-permute-start(f32[64,3584]{1,0:T(8,128)S(1)} %get-tuple-element.120), channel_id=1, source_target_pairs={{0,4},{4,0},{8,12},{12,8},{16,20},{20,16},{24,28},{28,24},{1,5},{5... | collective-permute-start | bytes 2752520 | tf_op jit(solution)/shard_map/ppermute | solution.py:340

commit v6 on v5

--- a/solution.py
+++ b/solution.py
@@ -110,7 +110,7 @@
     half = inputs[0].shape[1]
     width = acc.shape[1]
     z = lax.axis_index("feat")
-    step = block_of(half, 1024)
+    step = block_of(half, 4096)
     acc[...] = jnp.zeros(acc.shape, jnp.float32)
 
     @pl.loop(0, half // step)
@@ -233,7 +233,7 @@
                 full[pl.ds(to + (z ^ s) * part, part)] = pieces[s][at : at + part, left : left + columns]
     h, l = split(full[...].T)
     both = jnp.concatenate([h, l], 0)
-    step = block_of(size, 896)
+    step = block_of(size, 4096)
 
     @pl.loop(0, size // step)
     def _(i):

time: 127 us -> 126 us (level)
  Pallas kernels: 17.7 us -> 13.6 us
  waiting for transfers between devices: 63.8 us -> 66.7 us
    ppermute x16, waiting for transfers between devices: 49 us -> 52 us  [shards(): send = lambda x, pairs: lax.ppermute(x, 'tok', pairs)]
    pallas_call x3, Pallas kernels: 6.36 us -> 4.17 us  [mix(): pl.pallas_call(functools.partial(mix_kernel, count, zs), out_shape=[piece...]
    pallas_call x3, Pallas kernels: 7.86 us -> 5.95 us  [terms(): pl.pallas_call(functools.partial(term_kernel, zs, spots, len(acts), left)...]
  transfers between devices with their start and end apart: 31 -> 31, of which waited for: 15 -> 15; matrix products, arithmetic and copies ran while one was open for 0% -> 0% of each run, Pallas kernels for 10% -> 7%
where the time goes in v6:
time: 126 us; the launch traced here: 125 us
  waiting for transfers between devices  66.7 us (53%)
  starting transfers between devices  41.1 us (33%)
  Pallas kernels  13.6 us (11%)
  local copies, waits for them, and re-layouts  3.8 us (3%)
    ppermute x16, waiting for transfers between devices, shards(): send = lambda x, pairs: lax.ppermute(x, 'tok', pairs)  52 us
    ppermute x15, starting transfers between devices, shards(): lax.ppermute(x, 'feat', [(i, i ^ s) for i in range(zs)])  26.6 us
    ppermute x15, waiting for transfers between devices, shards(): lax.ppermute(x, 'feat', [(i, i ^ s) for i in range(zs)])  14.7 us
    ppermute x16, starting transfers between devices, shards(): send = lambda x, pairs: lax.ppermute(x, 'tok', pairs)  14.4 us
    pallas_call x3, Pallas kernels, terms(): pl.pallas_call(functools.partial(term_kernel, zs, spots, len(acts), left)...  5.95 us
    pallas_call x3, Pallas kernels, mix(): pl.pallas_call(functools.partial(mix_kernel, count, zs), out_shape=[piece...  4.17 us
    unnamed x4, local copies, waits for them, and re-layouts  3.8 us
  transfers between devices with their start and end apart: 31, of which 15 were waited for; matrix products, arithmetic and copies ran while one was open for 0% of the time, Pallas kernels for 7%

profile of v6, /device:TPU:0, one launch (start us, length us, event | category | flops | bytes accessed | tf_op | source)
XLA Modules:
  0.0 125.4 jit_solution(280424781530217564)
XLA Ops:
  0.0 1.5 %copy-done.1 = f32[7168,64]{0,1:T(8,128)S(1)} copy-done((f32[7168,64]{0,1:T(8,128)S(1)}, f32[7168,64]{0,1:T(8,128)}, u32[]{:S(2)}) %copy-start.1) | copy-done | bytes 1835032
  1.7 0.5 collective-permute-start.4
  2.2 2.6 %collective-permute-start.5 = (f32[64,3584]{1,0:T(8,128)S(1)}, f32[64,3584]{1,0:T(8,128)S(1)}, u32[]{:S(2)}, u32[]{:S(2)}) collective-permute-start(f32[64,3584]{1,0:T(8,128)S(1)} %get-tuple-element.67.refs_0_), channel_id=1, source_target_pairs={{0,16},{4,12},{8,24},{12,4},{16,0},{20,28},{24,8},{28,20},{1,17},{... | collective-permute-start | bytes 2752520 | tf_op jit(solution)/shard_map/ppermute | solution.py:340
  4.8 2.3 %copy-done = f32[160,7168]{1,0:T(8,128)S(1)} copy-done((f32[160,7168]{1,0:T(8,128)S(1)}, f32[160,7168]{1,0:T(8,128)}, u32[]{:S(2)}) %copy-start) | copy-done | bytes 4587544
  7.1 0.4 cut.2
  7.7 0.4 collective-permute-start.2
  8.1 1.7 %collective-permute-start = (f32[96,3584]{1,0:T(8,128)S(1)}, f32[96,3584]{1,0:T(8,128)S(1)}, u32[]{:S(2)}, u32[]{:S(2)}) collective-permute-start(f32[96,3584]{1,0:T(8,128)S(1)} %get-tuple-element.63.refs_0_), channel_id=1, source_target_pairs={{0,8},{4,20},{8,0},{12,28},{16,24},{20,4},{24,16},{28,12},{1,9},{5... | collective-permute-start | bytes 4128776 | tf_op jit(solution)/shard_map/ppermute | solution.py:340
  9.8 15.6 %collective-permute-done.5.refs_2_ = f32[64,3584]{1,0:T(8,128)S(1)} collective-permute-done((f32[64,3584]{1,0:T(8,128)S(1)}, f32[64,3584]{1,0:T(8,128)S(1)}, u32[]{:S(2)}, u32[]{:S(2)}) %collective-permute-start.5) | collective-permute-done | bytes 917536 | tf_op jit(solution)/shard_map/ppermute | solution.py:340
  25.5 0.5 collective-permute-done.6.refs_3_
  26.0 2.0 %collective-permute-start.10 = (f32[64,3584]{1,0:T(8,128)S(1)}, f32[64,3584]{1,0:T(8,128)S(1)}, u32[]{:S(2)}, u32[]{:S(2)}) collective-permute-start(f32[64,3584]{1,0:T(8,128)S(1)} %get-tuple-element.65.refs_2_), channel_id=1, source_target_pairs={{0,8},{4,20},{8,0},{12,28},{16,24},{20,4},{24,16},{28,12},{1,9},{5... | collective-permute-start | bytes 2752520 | tf_op jit(solution)/shard_map/ppermute | solution.py:340
  28.0 1.3 %collective-permute-start.11 = (f32[64,3584]{1,0:T(8,128)S(1)}, f32[64,3584]{1,0:T(8,128)S(1)}, u32[]{:S(2)}, u32[]{:S(2)}) collective-permute-start(f32[64,3584]{1,0:T(8,128)S(1)} %get-tuple-element.66), channel_id=1, source_target_pairs={{0,20},{4,8},{8,28},{12,0},{16,4},{20,24},{24,12},{28,16},{1,21},{... | collective-permute-start | bytes 2752520 | tf_op jit(solution)/shard_map/ppermute | solution.py:340
  29.3 1.4 %turn.1.refs_4_.refs_2_ = bf16[3584,512]{1,0:T(8,128)(2,1)S(1)} custom-call(f32[64,3584]{1,0:T(8,128)S(1)} %get-tuple-element.67.refs_0_, f32[64,3584]{1,0:T(8,128)S(1)} %collective-permute-done.4.refs_1_, f32[64,3584]{1,0:T(8,128)S(1)} %collective-permute-done.5.refs_2_, f32[64,3584]{1,0:T(8,128)S(1)} %collective-permute-done.6.refs_3_), custom_call_target="tpu_custom_call" | custom-call | tf_op jit(solution)/shard_map/turn/pallas_call | solution.py:97
  30.7 2.0 %mix.3 = (f32[80,256]{1,0:T(8,128)S(1)}, f32[80,256]{1,0:T(8,128)S(1)}, f32[80,256]{1,0:T(8,128)S(1)}, f32[80,256]{1,0:T(8,128)S(1)}, bf16[320,3584]{1,0:T(8,128)(2,1)S(1)}, /*index=5*/bf16[320,3584]{1,0:T(8,128)(2,1)S(1)}) custom-call(f32[96,3584]{1,0:T(8,128)S(1)} %get-tuple-element.63.refs_0_, f32[96,3584]{1,0:T(8,128)S(1)} %collective-permute-done.2.refs_1_, ...), custom_call_target="tpu_custom_call" | custom-call | flops 1761607680 | bytes 12845056 | tf_op jit(solution)/shard_map/mix/pallas_call | solution.py:139
  32.7 2.7 %collective-permute-start.7 = (f32[80,256]{1,0:T(8,128)S(1)}, f32[80,256]{1,0:T(8,128)S(1)}, u32[]{:S(2)}, u32[]{:S(2)}) collective-permute-start(f32[80,256]{1,0:T(8,128)S(1)} %get-tuple-element.70), channel_id=1, source_target_pairs={{0,2},{1,3},{2,0},{3,1},{4,6},{5,7},{6,4},{7,5},{8,10},{9,11},{10,... | collective-permute-start | bytes 245768 | tf_op jit(solution)/shard_map/ppermute | solution.py:341
  35.4 17.0 %collective-permute-done.refs_0_ = f32[96,3584]{1,0:T(8,128)S(1)} collective-permute-done((f32[96,3584]{1,0:T(8,128)S(1)}, f32[96,3584]{1,0:T(8,128)S(1)}, u32[]{:S(2)}, u32[]{:S(2)}) %collective-permute-start) | collective-permute-done | bytes 1376288 | tf_op jit(solution)/shard_map/ppermute | solution.py:340
  52.4 4.0 %collective-permute-start.8 = (f32[80,256]{1,0:T(8,128)S(1)}, f32[80,256]{1,0:T(8,128)S(1)}, u32[]{:S(2)}, u32[]{:S(2)}) collective-permute-start(f32[80,256]{1,0:T(8,128)S(1)} %get-tuple-element.71), channel_id=1, source_target_pairs={{0,3},{1,2},{2,1},{3,0},{4,7},{5,6},{6,5},{7,4},{8,11},{9,10},{10,... | collective-permute-start | bytes 245768 | tf_op jit(solution)/shard_map/ppermute | solution.py:341
  56.4 1.6 %collective-permute-done.1.refs_1_ = f32[96,3584]{1,0:T(8,128)S(1)} collective-permute-done((f32[96,3584]{1,0:T(8,128)S(1)}, f32[96,3584]{1,0:T(8,128)S(1)}, u32[]{:S(2)}, u32[]{:S(2)}) %collective-permute-start.1) | collective-permute-done | bytes 1376288 | tf_op jit(solution)/shard_map/ppermute | solution.py:340
  58.0 1.7 %collective-permute-start.9 = (f32[80,256]{1,0:T(8,128)S(1)}, f32[80,256]{1,0:T(8,128)S(1)}, u32[]{:S(2)}, u32[]{:S(2)}) collective-permute-start(f32[80,256]{1,0:T(8,128)S(1)} %get-tuple-element.72), channel_id=1, source_target_pairs={{0,1},{1,0},{2,3},{3,2},{4,5},{5,4},{6,7},{7,6},{8,9},{9,8},{10,11... | collective-permute-start | bytes 245768 | tf_op jit(solution)/shard_map/ppermute | solution.py:341
  59.7 3.4 %collective-permute-done.9.refs_3_ = f32[80,256]{1,0:T(8,128)S(1)} collective-permute-done((f32[80,256]{1,0:T(8,128)S(1)}, f32[80,256]{1,0:T(8,128)S(1)}, u32[]{:S(2)}, u32[]{:S(2)}) %collective-permute-start.9) | collective-permute-done | bytes 81952 | tf_op jit(solution)/shard_map/ppermute | solution.py:341
  63.1 1.3 %mix.4 = (f32[48,256]{1,0:T(8,128)S(1)}, f32[48,256]{1,0:T(8,128)S(1)}, f32[48,256]{1,0:T(8,128)S(1)}, f32[48,256]{1,0:T(8,128)S(1)}, bf16[192,3584]{1,0:T(8,128)(2,1)S(1)}, /*index=5*/bf16[192,3584]{1,0:T(8,128)(2,1)S(1)}) custom-call(f32[96,3584]{1,0:T(8,128)S(1)} %collective-permute-done.refs_0_, f32[96,3584]{1,0:T(8,128)S(1)} %collective-permute-done.1.refs_1_, ...), custom_call_target="tpu_custom_call" | custom-call | flops 1056964608 | bytes 9175040 | tf_op jit(solution)/shard_map/mix/pallas_call | solution.py:139
  64.4 2.8 %collective-permute-start.12 = (f32[48,256]{1,0:T(8,128)S(1)}, f32[48,256]{1,0:T(8,128)S(1)}, u32[]{:S(2)}, u32[]{:S(2)}) collective-permute-start(f32[48,256]{1,0:T(8,128)S(1)} %get-tuple-element.80), channel_id=1, source_target_pairs={{0,2},{1,3},{2,0},{3,1},{4,6},{5,7},{6,4},{7,5},{8,10},{9,11},{10,... | collective-permute-start | bytes 147464 | tf_op jit(solution)/shard_map/ppermute | solution.py:341
  67.2 1.3 %collective-permute-start.13 = (f32[48,256]{1,0:T(8,128)S(1)}, f32[48,256]{1,0:T(8,128)S(1)}, u32[]{:S(2)}, u32[]{:S(2)}) collective-permute-start(f32[48,256]{1,0:T(8,128)S(1)} %get-tuple-element.81), channel_id=1, source_target_pairs={{0,3},{1,2},{2,1},{3,0},{4,7},{5,6},{6,5},{7,4},{8,11},{9,10},{10,... | collective-permute-start | bytes 147464 | tf_op jit(solution)/shard_map/ppermute | solution.py:341
  68.8 3.3 %collective-permute-done.10.refs_0_ = f32[64,3584]{1,0:T(8,128)S(1)} collective-permute-done((f32[64,3584]{1,0:T(8,128)S(1)}, f32[64,3584]{1,0:T(8,128)S(1)}, u32[]{:S(2)}, u32[]{:S(2)}) %collective-permute-start.10) | collective-permute-done | bytes 917536 | tf_op jit(solution)/shard_map/ppermute | solution.py:340
  72.1 2.8 %collective-permute-done.11.refs_1_ = f32[64,3584]{1,0:T(8,128)S(1)} collective-permute-done((f32[64,3584]{1,0:T(8,128)S(1)}, f32[64,3584]{1,0:T(8,128)S(1)}, u32[]{:S(2)}, u32[]{:S(2)}) %collective-permute-start.11) | collective-permute-done | bytes 917536 | tf_op jit(solution)/shard_map/ppermute | solution.py:340
  74.9 0.9 mix.5
  75.8 2.9 %collective-permute-start.15 = (f32[32,256]{1,0:T(8,128)S(1)}, f32[32,256]{1,0:T(8,128)S(1)}, u32[]{:S(2)}, u32[]{:S(2)}) collective-permute-start(f32[32,256]{1,0:T(8,128)S(1)} %get-tuple-element.90), channel_id=1, source_target_pairs={{0,2},{1,3},{2,0},{3,1},{4,6},{5,7},{6,4},{7,5},{8,10},{9,11},{10,... | collective-permute-start | bytes 98312 | tf_op jit(solution)/shard_map/ppermute | solution.py:341
  78.7 1.4 %collective-permute-start.16 = (f32[32,256]{1,0:T(8,128)S(1)}, f32[32,256]{1,0:T(8,128)S(1)}, u32[]{:S(2)}, u32[]{:S(2)}) collective-permute-start(f32[32,256]{1,0:T(8,128)S(1)} %get-tuple-element.91), channel_id=1, source_target_pairs={{0,3},{1,2},{2,1},{3,0},{4,7},{5,6},{6,5},{7,4},{8,11},{9,10},{10,... | collective-permute-start | bytes 98312 | tf_op jit(solution)/shard_map/ppermute | solution.py:341
  80.3 0.4 collective-permute-done.15.refs_9_
  80.7 3.7 %collective-permute-done.16.refs_10_ = f32[32,256]{1,0:T(8,128)S(1)} collective-permute-done((f32[32,256]{1,0:T(8,128)S(1)}, f32[32,256]{1,0:T(8,128)S(1)}, u32[]{:S(2)}, u32[]{:S(2)}) %collective-permute-start.16) | collective-permute-done | bytes 32800 | tf_op jit(solution)/shard_map/ppermute | solution.py:341
  84.6 2.6 %collective-permute-start.21 = (f32[80,128]{1,0:T(8,128)S(1)}, f32[80,128]{1,0:T(8,128)S(1)}, u32[]{:S(2)}, u32[]{:S(2)}) collective-permute-start(f32[80,128]{1,0:T(8,128)S(1)} %get-tuple-element.97), channel_id=1, source_target_pairs={{0,28},{4,24},{8,20},{12,16},{16,12},{20,8},{24,4},{28,0},{1,29},{... | collective-permute-start | bytes 122888 | tf_op jit(solution)/shard_map/ppermute | solution.py:340
  87.3 0.7 collective-permute-done.20.refs_1_
  88.0 1.4 %collective-permute-done.21.refs_2_ = f32[80,128]{1,0:T(8,128)S(1)} collective-permute-done((f32[80,128]{1,0:T(8,128)S(1)}, f32[80,128]{1,0:T(8,128)S(1)}, u32[]{:S(2)}, u32[]{:S(2)}) %collective-permute-start.21) | collective-permute-done | bytes 40992 | tf_op jit(solution)/shard_map/ppermute | solution.py:340
  89.5 2.6 %collective-permute-start.23 = (f32[160,128]{1,0:T(8,128)S(1)}, f32[160,128]{1,0:T(8,128)S(1)}, u32[]{:S(2)}, u32[]{:S(2)}) collective-permute-start(f32[160,128]{1,0:T(8,128)S(1)} %merge.3.refs_0_), channel_id=1, source_target_pairs={{0,2},{1,3},{2,0},{3,1},{4,6},{5,7},{6,4},{7,5},{8,10},{9,11},{10,... | collective-permute-start | bytes 245768 | tf_op jit(solution)/shard_map/ppermute | solution.py:341
  92.1 1.7 %collective-permute-start.24 = (f32[160,128]{1,0:T(8,128)S(1)}, f32[160,128]{1,0:T(8,128)S(1)}, u32[]{:S(2)}, u32[]{:S(2)}) collective-permute-start(f32[160,128]{1,0:T(8,128)S(1)} %merge.3.refs_0_), channel_id=1, source_target_pairs={{0,3},{1,2},{2,1},{3,0},{4,7},{5,6},{6,5},{7,4},{8,11},{9,10},{10,... | collective-permute-start | bytes 245768 | tf_op jit(solution)/shard_map/ppermute | solution.py:341
  93.9 0.3 collective-permute-start.18
  94.2 0.9 collective-permute-start.19
  95.1 2.5 %collective-permute-done.19.refs_2_ = f32[80,128]{1,0:T(8,128)S(1)} collective-permute-done((f32[80,128]{1,0:T(8,128)S(1)}, f32[80,128]{1,0:T(8,128)S(1)}, u32[]{:S(2)}, u32[]{:S(2)}) %collective-permute-start.19) | collective-permute-done | bytes 40992 | tf_op jit(solution)/shard_map/ppermute | solution.py:340
  97.6 1.6 %collective-permute-done.24.refs_3_ = f32[160,128]{1,0:T(8,128)S(1)} collective-permute-done((f32[160,128]{1,0:T(8,128)S(1)}, f32[160,128]{1,0:T(8,128)S(1)}, u32[]{:S(2)}, u32[]{:S(2)}) %collective-permute-start.24) | collective-permute-done | bytes 81952 | tf_op jit(solution)/shard_map/ppermute | solution.py:341
  99.2 1.9 %term.3 = f32[64,3584]{1,0:T(8,128)S(1)} custom-call(f32[160,128]{1,0:T(8,128)S(1)} %merge.3.refs_0_, f32[160,128]{1,0:T(8,128)S(1)} %collective-permute-done.22.refs_1_, f32[160,128]{1,0:T(8,128)S(1)} %collective-permute-done.23.refs_2_, f32[160,128]{1,0:T(8,128)S(1)} %collective-permute-done.24.refs_3_, bf16[320,3584]{1,0:T(8,128)(2,1)S(1)} %get-tuple-element.103.refs_4_, ...), custom_call_target="tpu_custom_call" | custom-call | tf_op jit(solution)/shard_map/term/pallas_call | solution.py:255
  101.2 1.7 %term.4 = f32[64,3584]{1,0:T(8,128)S(1)} custom-call(f32[160,128]{1,0:T(8,128)S(1)} %merge.3.refs_0_, f32[160,128]{1,0:T(8,128)S(1)} %collective-permute-done.22.refs_1_, f32[160,128]{1,0:T(8,128)S(1)} %collective-permute-done.23.refs_2_, f32[160,128]{1,0:T(8,128)S(1)} %collective-permute-done.24.refs_3_, bf16[320,3584]{1,0:T(8,128)(2,1)S(1)} %get-tuple-element.103.refs_4_, ...), custom_call_target="tpu_custom_call" | custom-call | tf_op jit(solution)/shard_map/term/pallas_call | solution.py:255
  102.9 2.5 %collective-permute-start.25 = (f32[160,128]{1,0:T(8,128)S(1)}, f32[160,128]{1,0:T(8,128)S(1)}, u32[]{:S(2)}, u32[]{:S(2)}) collective-permute-start(f32[160,128]{1,0:T(8,128)S(1)} %merge.2.refs_0_), channel_id=1, source_target_pairs={{0,1},{1,0},{2,3},{3,2},{4,5},{5,4},{6,7},{7,6},{8,9},{9,8},{10,11... | collective-permute-start | bytes 245768 | tf_op jit(solution)/shard_map/ppermute | solution.py:341
  105.4 1.1 collective-permute-start.26
  106.5 1.4 %collective-permute-start.27 = (f32[160,128]{1,0:T(8,128)S(1)}, f32[160,128]{1,0:T(8,128)S(1)}, u32[]{:S(2)}, u32[]{:S(2)}) collective-permute-start(f32[160,128]{1,0:T(8,128)S(1)} %merge.2.refs_0_), channel_id=1, source_target_pairs={{0,3},{1,2},{2,1},{3,0},{4,7},{5,6},{6,5},{7,4},{8,11},{9,10},{10,... | collective-permute-start | bytes 245768 | tf_op jit(solution)/shard_map/ppermute | solution.py:341
  107.9 1.6 %collective-permute-start.28 = (f32[64,3584]{1,0:T(8,128)S(1)}, f32[64,3584]{1,0:T(8,128)S(1)}, u32[]{:S(2)}, u32[]{:S(2)}) collective-permute-start(f32[64,3584]{1,0:T(8,128)S(1)} %term.4), channel_id=1, source_target_pairs={{0,16},{4,12},{8,24},{12,4},{16,0},{20,28},{24,8},{28,20},{1,17},{... | collective-permute-start | bytes 2752520 | tf_op jit(solution)/shard_map/ppermute | solution.py:340
  109.5 5.6 %collective-permute-done.26.refs_2_ = f32[160,128]{1,0:T(8,128)S(1)} collective-permute-done((f32[160,128]{1,0:T(8,128)S(1)}, f32[160,128]{1,0:T(8,128)S(1)}, u32[]{:S(2)}, u32[]{:S(2)}) %collective-permute-start.26) | collective-permute-done | bytes 81952 | tf_op jit(solution)/shard_map/ppermute | solution.py:341
  115.1 2.4 %term.5 = (f32[64,3584]{1,0:T(8,128)S(1)}, f32[64,3584]{1,0:T(8,128)S(1)}) custom-call(f32[160,128]{1,0:T(8,128)S(1)} %merge.2.refs_0_, f32[160,128]{1,0:T(8,128)S(1)} %collective-permute-done.25.refs_1_, f32[160,128]{1,0:T(8,128)S(1)} %collective-permute-done.26.refs_2_, f32[160,128]{1,0:T(8,128)S(1)} %collective-permute-done.27.refs_3_, ...), custom_call_target="tpu_custom_call" | custom-call | tf_op jit(solution)/shard_map/term/pallas_call | solution.py:255
  117.5 6.5 %collective-permute-done.28.refs_0_.refs_1_ = f32[64,3584]{1,0:T(8,128)S(1)} collective-permute-done((f32[64,3584]{1,0:T(8,128)S(1)}, f32[64,3584]{1,0:T(8,128)S(1)}, u32[]{:S(2)}, u32[]{:S(2)}) %collective-permute-start.28) | collective-permute-done | bytes 917536 | tf_op jit(solution)/shard_map/ppermute | solution.py:340
  124.1 1.3 %join.1 = f32[64,7168]{1,0:T(8,128)} custom-call(f32[64,3584]{1,0:T(8,128)S(1)} %get-tuple-element.119.refs_0_, f32[64,3584]{1,0:T(8,128)S(1)} %collective-permute-done.28.refs_0_.refs_1_, f32[64,3584]{1,0:T(8,128)S(1)} %collective-permute-done.29.refs_2_, f32[64,3584]{1,0:T(8,128)S(1)} %collective-permute-done.30.refs_0_.refs_3_, f32[8,128]{1,0:T(8,128)S(1)} %arrived.3.refs_4_), custom_call_target="tpu_custom_call" | custom-call | tf_op jit(solution)/shard_map/join/pallas_call | solution.py:319
  (33 shorter events, 1.4 us)
Async XLA Ops:
  0.0 1.5 %copy-start.1 = (f32[7168,64]{0,1:T(8,128)S(1)}, f32[7168,64]{0,1:T(8,128)}, u32[]{:S(2)}) copy-start(f32[7168,64]{0,1:T(8,128)} %param.3) | copy-start | bytes 5505028
  1.7 6.4 %collective-permute-start.4 = (f32[64,3584]{1,0:T(8,128)S(1)}, f32[64,3584]{1,0:T(8,128)S(1)}, u32[]{:S(2)}, u32[]{:S(2)}) collective-permute-start(f32[64,3584]{1,0:T(8,128)S(1)} %get-tuple-element.68), channel_id=1, source_target_pairs={{0,4},{4,0},{8,12},{12,8},{16,20},{20,16},{24,28},{28,24},{1,5},{5... | collective-permute-start | bytes 2752520 | tf_op jit(solution)/shard_map/ppermute | solution.py:340
  2.2 23.3 %collective-permute-start.5 = (f32[64,3584]{1,0:T(8,128)S(1)}, f32[64,3584]{1,0:T(8,128)S(1)}, u32[]{:S(2)}, u32[]{:S(2)}) collective-permute-start(f32[64,3584]{1,0:T(8,128)S(1)} %get-tuple-element.67.refs_0_), channel_id=1, source_target_pairs={{0,16},{4,12},{8,24},{12,4},{16,0},{20,28},{24,8},{28,20},{1,17},{... | collective-permute-start | bytes 2752520 | tf_op jit(solution)/shard_map/ppermute | solution.py:340
  4.8 21.2 %collective-permute-start.6 = (f32[64,3584]{1,0:T(8,128)S(1)}, f32[64,3584]{1,0:T(8,128)S(1)}, u32[]{:S(2)}, u32[]{:S(2)}) collective-permute-start(f32[64,3584]{1,0:T(8,128)S(1)} %get-tuple-element.68), channel_id=1, source_target_pairs={{0,12},{4,16},{8,4},{12,24},{16,28},{20,0},{24,20},{28,8},{1,13},{... | collective-permute-start | bytes 2752520 | tf_op jit(solution)/shard_map/ppermute | solution.py:340
  4.8 2.3 %copy-start = (f32[160,7168]{1,0:T(8,128)S(1)}, f32[160,7168]{1,0:T(8,128)}, u32[]{:S(2)}) copy-start(f32[160,7168]{1,0:T(8,128)} %source.1) | copy-start | bytes 13762564
  7.5 20.4 %collective-permute-start.3 = (f32[64,3584]{1,0:T(8,128)S(1)}, f32[64,3584]{1,0:T(8,128)S(1)}, u32[]{:S(2)}, u32[]{:S(2)}) collective-permute-start(f32[64,3584]{1,0:T(8,128)S(1)} %get-tuple-element.66), channel_id=1, source_target_pairs={{0,4},{4,0},{8,12},{12,8},{16,20},{20,16},{24,28},{28,24},{1,5},{5... | collective-permute-start | bytes 2752520 | tf_op jit(solution)/shard_map/ppermute | solution.py:340
  7.7 23.0 %collective-permute-start.2 = (f32[96,3584]{1,0:T(8,128)S(1)}, f32[96,3584]{1,0:T(8,128)S(1)}, u32[]{:S(2)}, u32[]{:S(2)}) collective-permute-start(f32[96,3584]{1,0:T(8,128)S(1)} %get-tuple-element.64), channel_id=1, source_target_pairs={{0,4},{4,0},{8,12},{12,8},{16,20},{20,16},{24,28},{28,24},{1,5},{5... | collective-permute-start | bytes 4128776 | tf_op jit(solution)/shard_map/ppermute | solution.py:340
  8.1 44.3 %collective-permute-start = (f32[96,3584]{1,0:T(8,128)S(1)}, f32[96,3584]{1,0:T(8,128)S(1)}, u32[]{:S(2)}, u32[]{:S(2)}) collective-permute-start(f32[96,3584]{1,0:T(8,128)S(1)} %get-tuple-element.63.refs_0_), channel_id=1, source_target_pairs={{0,8},{4,20},{8,0},{12,28},{16,24},{20,4},{24,16},{28,12},{1,9},{5... | collective-permute-start | bytes 4128776 | tf_op jit(solution)/shard_map/ppermute | solution.py:340
  25.5 32.5 %collective-permute-start.1 = (f32[96,3584]{1,0:T(8,128)S(1)}, f32[96,3584]{1,0:T(8,128)S(1)}, u32[]{:S(2)}, u32[]{:S(2)}) collective-permute-start(f32[96,3584]{1,0:T(8,128)S(1)} %get-tuple-element.64), channel_id=1, source_target_pairs={{0,20},{4,8},{8,28},{12,0},{16,4},{20,24},{24,12},{28,16},{1,21},{... | collective-permute-start | bytes 4128776 | tf_op jit(solution)/shard_map/ppermute | solution.py:340
  26.0 46.1 %collective-permute-start.10 = (f32[64,3584]{1,0:T(8,128)S(1)}, f32[64,3584]{1,0:T(8,128)S(1)}, u32[]{:S(2)}, u32[]{:S(2)}) collective-permute-start(f32[64,3584]{1,0:T(8,128)S(1)} %get-tuple-element.65.refs_2_), channel_id=1, source_target_pairs={{0,8},{4,20},{8,0},{12,28},{16,24},{20,4},{24,16},{28,12},{1,9},{5... | collective-permute-start | bytes 2752520 | tf_op jit(solution)/shard_map/ppermute | solution.py:340
  28.0 46.9 %collective-permute-start.11 = (f32[64,3584]{1,0:T(8,128)S(1)}, f32[64,3584]{1,0:T(8,128)S(1)}, u32[]{:S(2)}, u32[]{:S(2)}) collective-permute-start(f32[64,3584]{1,0:T(8,128)S(1)} %get-tuple-element.66), channel_id=1, source_target_pairs={{0,20},{4,8},{8,28},{12,0},{16,4},{20,24},{24,12},{28,16},{1,21},{... | collective-permute-start | bytes 2752520 | tf_op jit(solution)/shard_map/ppermute | solution.py:340
  32.7 26.9 %collective-permute-start.7 = (f32[80,256]{1,0:T(8,128)S(1)}, f32[80,256]{1,0:T(8,128)S(1)}, u32[]{:S(2)}, u32[]{:S(2)}) collective-permute-start(f32[80,256]{1,0:T(8,128)S(1)} %get-tuple-element.70), channel_id=1, source_target_pairs={{0,2},{1,3},{2,0},{3,1},{4,6},{5,7},{6,4},{7,5},{8,10},{9,11},{10,... | collective-permute-start | bytes 245768 | tf_op jit(solution)/shard_map/ppermute | solution.py:341
  52.4 7.3 %collective-permute-start.8 = (f32[80,256]{1,0:T(8,128)S(1)}, f32[80,256]{1,0:T(8,128)S(1)}, u32[]{:S(2)}, u32[]{:S(2)}) collective-permute-start(f32[80,256]{1,0:T(8,128)S(1)} %get-tuple-element.71), channel_id=1, source_target_pairs={{0,3},{1,2},{2,1},{3,0},{4,7},{5,6},{6,5},{7,4},{8,11},{9,10},{10,... | collective-permute-start | bytes 245768 | tf_op jit(solution)/shard_map/ppermute | solution.py:341
  58.0 5.1 %collective-permute-start.9 = (f32[80,256]{1,0:T(8,128)S(1)}, f32[80,256]{1,0:T(8,128)S(1)}, u32[]{:S(2)}, u32[]{:S(2)}) collective-permute-start(f32[80,256]{1,0:T(8,128)S(1)} %get-tuple-element.72), channel_id=1, source_target_pairs={{0,1},{1,0},{2,3},{3,2},{4,5},{5,4},{6,7},{7,6},{8,9},{9,8},{10,11... | collective-permute-start | bytes 245768 | tf_op jit(solution)/shard_map/ppermute | solution.py:341
  64.4 10.5 %collective-permute-start.12 = (f32[48,256]{1,0:T(8,128)S(1)}, f32[48,256]{1,0:T(8,128)S(1)}, u32[]{:S(2)}, u32[]{:S(2)}) collective-permute-start(f32[48,256]{1,0:T(8,128)S(1)} %get-tuple-element.80), channel_id=1, source_target_pairs={{0,2},{1,3},{2,0},{3,1},{4,6},{5,7},{6,4},{7,5},{8,10},{9,11},{10,... | collective-permute-start | bytes 147464 | tf_op jit(solution)/shard_map/ppermute | solution.py:341
  67.2 7.7 %collective-permute-start.13 = (f32[48,256]{1,0:T(8,128)S(1)}, f32[48,256]{1,0:T(8,128)S(1)}, u32[]{:S(2)}, u32[]{:S(2)}) collective-permute-start(f32[48,256]{1,0:T(8,128)S(1)} %get-tuple-element.81), channel_id=1, source_target_pairs={{0,3},{1,2},{2,1},{3,0},{4,7},{5,6},{6,5},{7,4},{8,11},{9,10},{10,... | collective-permute-start | bytes 147464 | tf_op jit(solution)/shard_map/ppermute | solution.py:341
  68.6 6.3 %collective-permute-start.14 = (f32[48,256]{1,0:T(8,128)S(1)}, f32[48,256]{1,0:T(8,128)S(1)}, u32[]{:S(2)}, u32[]{:S(2)}) collective-permute-start(f32[48,256]{1,0:T(8,128)S(1)} %get-tuple-element.82), channel_id=1, source_target_pairs={{0,1},{1,0},{2,3},{3,2},{4,5},{5,4},{6,7},{7,6},{8,9},{9,8},{10,11... | collective-permute-start | bytes 147464 | tf_op jit(solution)/shard_map/ppermute | solution.py:341
  75.8 4.9 %collective-permute-start.15 = (f32[32,256]{1,0:T(8,128)S(1)}, f32[32,256]{1,0:T(8,128)S(1)}, u32[]{:S(2)}, u32[]{:S(2)}) collective-permute-start(f32[32,256]{1,0:T(8,128)S(1)} %get-tuple-element.90), channel_id=1, source_target_pairs={{0,2},{1,3},{2,0},{3,1},{4,6},{5,7},{6,4},{7,5},{8,10},{9,11},{10,... | collective-permute-start | bytes 98312 | tf_op jit(solution)/shard_map/ppermute | solution.py:341
  78.7 5.7 %collective-permute-start.16 = (f32[32,256]{1,0:T(8,128)S(1)}, f32[32,256]{1,0:T(8,128)S(1)}, u32[]{:S(2)}, u32[]{:S(2)}) collective-permute-start(f32[32,256]{1,0:T(8,128)S(1)} %get-tuple-element.91), channel_id=1, source_target_pairs={{0,3},{1,2},{2,1},{3,0},{4,7},{5,6},{6,5},{7,4},{8,11},{9,10},{10,... | collective-permute-start | bytes 98312 | tf_op jit(solution)/shard_map/ppermute | solution.py:341
  80.1 4.4 %collective-permute-start.17 = (f32[32,256]{1,0:T(8,128)S(1)}, f32[32,256]{1,0:T(8,128)S(1)}, u32[]{:S(2)}, u32[]{:S(2)}) collective-permute-start(f32[32,256]{1,0:T(8,128)S(1)} %get-tuple-element.92), channel_id=1, source_target_pairs={{0,1},{1,0},{2,3},{3,2},{4,5},{5,4},{6,7},{7,6},{8,9},{9,8},{10,11... | collective-permute-start | bytes 98312 | tf_op jit(solution)/shard_map/ppermute | solution.py:341
  84.5 3.5 %collective-permute-start.20 = (f32[80,128]{1,0:T(8,128)S(1)}, f32[80,128]{1,0:T(8,128)S(1)}, u32[]{:S(2)}, u32[]{:S(2)}) collective-permute-start(f32[80,128]{1,0:T(8,128)S(1)} %get-tuple-element.96), channel_id=1, source_target_pairs={{0,12},{4,16},{8,4},{12,24},{16,28},{20,0},{24,20},{28,8},{1,13},{... | collective-permute-start | bytes 122888 | tf_op jit(solution)/shard_map/ppermute | solution.py:340
  84.6 4.8 %collective-permute-start.21 = (f32[80,128]{1,0:T(8,128)S(1)}, f32[80,128]{1,0:T(8,128)S(1)}, u32[]{:S(2)}, u32[]{:S(2)}) collective-permute-start(f32[80,128]{1,0:T(8,128)S(1)} %get-tuple-element.97), channel_id=1, source_target_pairs={{0,28},{4,24},{8,20},{12,16},{16,12},{20,8},{24,4},{28,0},{1,29},{... | collective-permute-start | bytes 122888 | tf_op jit(solution)/shard_map/ppermute | solution.py:340
  89.4 8.2 %collective-permute-start.22 = (f32[160,128]{1,0:T(8,128)S(1)}, f32[160,128]{1,0:T(8,128)S(1)}, u32[]{:S(2)}, u32[]{:S(2)}) collective-permute-start(f32[160,128]{1,0:T(8,128)S(1)} %merge.3.refs_0_), channel_id=1, source_target_pairs={{0,1},{1,0},{2,3},{3,2},{4,5},{5,4},{6,7},{7,6},{8,9},{9,8},{10,11... | collective-permute-start | bytes 245768 | tf_op jit(solution)/shard_map/ppermute | solution.py:341
  89.5 8.1 %collective-permute-start.23 = (f32[160,128]{1,0:T(8,128)S(1)}, f32[160,128]{1,0:T(8,128)S(1)}, u32[]{:S(2)}, u32[]{:S(2)}) collective-permute-start(f32[160,128]{1,0:T(8,128)S(1)} %merge.3.refs_0_), channel_id=1, source_target_pairs={{0,2},{1,3},{2,0},{3,1},{4,6},{5,7},{6,4},{7,5},{8,10},{9,11},{10,... | collective-permute-start | bytes 245768 | tf_op jit(solution)/shard_map/ppermute | solution.py:341
  92.1 7.1 %collective-permute-start.24 = (f32[160,128]{1,0:T(8,128)S(1)}, f32[160,128]{1,0:T(8,128)S(1)}, u32[]{:S(2)}, u32[]{:S(2)}) collective-permute-start(f32[160,128]{1,0:T(8,128)S(1)} %merge.3.refs_0_), channel_id=1, source_target_pairs={{0,3},{1,2},{2,1},{3,0},{4,7},{5,6},{6,5},{7,4},{8,11},{9,10},{10,... | collective-permute-start | bytes 245768 | tf_op jit(solution)/shard_map/ppermute | solution.py:341
  93.9 1.2 collective-permute-start.18
  94.2 3.4 %collective-permute-start.19 = (f32[80,128]{1,0:T(8,128)S(1)}, f32[80,128]{1,0:T(8,128)S(1)}, u32[]{:S(2)}, u32[]{:S(2)}) collective-permute-start(f32[80,128]{1,0:T(8,128)S(1)} %get-tuple-element.95), channel_id=1, source_target_pairs={{0,20},{4,8},{8,28},{12,0},{16,4},{20,24},{24,12},{28,16},{1,21},{... | collective-permute-start | bytes 122888 | tf_op jit(solution)/shard_map/ppermute | solution.py:340
  101.1 16.4 %collective-permute-start.30 = (f32[64,3584]{1,0:T(8,128)S(1)}, f32[64,3584]{1,0:T(8,128)S(1)}, u32[]{:S(2)}, u32[]{:S(2)}) collective-permute-start(f32[64,3584]{1,0:T(8,128)S(1)} %term.3), channel_id=1, source_target_pairs={{0,20},{4,8},{8,28},{12,0},{16,4},{20,24},{24,12},{28,16},{1,21},{... | collective-permute-start | bytes 2752520 | tf_op jit(solution)/shard_map/ppermute | solution.py:340
  102.9 6.6 %collective-permute-start.25 = (f32[160,128]{1,0:T(8,128)S(1)}, f32[160,128]{1,0:T(8,128)S(1)}, u32[]{:S(2)}, u32[]{:S(2)}) collective-permute-start(f32[160,128]{1,0:T(8,128)S(1)} %merge.2.refs_0_), channel_id=1, source_target_pairs={{0,1},{1,0},{2,3},{3,2},{4,5},{5,4},{6,7},{7,6},{8,9},{9,8},{10,11... | collective-permute-start | bytes 245768 | tf_op jit(solution)/shard_map/ppermute | solution.py:341
  105.4 9.6 %collective-permute-start.26 = (f32[160,128]{1,0:T(8,128)S(1)}, f32[160,128]{1,0:T(8,128)S(1)}, u32[]{:S(2)}, u32[]{:S(2)}) collective-permute-start(f32[160,128]{1,0:T(8,128)S(1)} %merge.2.refs_0_), channel_id=1, source_target_pairs={{0,2},{1,3},{2,0},{3,1},{4,6},{5,7},{6,4},{7,5},{8,10},{9,11},{10,... | collective-permute-start | bytes 245768 | tf_op jit(solution)/shard_map/ppermute | solution.py:341
  106.5 8.6 %collective-permute-start.27 = (f32[160,128]{1,0:T(8,128)S(1)}, f32[160,128]{1,0:T(8,128)S(1)}, u32[]{:S(2)}, u32[]{:S(2)}) collective-permute-start(f32[160,128]{1,0:T(8,128)S(1)} %merge.2.refs_0_), channel_id=1, source_target_pairs={{0,3},{1,2},{2,1},{3,0},{4,7},{5,6},{6,5},{7,4},{8,11},{9,10},{10,... | collective-permute-start | bytes 245768 | tf_op jit(solution)/shard_map/ppermute | solution.py:341
  107.9 16.2 %collective-permute-start.28 = (f32[64,3584]{1,0:T(8,128)S(1)}, f32[64,3584]{1,0:T(8,128)S(1)}, u32[]{:S(2)}, u32[]{:S(2)}) collective-permute-start(f32[64,3584]{1,0:T(8,128)S(1)} %term.4), channel_id=1, source_target_pairs={{0,16},{4,12},{8,24},{12,4},{16,0},{20,28},{24,8},{28,20},{1,17},{... | collective-permute-start | bytes 2752520 | tf_op jit(solution)/shard_map/ppermute | solution.py:340
  117.4 6.6 %collective-permute-start.29 = (f32[64,3584]{1,0:T(8,128)S(1)}, f32[64,3584]{1,0:T(8,128)S(1)}, u32[]{:S(2)}, u32[]{:S(2)}) collective-permute-start(f32[64,3584]{1,0:T(8,128)S(1)} %get-tuple-element.120), channel_id=1, source_target_pairs={{0,4},{4,0},{8,12},{12,8},{16,20},{20,16},{24,28},{28,24},{1,5},{5... | collective-permute-start | bytes 2752520 | tf_op jit(solution)/shard_map/ppermute | solution.py:340

commit v7 on v6

--- a/solution.py
+++ b/solution.py
@@ -83,7 +83,7 @@
     inputs, out = refs[:-1], refs[-1]
     width, half = inputs[0].shape
     columns = width * len(inputs)
-    step = block_of(half, 512)
+    step = block_of(half, 4096)
 
     @pl.loop(0, half // step)
     def _(i):
@@ -287,7 +287,7 @@
     core = lax.axis_index("tok") & 1
     half = out.shape[1] // 2
     width, size = staged.shape[1:]
-    rows = 16 if width % 16 == 0 else width
+    rows = 32 if width % 32 == 0 else width
     copies = []
     for i in range(0, width, rows):
         first = 0
@@ -314,7 +314,7 @@
     width, half = own[0].shape
     size = own[1].shape[1]
     inputs = [*own, *other]
-    rows = 16 if width % 16 == 0 else width
+    rows = 32 if width % 32 == 0 else width
     hbm = pl.BlockSpec(memory_space=pl.ANY)
     return pl.pallas_call(
         functools.partial(join_kernel, (len(own), len(other)), low),

time: 126 us -> 126 us (level)
  no operation moved by 1% of the time
where the time goes in v7:
time: 126 us
  waiting for transfers between devices  67.2 us (53%)
  starting transfers between devices  41.2 us (33%)
  Pallas kernels  13.1 us (10%)
  local copies, waits for them, and re-layouts  3.8 us (3%)
    ppermute x16, waiting for transfers between devices, shards(): send = lambda x, pairs: lax.ppermute(x, 'tok', pairs)  52.3 us
    ppermute x15, starting transfers between devices, shards(): lax.ppermute(x, 'feat', [(i, i ^ s) for i in range(zs)])  26.5 us
    ppermute x15, waiting for transfers between devices, shards(): lax.ppermute(x, 'feat', [(i, i ^ s) for i in range(zs)])  14.9 us
    ppermute x16, starting transfers between devices, shards(): send = lambda x, pairs: lax.ppermute(x, 'tok', pairs)  14.8 us
    pallas_call x3, Pallas kernels, terms(): pl.pallas_call(functools.partial(term_kernel, zs, spots, len(acts), left)...  5.94 us
    pallas_call x3, Pallas kernels, mix(): pl.pallas_call(functools.partial(mix_kernel, count, zs), out_shape=[piece...  4.18 us
    unnamed x4, local copies, waits for them, and re-layouts  3.8 us
  transfers between devices with their start and end apart: 31, of which 15 were waited for; matrix products, arithmetic and copies ran while one was open for 0% of the time, Pallas kernels for 7%

profile of v7, /device:TPU:0, one launch (start us, length us, event | category | flops | bytes accessed | tf_op | source)
XLA Modules:
  0.0 125.7 jit_solution(13130657611149904100)
XLA Ops:
  0.0 1.5 %copy-done.1 = f32[7168,64]{0,1:T(8,128)S(1)} copy-done((f32[7168,64]{0,1:T(8,128)S(1)}, f32[7168,64]{0,1:T(8,128)}, u32[]{:S(2)}) %copy-start.1) | copy-done | bytes 1835032
  1.7 0.5 collective-permute-start.4
  2.2 2.6 %collective-permute-start.5 = (f32[64,3584]{1,0:T(8,128)S(1)}, f32[64,3584]{1,0:T(8,128)S(1)}, u32[]{:S(2)}, u32[]{:S(2)}) collective-permute-start(f32[64,3584]{1,0:T(8,128)S(1)} %get-tuple-element.67.refs_0_), channel_id=1, source_target_pairs={{0,16},{4,12},{8,24},{12,4},{16,0},{20,28},{24,8},{28,20},{1,17},{... | collective-permute-start | bytes 2752520 | tf_op jit(solution)/shard_map/ppermute | solution.py:340
  4.8 2.3 %copy-done = f32[160,7168]{1,0:T(8,128)S(1)} copy-done((f32[160,7168]{1,0:T(8,128)S(1)}, f32[160,7168]{1,0:T(8,128)}, u32[]{:S(2)}) %copy-start) | copy-done | bytes 4587544
  7.1 0.4 cut.2
  7.7 0.4 collective-permute-start.2
  8.1 1.7 %collective-permute-start = (f32[96,3584]{1,0:T(8,128)S(1)}, f32[96,3584]{1,0:T(8,128)S(1)}, u32[]{:S(2)}, u32[]{:S(2)}) collective-permute-start(f32[96,3584]{1,0:T(8,128)S(1)} %get-tuple-element.63.refs_0_), channel_id=1, source_target_pairs={{0,8},{4,20},{8,0},{12,28},{16,24},{20,4},{24,16},{28,12},{1,9},{5... | collective-permute-start | bytes 4128776 | tf_op jit(solution)/shard_map/ppermute | solution.py:340
  9.8 15.6 %collective-permute-done.5.refs_2_ = f32[64,3584]{1,0:T(8,128)S(1)} collective-permute-done((f32[64,3584]{1,0:T(8,128)S(1)}, f32[64,3584]{1,0:T(8,128)S(1)}, u32[]{:S(2)}, u32[]{:S(2)}) %collective-permute-start.5) | collective-permute-done | bytes 917536 | tf_op jit(solution)/shard_map/ppermute | solution.py:340
  25.5 0.5 collective-permute-done.6.refs_3_
  26.0 2.0 %collective-permute-start.10 = (f32[64,3584]{1,0:T(8,128)S(1)}, f32[64,3584]{1,0:T(8,128)S(1)}, u32[]{:S(2)}, u32[]{:S(2)}) collective-permute-start(f32[64,3584]{1,0:T(8,128)S(1)} %get-tuple-element.65.refs_2_), channel_id=1, source_target_pairs={{0,8},{4,20},{8,0},{12,28},{16,24},{20,4},{24,16},{28,12},{1,9},{5... | collective-permute-start | bytes 2752520 | tf_op jit(solution)/shard_map/ppermute | solution.py:340
  28.0 1.3 %collective-permute-start.11 = (f32[64,3584]{1,0:T(8,128)S(1)}, f32[64,3584]{1,0:T(8,128)S(1)}, u32[]{:S(2)}, u32[]{:S(2)}) collective-permute-start(f32[64,3584]{1,0:T(8,128)S(1)} %get-tuple-element.66), channel_id=1, source_target_pairs={{0,20},{4,8},{8,28},{12,0},{16,4},{20,24},{24,12},{28,16},{1,21},{... | collective-permute-start | bytes 2752520 | tf_op jit(solution)/shard_map/ppermute | solution.py:340
  29.3 1.0 turn.1.refs_4_.refs_2_
  30.3 2.0 %mix.3 = (f32[80,256]{1,0:T(8,128)S(1)}, f32[80,256]{1,0:T(8,128)S(1)}, f32[80,256]{1,0:T(8,128)S(1)}, f32[80,256]{1,0:T(8,128)S(1)}, bf16[320,3584]{1,0:T(8,128)(2,1)S(1)}, /*index=5*/bf16[320,3584]{1,0:T(8,128)(2,1)S(1)}) custom-call(f32[96,3584]{1,0:T(8,128)S(1)} %get-tuple-element.63.refs_0_, f32[96,3584]{1,0:T(8,128)S(1)} %collective-permute-done.2.refs_1_, ...), custom_call_target="tpu_custom_call" | custom-call | flops 1761607680 | bytes 12845056 | tf_op jit(solution)/shard_map/mix/pallas_call | solution.py:139
  32.3 2.7 %collective-permute-start.7 = (f32[80,256]{1,0:T(8,128)S(1)}, f32[80,256]{1,0:T(8,128)S(1)}, u32[]{:S(2)}, u32[]{:S(2)}) collective-permute-start(f32[80,256]{1,0:T(8,128)S(1)} %get-tuple-element.70), channel_id=1, source_target_pairs={{0,2},{1,3},{2,0},{3,1},{4,6},{5,7},{6,4},{7,5},{8,10},{9,11},{10,... | collective-permute-start | bytes 245768 | tf_op jit(solution)/shard_map/ppermute | solution.py:341
  35.0 17.4 %collective-permute-done.refs_0_ = f32[96,3584]{1,0:T(8,128)S(1)} collective-permute-done((f32[96,3584]{1,0:T(8,128)S(1)}, f32[96,3584]{1,0:T(8,128)S(1)}, u32[]{:S(2)}, u32[]{:S(2)}) %collective-permute-start) | collective-permute-done | bytes 1376288 | tf_op jit(solution)/shard_map/ppermute | solution.py:340
  52.4 4.0 %collective-permute-start.8 = (f32[80,256]{1,0:T(8,128)S(1)}, f32[80,256]{1,0:T(8,128)S(1)}, u32[]{:S(2)}, u32[]{:S(2)}) collective-permute-start(f32[80,256]{1,0:T(8,128)S(1)} %get-tuple-element.71), channel_id=1, source_target_pairs={{0,3},{1,2},{2,1},{3,0},{4,7},{5,6},{6,5},{7,4},{8,11},{9,10},{10,... | collective-permute-start | bytes 245768 | tf_op jit(solution)/shard_map/ppermute | solution.py:341
  56.4 1.6 %collective-permute-done.1.refs_1_ = f32[96,3584]{1,0:T(8,128)S(1)} collective-permute-done((f32[96,3584]{1,0:T(8,128)S(1)}, f32[96,3584]{1,0:T(8,128)S(1)}, u32[]{:S(2)}, u32[]{:S(2)}) %collective-permute-start.1) | collective-permute-done | bytes 1376288 | tf_op jit(solution)/shard_map/ppermute | solution.py:340
  58.0 1.7 %collective-permute-start.9 = (f32[80,256]{1,0:T(8,128)S(1)}, f32[80,256]{1,0:T(8,128)S(1)}, u32[]{:S(2)}, u32[]{:S(2)}) collective-permute-start(f32[80,256]{1,0:T(8,128)S(1)} %get-tuple-element.72), channel_id=1, source_target_pairs={{0,1},{1,0},{2,3},{3,2},{4,5},{5,4},{6,7},{7,6},{8,9},{9,8},{10,11... | collective-permute-start | bytes 245768 | tf_op jit(solution)/shard_map/ppermute | solution.py:341
  59.7 3.4 %collective-permute-done.9.refs_3_ = f32[80,256]{1,0:T(8,128)S(1)} collective-permute-done((f32[80,256]{1,0:T(8,128)S(1)}, f32[80,256]{1,0:T(8,128)S(1)}, u32[]{:S(2)}, u32[]{:S(2)}) %collective-permute-start.9) | collective-permute-done | bytes 81952 | tf_op jit(solution)/shard_map/ppermute | solution.py:341
  63.1 1.3 %mix.4 = (f32[48,256]{1,0:T(8,128)S(1)}, f32[48,256]{1,0:T(8,128)S(1)}, f32[48,256]{1,0:T(8,128)S(1)}, f32[48,256]{1,0:T(8,128)S(1)}, bf16[192,3584]{1,0:T(8,128)(2,1)S(1)}, /*index=5*/bf16[192,3584]{1,0:T(8,128)(2,1)S(1)}) custom-call(f32[96,3584]{1,0:T(8,128)S(1)} %collective-permute-done.refs_0_, f32[96,3584]{1,0:T(8,128)S(1)} %collective-permute-done.1.refs_1_, ...), custom_call_target="tpu_custom_call" | custom-call | flops 1056964608 | bytes 9175040 | tf_op jit(solution)/shard_map/mix/pallas_call | solution.py:139
  64.4 2.8 %collective-permute-start.12 = (f32[48,256]{1,0:T(8,128)S(1)}, f32[48,256]{1,0:T(8,128)S(1)}, u32[]{:S(2)}, u32[]{:S(2)}) collective-permute-start(f32[48,256]{1,0:T(8,128)S(1)} %get-tuple-element.80), channel_id=1, source_target_pairs={{0,2},{1,3},{2,0},{3,1},{4,6},{5,7},{6,4},{7,5},{8,10},{9,11},{10,... | collective-permute-start | bytes 147464 | tf_op jit(solution)/shard_map/ppermute | solution.py:341
  67.2 1.3 %collective-permute-start.13 = (f32[48,256]{1,0:T(8,128)S(1)}, f32[48,256]{1,0:T(8,128)S(1)}, u32[]{:S(2)}, u32[]{:S(2)}) collective-permute-start(f32[48,256]{1,0:T(8,128)S(1)} %get-tuple-element.81), channel_id=1, source_target_pairs={{0,3},{1,2},{2,1},{3,0},{4,7},{5,6},{6,5},{7,4},{8,11},{9,10},{10,... | collective-permute-start | bytes 147464 | tf_op jit(solution)/shard_map/ppermute | solution.py:341
  68.8 3.3 %collective-permute-done.10.refs_0_ = f32[64,3584]{1,0:T(8,128)S(1)} collective-permute-done((f32[64,3584]{1,0:T(8,128)S(1)}, f32[64,3584]{1,0:T(8,128)S(1)}, u32[]{:S(2)}, u32[]{:S(2)}) %collective-permute-start.10) | collective-permute-done | bytes 917536 | tf_op jit(solution)/shard_map/ppermute | solution.py:340
  72.1 2.8 %collective-permute-done.11.refs_1_ = f32[64,3584]{1,0:T(8,128)S(1)} collective-permute-done((f32[64,3584]{1,0:T(8,128)S(1)}, f32[64,3584]{1,0:T(8,128)S(1)}, u32[]{:S(2)}, u32[]{:S(2)}) %collective-permute-start.11) | collective-permute-done | bytes 917536 | tf_op jit(solution)/shard_map/ppermute | solution.py:340
  74.9 0.9 mix.5
  75.8 2.9 %collective-permute-start.15 = (f32[32,256]{1,0:T(8,128)S(1)}, f32[32,256]{1,0:T(8,128)S(1)}, u32[]{:S(2)}, u32[]{:S(2)}) collective-permute-start(f32[32,256]{1,0:T(8,128)S(1)} %get-tuple-element.90), channel_id=1, source_target_pairs={{0,2},{1,3},{2,0},{3,1},{4,6},{5,7},{6,4},{7,5},{8,10},{9,11},{10,... | collective-permute-start | bytes 98312 | tf_op jit(solution)/shard_map/ppermute | solution.py:341
  78.7 1.4 %collective-permute-start.16 = (f32[32,256]{1,0:T(8,128)S(1)}, f32[32,256]{1,0:T(8,128)S(1)}, u32[]{:S(2)}, u32[]{:S(2)}) collective-permute-start(f32[32,256]{1,0:T(8,128)S(1)} %get-tuple-element.91), channel_id=1, source_target_pairs={{0,3},{1,2},{2,1},{3,0},{4,7},{5,6},{6,5},{7,4},{8,11},{9,10},{10,... | collective-permute-start | bytes 98312 | tf_op jit(solution)/shard_map/ppermute | solution.py:341
  80.3 0.4 collective-permute-done.15.refs_9_
  80.7 3.8 %collective-permute-done.16.refs_10_ = f32[32,256]{1,0:T(8,128)S(1)} collective-permute-done((f32[32,256]{1,0:T(8,128)S(1)}, f32[32,256]{1,0:T(8,128)S(1)}, u32[]{:S(2)}, u32[]{:S(2)}) %collective-permute-start.16) | collective-permute-done | bytes 32800 | tf_op jit(solution)/shard_map/ppermute | solution.py:341
  84.6 2.6 %collective-permute-start.21 = (f32[80,128]{1,0:T(8,128)S(1)}, f32[80,128]{1,0:T(8,128)S(1)}, u32[]{:S(2)}, u32[]{:S(2)}) collective-permute-start(f32[80,128]{1,0:T(8,128)S(1)} %get-tuple-element.97), channel_id=1, source_target_pairs={{0,28},{4,24},{8,20},{12,16},{16,12},{20,8},{24,4},{28,0},{1,29},{... | collective-permute-start | bytes 122888 | tf_op jit(solution)/shard_map/ppermute | solution.py:340
  87.3 0.7 collective-permute-done.20.refs_1_
  88.0 1.4 %collective-permute-done.21.refs_2_ = f32[80,128]{1,0:T(8,128)S(1)} collective-permute-done((f32[80,128]{1,0:T(8,128)S(1)}, f32[80,128]{1,0:T(8,128)S(1)}, u32[]{:S(2)}, u32[]{:S(2)}) %collective-permute-start.21) | collective-permute-done | bytes 40992 | tf_op jit(solution)/shard_map/ppermute | solution.py:340
  89.5 2.6 %collective-permute-start.23 = (f32[160,128]{1,0:T(8,128)S(1)}, f32[160,128]{1,0:T(8,128)S(1)}, u32[]{:S(2)}, u32[]{:S(2)}) collective-permute-start(f32[160,128]{1,0:T(8,128)S(1)} %merge.3.refs_0_), channel_id=1, source_target_pairs={{0,2},{1,3},{2,0},{3,1},{4,6},{5,7},{6,4},{7,5},{8,10},{9,11},{10,... | collective-permute-start | bytes 245768 | tf_op jit(solution)/shard_map/ppermute | solution.py:341
  92.1 1.8 %collective-permute-start.24 = (f32[160,128]{1,0:T(8,128)S(1)}, f32[160,128]{1,0:T(8,128)S(1)}, u32[]{:S(2)}, u32[]{:S(2)}) collective-permute-start(f32[160,128]{1,0:T(8,128)S(1)} %merge.3.refs_0_), channel_id=1, source_target_pairs={{0,3},{1,2},{2,1},{3,0},{4,7},{5,6},{6,5},{7,4},{8,11},{9,10},{10,... | collective-permute-start | bytes 245768 | tf_op jit(solution)/shard_map/ppermute | solution.py:341
  94.2 0.9 collective-permute-start.19
  95.1 2.5 %collective-permute-done.19.refs_2_ = f32[80,128]{1,0:T(8,128)S(1)} collective-permute-done((f32[80,128]{1,0:T(8,128)S(1)}, f32[80,128]{1,0:T(8,128)S(1)}, u32[]{:S(2)}, u32[]{:S(2)}) %collective-permute-start.19) | collective-permute-done | bytes 40992 | tf_op jit(solution)/shard_map/ppermute | solution.py:340
  97.7 1.6 %collective-permute-done.24.refs_3_ = f32[160,128]{1,0:T(8,128)S(1)} collective-permute-done((f32[160,128]{1,0:T(8,128)S(1)}, f32[160,128]{1,0:T(8,128)S(1)}, u32[]{:S(2)}, u32[]{:S(2)}) %collective-permute-start.24) | collective-permute-done | bytes 81952 | tf_op jit(solution)/shard_map/ppermute | solution.py:341
  99.2 1.8 %term.3 = f32[64,3584]{1,0:T(8,128)S(1)} custom-call(f32[160,128]{1,0:T(8,128)S(1)} %merge.3.refs_0_, f32[160,128]{1,0:T(8,128)S(1)} %collective-permute-done.22.refs_1_, f32[160,128]{1,0:T(8,128)S(1)} %collective-permute-done.23.refs_2_, f32[160,128]{1,0:T(8,128)S(1)} %collective-permute-done.24.refs_3_, bf16[320,3584]{1,0:T(8,128)(2,1)S(1)} %get-tuple-element.103.refs_4_, ...), custom_call_target="tpu_custom_call" | custom-call | tf_op jit(solution)/shard_map/term/pallas_call | solution.py:255
  101.1 0.4 collective-permute-start.30
  101.5 1.7 %term.4 = f32[64,3584]{1,0:T(8,128)S(1)} custom-call(f32[160,128]{1,0:T(8,128)S(1)} %merge.3.refs_0_, f32[160,128]{1,0:T(8,128)S(1)} %collective-permute-done.22.refs_1_, f32[160,128]{1,0:T(8,128)S(1)} %collective-permute-done.23.refs_2_, f32[160,128]{1,0:T(8,128)S(1)} %collective-permute-done.24.refs_3_, bf16[320,3584]{1,0:T(8,128)(2,1)S(1)} %get-tuple-element.103.refs_4_, ...), custom_call_target="tpu_custom_call" | custom-call | tf_op jit(solution)/shard_map/term/pallas_call | solution.py:255
  103.3 2.4 %collective-permute-start.25 = (f32[160,128]{1,0:T(8,128)S(1)}, f32[160,128]{1,0:T(8,128)S(1)}, u32[]{:S(2)}, u32[]{:S(2)}) collective-permute-start(f32[160,128]{1,0:T(8,128)S(1)} %merge.2.refs_0_), channel_id=1, source_target_pairs={{0,1},{1,0},{2,3},{3,2},{4,5},{5,4},{6,7},{7,6},{8,9},{9,8},{10,11... | collective-permute-start | bytes 245768 | tf_op jit(solution)/shard_map/ppermute | solution.py:341
  105.6 1.0 collective-permute-start.26
  106.7 1.4 %collective-permute-start.27 = (f32[160,128]{1,0:T(8,128)S(1)}, f32[160,128]{1,0:T(8,128)S(1)}, u32[]{:S(2)}, u32[]{:S(2)}) collective-permute-start(f32[160,128]{1,0:T(8,128)S(1)} %merge.2.refs_0_), channel_id=1, source_target_pairs={{0,3},{1,2},{2,1},{3,0},{4,7},{5,6},{6,5},{7,4},{8,11},{9,10},{10,... | collective-permute-start | bytes 245768 | tf_op jit(solution)/shard_map/ppermute | solution.py:341
  108.1 1.6 %collective-permute-start.28 = (f32[64,3584]{1,0:T(8,128)S(1)}, f32[64,3584]{1,0:T(8,128)S(1)}, u32[]{:S(2)}, u32[]{:S(2)}) collective-permute-start(f32[64,3584]{1,0:T(8,128)S(1)} %term.4), channel_id=1, source_target_pairs={{0,16},{4,12},{8,24},{12,4},{16,0},{20,28},{24,8},{28,20},{1,17},{... | collective-permute-start | bytes 2752520 | tf_op jit(solution)/shard_map/ppermute | solution.py:340
  109.7 5.7 %collective-permute-done.26.refs_2_ = f32[160,128]{1,0:T(8,128)S(1)} collective-permute-done((f32[160,128]{1,0:T(8,128)S(1)}, f32[160,128]{1,0:T(8,128)S(1)}, u32[]{:S(2)}, u32[]{:S(2)}) %collective-permute-start.26) | collective-permute-done | bytes 81952 | tf_op jit(solution)/shard_map/ppermute | solution.py:341
  115.4 2.4 %term.5 = (f32[64,3584]{1,0:T(8,128)S(1)}, f32[64,3584]{1,0:T(8,128)S(1)}) custom-call(f32[160,128]{1,0:T(8,128)S(1)} %merge.2.refs_0_, f32[160,128]{1,0:T(8,128)S(1)} %collective-permute-done.25.refs_1_, f32[160,128]{1,0:T(8,128)S(1)} %collective-permute-done.26.refs_2_, f32[160,128]{1,0:T(8,128)S(1)} %collective-permute-done.27.refs_3_, ...), custom_call_target="tpu_custom_call" | custom-call | tf_op jit(solution)/shard_map/term/pallas_call | solution.py:255
  117.8 6.4 %collective-permute-done.28.refs_0_.refs_1_ = f32[64,3584]{1,0:T(8,128)S(1)} collective-permute-done((f32[64,3584]{1,0:T(8,128)S(1)}, f32[64,3584]{1,0:T(8,128)S(1)}, u32[]{:S(2)}, u32[]{:S(2)}) %collective-permute-start.28) | collective-permute-done | bytes 917536 | tf_op jit(solution)/shard_map/ppermute | solution.py:340
  124.2 1.3 %join.1 = f32[64,7168]{1,0:T(8,128)} custom-call(f32[64,3584]{1,0:T(8,128)S(1)} %get-tuple-element.119.refs_0_, f32[64,3584]{1,0:T(8,128)S(1)} %collective-permute-done.28.refs_0_.refs_1_, f32[64,3584]{1,0:T(8,128)S(1)} %collective-permute-done.29.refs_2_, f32[64,3584]{1,0:T(8,128)S(1)} %collective-permute-done.30.refs_0_.refs_3_, f32[8,128]{1,0:T(8,128)S(1)} %arrived.3.refs_4_), custom_call_target="tpu_custom_call" | custom-call | tf_op jit(solution)/shard_map/join/pallas_call | solution.py:319
  (33 shorter events, 1.6 us)
Async XLA Ops:
  0.0 1.5 %copy-start.1 = (f32[7168,64]{0,1:T(8,128)S(1)}, f32[7168,64]{0,1:T(8,128)}, u32[]{:S(2)}) copy-start(f32[7168,64]{0,1:T(8,128)} %param.3) | copy-start | bytes 5505028
  1.7 6.4 %collective-permute-start.4 = (f32[64,3584]{1,0:T(8,128)S(1)}, f32[64,3584]{1,0:T(8,128)S(1)}, u32[]{:S(2)}, u32[]{:S(2)}) collective-permute-start(f32[64,3584]{1,0:T(8,128)S(1)} %get-tuple-element.68), channel_id=1, source_target_pairs={{0,4},{4,0},{8,12},{12,8},{16,20},{20,16},{24,28},{28,24},{1,5},{5... | collective-permute-start | bytes 2752520 | tf_op jit(solution)/shard_map/ppermute | solution.py:340
  2.2 23.3 %collective-permute-start.5 = (f32[64,3584]{1,0:T(8,128)S(1)}, f32[64,3584]{1,0:T(8,128)S(1)}, u32[]{:S(2)}, u32[]{:S(2)}) collective-permute-start(f32[64,3584]{1,0:T(8,128)S(1)} %get-tuple-element.67.refs_0_), channel_id=1, source_target_pairs={{0,16},{4,12},{8,24},{12,4},{16,0},{20,28},{24,8},{28,20},{1,17},{... | collective-permute-start | bytes 2752520 | tf_op jit(solution)/shard_map/ppermute | solution.py:340
  4.8 21.2 %collective-permute-start.6 = (f32[64,3584]{1,0:T(8,128)S(1)}, f32[64,3584]{1,0:T(8,128)S(1)}, u32[]{:S(2)}, u32[]{:S(2)}) collective-permute-start(f32[64,3584]{1,0:T(8,128)S(1)} %get-tuple-element.68), channel_id=1, source_target_pairs={{0,12},{4,16},{8,4},{12,24},{16,28},{20,0},{24,20},{28,8},{1,13},{... | collective-permute-start | bytes 2752520 | tf_op jit(solution)/shard_map/ppermute | solution.py:340
  4.8 2.3 %copy-start = (f32[160,7168]{1,0:T(8,128)S(1)}, f32[160,7168]{1,0:T(8,128)}, u32[]{:S(2)}) copy-start(f32[160,7168]{1,0:T(8,128)} %source.1) | copy-start | bytes 13762564
  7.5 20.4 %collective-permute-start.3 = (f32[64,3584]{1,0:T(8,128)S(1)}, f32[64,3584]{1,0:T(8,128)S(1)}, u32[]{:S(2)}, u32[]{:S(2)}) collective-permute-start(f32[64,3584]{1,0:T(8,128)S(1)} %get-tuple-element.66), channel_id=1, source_target_pairs={{0,4},{4,0},{8,12},{12,8},{16,20},{20,16},{24,28},{28,24},{1,5},{5... | collective-permute-start | bytes 2752520 | tf_op jit(solution)/shard_map/ppermute | solution.py:340
  7.7 22.6 %collective-permute-start.2 = (f32[96,3584]{1,0:T(8,128)S(1)}, f32[96,3584]{1,0:T(8,128)S(1)}, u32[]{:S(2)}, u32[]{:S(2)}) collective-permute-start(f32[96,3584]{1,0:T(8,128)S(1)} %get-tuple-element.64), channel_id=1, source_target_pairs={{0,4},{4,0},{8,12},{12,8},{16,20},{20,16},{24,28},{28,24},{1,5},{5... | collective-permute-start | bytes 4128776 | tf_op jit(solution)/shard_map/ppermute | solution.py:340
  8.1 44.3 %collective-permute-start = (f32[96,3584]{1,0:T(8,128)S(1)}, f32[96,3584]{1,0:T(8,128)S(1)}, u32[]{:S(2)}, u32[]{:S(2)}) collective-permute-start(f32[96,3584]{1,0:T(8,128)S(1)} %get-tuple-element.63.refs_0_), channel_id=1, source_target_pairs={{0,8},{4,20},{8,0},{12,28},{16,24},{20,4},{24,16},{28,12},{1,9},{5... | collective-permute-start | bytes 4128776 | tf_op jit(solution)/shard_map/ppermute | solution.py:340
  25.5 32.5 %collective-permute-start.1 = (f32[96,3584]{1,0:T(8,128)S(1)}, f32[96,3584]{1,0:T(8,128)S(1)}, u32[]{:S(2)}, u32[]{:S(2)}) collective-permute-start(f32[96,3584]{1,0:T(8,128)S(1)} %get-tuple-element.64), channel_id=1, source_target_pairs={{0,20},{4,8},{8,28},{12,0},{16,4},{20,24},{24,12},{28,16},{1,21},{... | collective-permute-start | bytes 4128776 | tf_op jit(solution)/shard_map/ppermute | solution.py:340
  26.0 46.1 %collective-permute-start.10 = (f32[64,3584]{1,0:T(8,128)S(1)}, f32[64,3584]{1,0:T(8,128)S(1)}, u32[]{:S(2)}, u32[]{:S(2)}) collective-permute-start(f32[64,3584]{1,0:T(8,128)S(1)} %get-tuple-element.65.refs_2_), channel_id=1, source_target_pairs={{0,8},{4,20},{8,0},{12,28},{16,24},{20,4},{24,16},{28,12},{1,9},{5... | collective-permute-start | bytes 2752520 | tf_op jit(solution)/shard_map/ppermute | solution.py:340
  28.0 46.9 %collective-permute-start.11 = (f32[64,3584]{1,0:T(8,128)S(1)}, f32[64,3584]{1,0:T(8,128)S(1)}, u32[]{:S(2)}, u32[]{:S(2)}) collective-permute-start(f32[64,3584]{1,0:T(8,128)S(1)} %get-tuple-element.66), channel_id=1, source_target_pairs={{0,20},{4,8},{8,28},{12,0},{16,4},{20,24},{24,12},{28,16},{1,21},{... | collective-permute-start | bytes 2752520 | tf_op jit(solution)/shard_map/ppermute | solution.py:340
  32.3 27.4 %collective-permute-start.7 = (f32[80,256]{1,0:T(8,128)S(1)}, f32[80,256]{1,0:T(8,128)S(1)}, u32[]{:S(2)}, u32[]{:S(2)}) collective-permute-start(f32[80,256]{1,0:T(8,128)S(1)} %get-tuple-element.70), channel_id=1, source_target_pairs={{0,2},{1,3},{2,0},{3,1},{4,6},{5,7},{6,4},{7,5},{8,10},{9,11},{10,... | collective-permute-start | bytes 245768 | tf_op jit(solution)/shard_map/ppermute | solution.py:341
  52.4 7.3 %collective-permute-start.8 = (f32[80,256]{1,0:T(8,128)S(1)}, f32[80,256]{1,0:T(8,128)S(1)}, u32[]{:S(2)}, u32[]{:S(2)}) collective-permute-start(f32[80,256]{1,0:T(8,128)S(1)} %get-tuple-element.71), channel_id=1, source_target_pairs={{0,3},{1,2},{2,1},{3,0},{4,7},{5,6},{6,5},{7,4},{8,11},{9,10},{10,... | collective-permute-start | bytes 245768 | tf_op jit(solution)/shard_map/ppermute | solution.py:341
  58.0 5.1 %collective-permute-start.9 = (f32[80,256]{1,0:T(8,128)S(1)}, f32[80,256]{1,0:T(8,128)S(1)}, u32[]{:S(2)}, u32[]{:S(2)}) collective-permute-start(f32[80,256]{1,0:T(8,128)S(1)} %get-tuple-element.72), channel_id=1, source_target_pairs={{0,1},{1,0},{2,3},{3,2},{4,5},{5,4},{6,7},{7,6},{8,9},{9,8},{10,11... | collective-permute-start | bytes 245768 | tf_op jit(solution)/shard_map/ppermute | solution.py:341
  64.4 10.4 %collective-permute-start.12 = (f32[48,256]{1,0:T(8,128)S(1)}, f32[48,256]{1,0:T(8,128)S(1)}, u32[]{:S(2)}, u32[]{:S(2)}) collective-permute-start(f32[48,256]{1,0:T(8,128)S(1)} %get-tuple-element.80), channel_id=1, source_target_pairs={{0,2},{1,3},{2,0},{3,1},{4,6},{5,7},{6,4},{7,5},{8,10},{9,11},{10,... | collective-permute-start | bytes 147464 | tf_op jit(solution)/shard_map/ppermute | solution.py:341
  67.2 7.7 %collective-permute-start.13 = (f32[48,256]{1,0:T(8,128)S(1)}, f32[48,256]{1,0:T(8,128)S(1)}, u32[]{:S(2)}, u32[]{:S(2)}) collective-permute-start(f32[48,256]{1,0:T(8,128)S(1)} %get-tuple-element.81), channel_id=1, source_target_pairs={{0,3},{1,2},{2,1},{3,0},{4,7},{5,6},{6,5},{7,4},{8,11},{9,10},{10,... | collective-permute-start | bytes 147464 | tf_op jit(solution)/shard_map/ppermute | solution.py:341
  68.6 6.3 %collective-permute-start.14 = (f32[48,256]{1,0:T(8,128)S(1)}, f32[48,256]{1,0:T(8,128)S(1)}, u32[]{:S(2)}, u32[]{:S(2)}) collective-permute-start(f32[48,256]{1,0:T(8,128)S(1)} %get-tuple-element.82), channel_id=1, source_target_pairs={{0,1},{1,0},{2,3},{3,2},{4,5},{5,4},{6,7},{7,6},{8,9},{9,8},{10,11... | collective-permute-start | bytes 147464 | tf_op jit(solution)/shard_map/ppermute | solution.py:341
  75.8 4.9 %collective-permute-start.15 = (f32[32,256]{1,0:T(8,128)S(1)}, f32[32,256]{1,0:T(8,128)S(1)}, u32[]{:S(2)}, u32[]{:S(2)}) collective-permute-start(f32[32,256]{1,0:T(8,128)S(1)} %get-tuple-element.90), channel_id=1, source_target_pairs={{0,2},{1,3},{2,0},{3,1},{4,6},{5,7},{6,4},{7,5},{8,10},{9,11},{10,... | collective-permute-start | bytes 98312 | tf_op jit(solution)/shard_map/ppermute | solution.py:341
  78.7 5.7 %collective-permute-start.16 = (f32[32,256]{1,0:T(8,128)S(1)}, f32[32,256]{1,0:T(8,128)S(1)}, u32[]{:S(2)}, u32[]{:S(2)}) collective-permute-start(f32[32,256]{1,0:T(8,128)S(1)} %get-tuple-element.91), channel_id=1, source_target_pairs={{0,3},{1,2},{2,1},{3,0},{4,7},{5,6},{6,5},{7,4},{8,11},{9,10},{10,... | collective-permute-start | bytes 98312 | tf_op jit(solution)/shard_map/ppermute | solution.py:341
  80.1 4.4 %collective-permute-start.17 = (f32[32,256]{1,0:T(8,128)S(1)}, f32[32,256]{1,0:T(8,128)S(1)}, u32[]{:S(2)}, u32[]{:S(2)}) collective-permute-start(f32[32,256]{1,0:T(8,128)S(1)} %get-tuple-element.92), channel_id=1, source_target_pairs={{0,1},{1,0},{2,3},{3,2},{4,5},{5,4},{6,7},{7,6},{8,9},{9,8},{10,11... | collective-permute-start | bytes 98312 | tf_op jit(solution)/shard_map/ppermute | solution.py:341
  84.6 3.5 %collective-permute-start.20 = (f32[80,128]{1,0:T(8,128)S(1)}, f32[80,128]{1,0:T(8,128)S(1)}, u32[]{:S(2)}, u32[]{:S(2)}) collective-permute-start(f32[80,128]{1,0:T(8,128)S(1)} %get-tuple-element.96), channel_id=1, source_target_pairs={{0,12},{4,16},{8,4},{12,24},{16,28},{20,0},{24,20},{28,8},{1,13},{... | collective-permute-start | bytes 122888 | tf_op jit(solution)/shard_map/ppermute | solution.py:340
  84.6 4.8 %collective-permute-start.21 = (f32[80,128]{1,0:T(8,128)S(1)}, f32[80,128]{1,0:T(8,128)S(1)}, u32[]{:S(2)}, u32[]{:S(2)}) collective-permute-start(f32[80,128]{1,0:T(8,128)S(1)} %get-tuple-element.97), channel_id=1, source_target_pairs={{0,28},{4,24},{8,20},{12,16},{16,12},{20,8},{24,4},{28,0},{1,29},{... | collective-permute-start | bytes 122888 | tf_op jit(solution)/shard_map/ppermute | solution.py:340
  89.4 8.2 %collective-permute-start.22 = (f32[160,128]{1,0:T(8,128)S(1)}, f32[160,128]{1,0:T(8,128)S(1)}, u32[]{:S(2)}, u32[]{:S(2)}) collective-permute-start(f32[160,128]{1,0:T(8,128)S(1)} %merge.3.refs_0_), channel_id=1, source_target_pairs={{0,1},{1,0},{2,3},{3,2},{4,5},{5,4},{6,7},{7,6},{8,9},{9,8},{10,11... | collective-permute-start | bytes 245768 | tf_op jit(solution)/shard_map/ppermute | solution.py:341
  89.5 8.1 %collective-permute-start.23 = (f32[160,128]{1,0:T(8,128)S(1)}, f32[160,128]{1,0:T(8,128)S(1)}, u32[]{:S(2)}, u32[]{:S(2)}) collective-permute-start(f32[160,128]{1,0:T(8,128)S(1)} %merge.3.refs_0_), channel_id=1, source_target_pairs={{0,2},{1,3},{2,0},{3,1},{4,6},{5,7},{6,4},{7,5},{8,10},{9,11},{10,... | collective-permute-start | bytes 245768 | tf_op jit(solution)/shard_map/ppermute | solution.py:341
  92.1 7.1 %collective-permute-start.24 = (f32[160,128]{1,0:T(8,128)S(1)}, f32[160,128]{1,0:T(8,128)S(1)}, u32[]{:S(2)}, u32[]{:S(2)}) collective-permute-start(f32[160,128]{1,0:T(8,128)S(1)} %merge.3.refs_0_), channel_id=1, source_target_pairs={{0,3},{1,2},{2,1},{3,0},{4,7},{5,6},{6,5},{7,4},{8,11},{9,10},{10,... | collective-permute-start | bytes 245768 | tf_op jit(solution)/shard_map/ppermute | solution.py:341
  93.9 1.2 collective-permute-start.18
  94.2 3.4 %collective-permute-start.19 = (f32[80,128]{1,0:T(8,128)S(1)}, f32[80,128]{1,0:T(8,128)S(1)}, u32[]{:S(2)}, u32[]{:S(2)}) collective-permute-start(f32[80,128]{1,0:T(8,128)S(1)} %get-tuple-element.95), channel_id=1, source_target_pairs={{0,20},{4,8},{8,28},{12,0},{16,4},{20,24},{24,12},{28,16},{1,21},{... | collective-permute-start | bytes 122888 | tf_op jit(solution)/shard_map/ppermute | solution.py:340
  101.1 16.7 %collective-permute-start.30 = (f32[64,3584]{1,0:T(8,128)S(1)}, f32[64,3584]{1,0:T(8,128)S(1)}, u32[]{:S(2)}, u32[]{:S(2)}) collective-permute-start(f32[64,3584]{1,0:T(8,128)S(1)} %term.3), channel_id=1, source_target_pairs={{0,20},{4,8},{8,28},{12,0},{16,4},{20,24},{24,12},{28,16},{1,21},{... | collective-permute-start | bytes 2752520 | tf_op jit(solution)/shard_map/ppermute | solution.py:340
  103.3 6.4 %collective-permute-start.25 = (f32[160,128]{1,0:T(8,128)S(1)}, f32[160,128]{1,0:T(8,128)S(1)}, u32[]{:S(2)}, u32[]{:S(2)}) collective-permute-start(f32[160,128]{1,0:T(8,128)S(1)} %merge.2.refs_0_), channel_id=1, source_target_pairs={{0,1},{1,0},{2,3},{3,2},{4,5},{5,4},{6,7},{7,6},{8,9},{9,8},{10,11... | collective-permute-start | bytes 245768 | tf_op jit(solution)/shard_map/ppermute | solution.py:341
  105.6 9.7 %collective-permute-start.26 = (f32[160,128]{1,0:T(8,128)S(1)}, f32[160,128]{1,0:T(8,128)S(1)}, u32[]{:S(2)}, u32[]{:S(2)}) collective-permute-start(f32[160,128]{1,0:T(8,128)S(1)} %merge.2.refs_0_), channel_id=1, source_target_pairs={{0,2},{1,3},{2,0},{3,1},{4,6},{5,7},{6,4},{7,5},{8,10},{9,11},{10,... | collective-permute-start | bytes 245768 | tf_op jit(solution)/shard_map/ppermute | solution.py:341
  106.7 8.7 %collective-permute-start.27 = (f32[160,128]{1,0:T(8,128)S(1)}, f32[160,128]{1,0:T(8,128)S(1)}, u32[]{:S(2)}, u32[]{:S(2)}) collective-permute-start(f32[160,128]{1,0:T(8,128)S(1)} %merge.2.refs_0_), channel_id=1, source_target_pairs={{0,3},{1,2},{2,1},{3,0},{4,7},{5,6},{6,5},{7,4},{8,11},{9,10},{10,... | collective-permute-start | bytes 245768 | tf_op jit(solution)/shard_map/ppermute | solution.py:341
  108.1 16.2 %collective-permute-start.28 = (f32[64,3584]{1,0:T(8,128)S(1)}, f32[64,3584]{1,0:T(8,128)S(1)}, u32[]{:S(2)}, u32[]{:S(2)}) collective-permute-start(f32[64,3584]{1,0:T(8,128)S(1)} %term.4), channel_id=1, source_target_pairs={{0,16},{4,12},{8,24},{12,4},{16,0},{20,28},{24,8},{28,20},{1,17},{... | collective-permute-start | bytes 2752520 | tf_op jit(solution)/shard_map/ppermute | solution.py:340
  117.7 6.5 %collective-permute-start.29 = (f32[64,3584]{1,0:T(8,128)S(1)}, f32[64,3584]{1,0:T(8,128)S(1)}, u32[]{:S(2)}, u32[]{:S(2)}) collective-permute-start(f32[64,3584]{1,0:T(8,128)S(1)} %get-tuple-element.120), channel_id=1, source_target_pairs={{0,4},{4,0},{8,12},{12,8},{16,20},{20,16},{24,28},{28,24},{1,5},{5... | collective-permute-start | bytes 2752520 | tf_op jit(solution)/shard_map/ppermute | solution.py:340
